TPU v7x, 512 devices: a whole 4x8x8 slice. The times are simulated.
512 devices in a mesh: grp: 8 (over z_hi, core), seq: 64 (over y, z_lo, x).
Axes of the slice: x: 4, y: 8, z: 8 (z_hi: 4, z_lo: 2; z = z_hi * 2 + z_lo), core: 2. Of those that a mesh axis runs over, the one named last changes fastest.
Arguments:
- queries: bfloat16 [65536, 3072], P(('grp', 'seq'))
- keys: bfloat16 [65536, 3072], P(('grp', 'seq'))
- values: bfloat16 [65536, 3072], P(('grp', 'seq')), may hold values from -6 to 6
- head_order: int32 [24], replicated, may hold values from 0 to 23, each once
- key_blocks: int32 [128, 6], replicated, may hold values from 0 to 127, as said below
- block_count: int32 [128], replicated, may hold values from 2 to 6, as said below
Outputs:
- attended: bfloat16 [65536, 3072], P(('grp', 'seq'))
Inputs may be any that keep to these rules, and one draw needn't show every extreme that they name: `key_blocks`: each row lists distinct frames; entry 0 is the row's own frame; every entry lies within 3 frames of the row's frame on the closed loop of 128 frames. `block_count`: some frame uses all 6 entries.
All inputs are finite; a program needn't handle non-finite values.
Results may differ from a plain program's by a relative error of at most 0.009.
Values may be sent and summed in bfloat16 or wider, within the bound.
No kernel may reach another device: no remote copies, remote signals or barrier semaphores. Data moves between devices by JAX's collectives and lax.ppermute only.
A program may use at most 64 MiB of HBM per device.

v0:
```python
import functools
import math

import jax
import jax.numpy as jnp
from jax import lax
from jax.experimental import pallas as pl
from jax.experimental.pallas import tpu as pltpu
from jax.sharding import Mesh
from jax.sharding import PartitionSpec as P

HT = 8
W = 3
NB = 6
BLOCK = 4
DEPTH = 128
LANES = 128
BF = jnp.bfloat16
F32 = jnp.float32
VMEM = pl.BlockSpec(memory_space=pltpu.VMEM)
SMEM = pl.BlockSpec(memory_space=pltpu.SMEM)
ANY = pl.BlockSpec(memory_space=pl.ANY)
PARAMS = pltpu.CompilerParams(vmem_limit_bytes=40 * 1024 * 1024)
PACK_PARAMS = pltpu.CompilerParams(vmem_limit_bytes=58 * 1024 * 1024)


def estimate(gigaflops):
    return pl.CostEstimate(flops=gigaflops * 10**9, bytes_accessed=1 << 20, transcendentals=1 << 20)


def columns_of(order_ref, slot):
    return pl.ds(pl.multiple_of(order_ref[slot] * DEPTH, DEPTH), DEPTH)


def run_copies(copies):
    for copy in copies:
        copy.start()
    for copy in copies:
        copy.wait()


def pack_spatial_kernel(order_ref, *refs):
    dst, sems = refs[-2:]
    copies = []
    for which, src in enumerate(refs[:-2]):
        for head in range(dst.shape[0]):
            column = columns_of(order_ref, HT + head)
            copies.append(
                pltpu.make_async_copy(src.at[:, column], dst.at[head, which], sems.at[which, head])
            )
    run_copies(copies)


def pack_spatial(order, arrays):
    rows, width = arrays[0].shape
    heads = width // DEPTH - HT
    return pl.pallas_call(
        pack_spatial_kernel,
        out_shape=jax.ShapeDtypeStruct((heads, len(arrays), rows, DEPTH), BF),
        in_specs=[SMEM] + [ANY] * len(arrays),
        out_specs=ANY,
        scratch_shapes=[pltpu.SemaphoreType.DMA((len(arrays), heads))],
        compiler_params=PACK_PARAMS,
    )(order, *arrays)


def pack_temporal_kernel(order_ref, *refs):
    dst, sems = refs[-2:]
    pieces = refs[0].shape[0]
    copies = []
    for which, src in enumerate(refs[:-2]):
        for head in range(HT):
            copies.append(
                pltpu.make_async_copy(
                    src.at[:, :, columns_of(order_ref, head)],
                    dst.at[pl.ds(head * pieces, pieces), which],
                    sems.at[which, head],
                )
            )
    run_copies(copies)


def pack_temporal(order, arrays, items):
    rows, width = arrays[0].shape
    pieces = rows // items
    return pl.pallas_call(
        pack_temporal_kernel,
        out_shape=jax.ShapeDtypeStruct((HT * pieces, len(arrays), items, DEPTH), BF),
        in_specs=[SMEM] + [ANY] * len(arrays),
        out_specs=ANY,
        scratch_shapes=[pltpu.SemaphoreType.DMA((len(arrays), HT))],
        compiler_params=PACK_PARAMS,
        cost_estimate=estimate(10),
    )(order, *[array.reshape(pieces, items, width) for array in arrays])


def temporal_kernel(in_ref, out_ref):
    frames, _, items, depth = in_ref.shape
    total = frames * items
    step = 256
    factor = depth ** (-0.5) * math.log2(math.e)
    k = in_ref[:, 1].reshape(total, depth)
    v = in_ref[:, 2].reshape(total, depth)
    row_item = lax.broadcasted_iota(jnp.int32, (step, total), 0) % items
    col_item = lax.broadcasted_iota(jnp.int32, (step, total), 1) % items
    same = row_item == col_item
    per = step // items
    for at in range(frames // per):
        q = in_ref[at * per : (at + 1) * per, 0].reshape(step, depth)
        s = lax.dot_general(q, k, (((1,), (1,)), ((), ())), preferred_element_type=F32)
        s = jnp.where(same, s * factor, -jnp.inf)
        p = jnp.exp2(s - jnp.max(s, axis=1, keepdims=True))
        total_p = jnp.sum(p, axis=1, keepdims=True)
        o = jnp.dot(p.astype(BF), v, preferred_element_type=F32) / total_p
        out_ref[at * per : (at + 1) * per] = o.astype(BF).reshape(per, items, depth)


def temporal_attend(arrived):
    frames, _, items, depth = arrived.shape
    return pl.pallas_call(
        temporal_kernel,
        out_shape=jax.ShapeDtypeStruct((frames, items, depth), BF),
        in_specs=[VMEM],
        out_specs=VMEM,
        compiler_params=PARAMS,
        cost_estimate=estimate(50),
    )(arrived)


def row_norm(blocks):
    ones = jnp.ones((DEPTH, LANES), BF)
    best = None
    for block in blocks:
        norms = jnp.dot(block * block, ones, preferred_element_type=F32)
        most = jnp.max(norms.reshape(-1, 8, LANES), axis=0)
        best = most if best is None else jnp.maximum(best, most)
    return jnp.max(best)


def used_slot(frames, base, kb_ref, bc_ref, mine, slot):
    frame = base + mine
    target = lax.rem(base + slot + frames, frames)
    hit = False
    for n in range(NB):
        hit = hit | ((kb_ref[frame, n] == target) & (bc_ref[frame] > n))
    return hit


def score_factor():
    return DEPTH ** (-0.5) * math.log2(math.e)


def products(q, k):
    return lax.dot_general(q, k, (((1,), (1,)), ((), ())), preferred_element_type=F32)


def add_frames(acc, q, pairs):
    for k, v, hit in pairs:
        p = jnp.exp2(products(q, k) * score_factor()).astype(BF)
        weight = jnp.where(hit, 1.0, 0.0).astype(BF)
        wide = jnp.concatenate([v * weight, jnp.full(v.shape, weight)], axis=1)
        add = jnp.dot(p, wide, preferred_element_type=F32)
        acc = add if acc is None else acc + add
    return acc


def fold_frame(q, k, v, acc_ref, m_ref):
    wide = jnp.concatenate([v, jnp.ones_like(v)], axis=1)
    s = products(q, k) * score_factor()
    old = m_ref[...]
    new = jnp.maximum(old, jnp.max(s, axis=1, keepdims=True))
    p = jnp.exp2(s - new[:, :1]).astype(BF)
    alpha = jnp.exp2(old - new)
    both = jnp.concatenate([alpha, alpha], axis=1)
    acc_ref[...] = acc_ref[...] * both + jnp.dot(p, wide, preferred_element_type=F32)
    m_ref[...] = new


def small_scores(q_norm, k_norm):
    factor = score_factor() * 1.02
    return q_norm * k_norm * (factor * factor) <= 1e4


def frame_at(ref, which, at, pieces):
    block = ref[pl.ds(at * pieces, pieces), which]
    return block.reshape(pieces * block.shape[1], DEPTH)


def own_kernel(frames, base_ref, kb_ref, bc_ref, in_ref, acc_ref, m_ref, stat_ref):
    pieces = in_ref.shape[0] // BLOCK
    size = pieces * in_ref.shape[2]
    base = base_ref[0]
    part = functools.partial(frame_at, in_ref, pieces=pieces)
    q_norm = row_norm([part(0, at) for at in range(BLOCK)])
    k_norm = row_norm([part(1, at) for at in range(BLOCK)])
    fast = small_scores(q_norm, k_norm)
    stat_ref[0] = q_norm
    stat_ref[1] = jnp.where(fast, 1.0, 0.0)

    def used(mine, slot):
        return used_slot(frames, base, kb_ref, bc_ref, mine, slot)

    @pl.when(fast)
    def _():
        def frame(mine, carry):
            pairs = [(part(1, slot), part(2, slot), used(mine, slot)) for slot in range(BLOCK)]
            acc_ref[mine] = add_frames(None, part(0, mine), pairs)
            m_ref[mine] = jnp.zeros((size, LANES), F32)
            return carry

        lax.fori_loop(0, BLOCK, frame, 0)

    @pl.when(jnp.logical_not(fast))
    def _():
        def pair(at, carry):
            mine, slot = at // BLOCK, lax.rem(at, BLOCK)

            @pl.when(slot == 0)
            def _():
                acc_ref[mine] = jnp.zeros((size, 2 * DEPTH), F32)
                m_ref[mine] = jnp.full((size, LANES), -jnp.inf, F32)

            @pl.when(used(mine, slot))
            def _():
                fold_frame(part(0, mine), part(1, slot), part(2, slot), acc_ref.at[mine], m_ref.at[mine])

            return carry

        lax.fori_loop(0, BLOCK * BLOCK, pair, 0)


def near_kernel(
    frames, base_ref, kb_ref, bc_ref, stat_ref, in_ref, less_ref, more_ref, acc_in, m_in, o_ref,
    acc_ref, m_ref, near_ref, sems
):
    pieces = in_ref.shape[0] // BLOCK
    rows = in_ref.shape[2]
    base = base_ref[0]
    run_copies(
        [
            pltpu.make_async_copy(less_ref, near_ref.at[pl.ds(0, W * pieces)], sems.at[0]),
            pltpu.make_async_copy(more_ref, near_ref.at[pl.ds(W * pieces, W * pieces)], sems.at[1]),
        ]
    )
    part = functools.partial(frame_at, near_ref, pieces=pieces)
    k_norm = row_norm([part(0, at) for at in range(2 * W)])
    fast = small_scores(stat_ref[0], k_norm) & (stat_ref[1] > 0.5)

    def query(mine):
        return frame_at(in_ref, 0, mine, pieces)

    def used(mine, at):
        slot = jnp.where(at < W, at - W, at - W + BLOCK)
        return used_slot(frames, base, kb_ref, bc_ref, mine, slot)

    def finish(mine, acc):
        o = (acc[:, :DEPTH] / acc[:, DEPTH:]).astype(BF)
        o_ref[pl.ds(mine * pieces, pieces)] = o.reshape(pieces, rows, DEPTH)

    @pl.when(fast)
    def _():
        def frame(mine, carry):
            pairs = [
                (part(0, mine + j), part(1, mine + j), used(mine, mine + j)) for j in range(W)
            ]
            finish(mine, add_frames(acc_in[mine], query(mine), pairs))
            return carry

        lax.fori_loop(0, BLOCK, frame, 0)

    @pl.when(jnp.logical_not(fast))
    def _():
        def frame(mine, carry):
            acc_ref[...] = acc_in[mine]
            m_ref[...] = m_in[mine]

            def pair(j, inner):
                @pl.when(used(mine, mine + j))
                def _():
                    fold_frame(query(mine), part(0, mine + j), part(1, mine + j), acc_ref, m_ref)

                return inner

            lax.fori_loop(0, W, pair, 0)
            finish(mine, acc_ref[...])
            return carry

        lax.fori_loop(0, BLOCK, frame, 0)


def attend_own(base, kb, bc, arrived, frames):
    dests, _, rows, depth = arrived.shape
    size = dests // BLOCK * rows
    return pl.pallas_call(
        functools.partial(own_kernel, frames),
        out_shape=[
            jax.ShapeDtypeStruct((BLOCK, size, 2 * depth), F32),
            jax.ShapeDtypeStruct((BLOCK, size, LANES), F32),
            jax.ShapeDtypeStruct((2,), F32),
        ],
        in_specs=[SMEM] * 3 + [VMEM],
        out_specs=[VMEM, VMEM, SMEM],
        compiler_params=PARAMS,
        cost_estimate=estimate(10),
    )(base, kb, bc, arrived)


def attend_near(base, kb, bc, stat, arrived, less, more, acc, top, frames):
    dests, _, rows, depth = arrived.shape
    size = dests // BLOCK * rows
    return pl.pallas_call(
        functools.partial(near_kernel, frames),
        out_shape=jax.ShapeDtypeStruct((dests, rows, depth), BF),
        in_specs=[SMEM] * 4 + [VMEM, ANY, ANY, VMEM, VMEM],
        out_specs=VMEM,
        scratch_shapes=[
            pltpu.VMEM((size, 2 * depth), F32),
            pltpu.VMEM((size, LANES), F32),
            pltpu.VMEM((2 * less.shape[0], *less.shape[1:]), BF),
            pltpu.SemaphoreType.DMA((2,)),
        ],
        compiler_params=PARAMS,
    )(base, kb, bc, stat, arrived, less, more, acc, top)


def assemble_kernel(order_ref, t_ref, s_ref, out_ref):
    rows = out_ref.shape[0]
    pieces = t_ref.shape[0] // HT
    for head in range(HT):
        block = t_ref[head * pieces : (head + 1) * pieces].reshape(rows, DEPTH)
        out_ref[:, columns_of(order_ref, head)] = block
    for head in range(s_ref.shape[0]):
        out_ref[:, columns_of(order_ref, HT + head)] = s_ref[head]


def assemble(order, temporal, spatial, rows, width):
    return pl.pallas_call(
        assemble_kernel,
        out_shape=jax.ShapeDtypeStruct((rows, width), BF),
        in_specs=[SMEM, VMEM, VMEM],
        out_specs=VMEM,
        compiler_params=PARAMS,
    )(order, temporal, spatial)


def exchange(array, axes):
    return lax.all_to_all(array, axes, 0, 0, tiled=True)


def from_block(array, by):
    count = lax.axis_size("grp") * lax.axis_size("yh")
    return lax.ppermute(array, ("grp", "yh"), [((i + by) % count, i) for i in range(count)])


def local(queries, keys, values, head_order, key_blocks, block_count):
    rows, width = queries.shape
    blocks = lax.axis_size("grp") * lax.axis_size("yh")
    frames = blocks * BLOCK
    items = HT * rows // frames
    base = (lax.axis_index("grp") * lax.axis_size("yh") + lax.axis_index("yh")) * BLOCK
    base = base.astype(jnp.int32).reshape(1)

    block_axes = ("yl", "zl", "x")
    loop_axes = ("grp", "yh", "yl", "zl")
    st = pack_temporal(head_order, (queries, keys, values), items)
    qkv = exchange(pack_spatial(head_order, (queries, keys, values)), block_axes)
    pieces = qkv.shape[0] // BLOCK
    less = from_block(qkv[(BLOCK - W) * pieces :, 1:], -1)
    more = from_block(qkv[: W * pieces, 1:], 1)
    qkv, st = lax.optimization_barrier((qkv, st))
    at = exchange(st, loop_axes)
    acc, top, stat = attend_own(base, key_blocks, block_count, qkv, frames)
    to, stat = lax.optimization_barrier((temporal_attend(at), stat))
    tr = exchange(to, loop_axes)
    so = attend_near(base, key_blocks, block_count, stat, qkv, less, more, acc, top, frames)
    sr = exchange(so, block_axes)
    return assemble(head_order, tr, sr, rows, width)


def solution(mesh):
    grp, seq = mesh.shape["grp"], mesh.shape["seq"]
    fine = Mesh(mesh.devices.reshape(grp, seq // 16, 2, 2, 4), ("grp", "yh", "yl", "zl", "x"))
    tokens = P(("grp", "yh", "yl", "zl", "x"), None)
    return jax.shard_map(
        local,
        mesh=fine,
        in_specs=(tokens, tokens, tokens, P(), P(), P()),
        out_specs=tokens,
        check_vma=False,
    )
```

profile of v0, /device:TPU:1, one launch (start us, length us, event | category | flops | bytes accessed | tf_op | source)
XLA Modules:
  0.0 186.8 jit_solution(11113526476930770733)
XLA Ops:
  0.0 49.8 %shard_map.64 = bf16[16,3,128,128]{3,2,1,0:T(8,128)(2,1)} custom-call(s32[24]{0:T(128)} %order_ref.5, bf16[128,3072]{1,0:T(8,128)(2,1)} %refs_0_.1, bf16[128,3072]{1,0:T(8,128)(2,1)} %refs_1_.1, bf16[128,3072]{1,0:T(8,128)(2,1)} %refs_2_.1), custom_call_target="tpu_custom_call" | custom-call | tf_op jit(solution)/shard_map/pallas_call | solution.py:57
  49.9 7.8 %all-to-all-start = ((bf16[16,3,128,128]{3,2,1,0:T(8,128)(2,1)}), bf16[16,3,128,128]{3,2,1,0:T(8,128)(2,1)S(1)}, u32[]{:S(2)}, u32[]{:S(2)}) async-start(bf16[16,3,128,128]{3,2,1,0:T(8,128)(2,1)} %shard_map.64), calls=%async_computation | async-start | bytes 3145728 | tf_op jit(solution)/shard_map/all_to_all | solution.py:347
  57.6 25.8 %shard_map.65 = bf16[128,3,8,128]{3,2,1,0:T(8,128)(2,1)} custom-call(s32[24]{0:T(128)} %order_ref.5, bf16[16,8,3072]{2,1,0:T(8,128)(2,1)} %bitcast.4, bf16[16,8,3072]{2,1,0:T(8,128)(2,1)} %bitcast.5, bf16[16,8,3072]{2,1,0:T(8,128)(2,1)} %bitcast.6), custom_call_target="tpu_custom_call" | custom-call | flops 10000000000 | bytes 1048576 | tf_op jit(solution)/shard_map/pallas_call | solution.py:86
  83.5 0.0 copy-start.5
  83.5 0.0 all-to-all-done.in_ref
  83.5 16.5 %all-to-all-start.1 = ((bf16[128,3,8,128]{3,2,1,0:T(8,128)(2,1)}), bf16[128,3,8,128]{3,2,1,0:T(8,128)(2,1)S(1)}, u32[]{:S(2)}, u32[]{:S(2)}) async-start(bf16[128,3,8,128]{3,2,1,0:T(8,128)(2,1)} %shard_map.65), calls=%async_computation.1 | async-start | bytes 1572864 | tf_op jit(solution)/shard_map/all_to_all | solution.py:347
  100.0 0.0 copy-done.5
  100.1 0.1 copy.7.kb_ref
  100.2 0.0 copy-start.4
  100.2 1.5 fusion
  101.7 5.6 %collective-permute-start.1 = (bf16[12,2,128,128]{3,2,1,0:T(8,128)(2,1)}, bf16[12,2,128,128]{3,2,1,0:T(8,128)(2,1)}, u32[]{:S(2)}, u32[]{:S(2)}) collective-permute-start(bf16[12,2,128,128]{3,2,1,0:T(8,128)(2,1)} %get-tuple-element.19), channel_id=1, source_target_pairs={{16,0},{32,16},{48,32},{64,48},{80,64},{96,80},{112,96},{128,112},... | collective-permute-start | bytes 2359304 | tf_op jit(solution)/shard_map/ppermute | solution.py:352
  107.3 1.9 %collective-permute-start = (bf16[12,2,128,128]{3,2,1,0:T(8,128)(2,1)}, bf16[12,2,128,128]{3,2,1,0:T(8,128)(2,1)}, u32[]{:S(2)}, u32[]{:S(2)}) collective-permute-start(bf16[12,2,128,128]{3,2,1,0:T(8,128)(2,1)} %get-tuple-element.20), channel_id=1, source_target_pairs={{496,0},{0,16},{16,32},{32,48},{48,64},{64,80},{80,96},{96,112},{1... | collective-permute-start | bytes 2359304 | tf_op jit(solution)/shard_map/ppermute | solution.py:352
  109.2 0.0 copy-done.4
  109.2 21.5 %shard_map.67 = (f32[4,512,256]{2,1,0:T(8,128)S(1)}, f32[4,512,128]{2,1,0:T(8,128)S(1)}, f32[2]{0:T(128)S(1)}) custom-call(s32[1]{0:T(128)} %bitcast.3.base_ref, s32[128,6]{1,0:T(8,128)S(1)} %copy.7.kb_ref, s32[128]{0:T(128)S(1)} %copy-done.4, bf16[16,3,128,128]{3,2,1,0:T(8,128)(2,1)S(1)} %all-to-all-done.in_ref), custom_call_target="tpu_custom_call" | custom-call | flops 10000000000 | bytes 1048576 | tf_op jit(solution)/shard_map/pallas_call | solution.py:294
  130.7 0.0 copy-start
  130.8 1.3 copy-done
  132.1 0.0 all-to-all-done.1.in_ref
  132.1 2.1 %shard_map.66 = bf16[128,8,128]{2,1,0:T(8,128)(2,1)S(1)} custom-call(bf16[128,3,8,128]{3,2,1,0:T(8,128)(2,1)S(1)} %all-to-all-done.1.in_ref), custom_call_target="tpu_custom_call" | custom-call | flops 49999998976 | bytes 1048576 | tf_op jit(solution)/shard_map/pallas_call | solution.py:120
  134.2 0.0 copy-start.2
  134.2 0.7 copy-done.2
  134.9 9.0 %all-to-all-start.2 = ((bf16[128,8,128]{2,1,0:T(8,128)(2,1)}), bf16[128,8,128]{2,1,0:T(8,128)(2,1)S(1)}, u32[]{:S(2)}, u32[]{:S(2)}) async-start(bf16[128,8,128]{2,1,0:T(8,128)(2,1)} %copy-done.2), calls=%async_computation.2 | async-start | bytes 524288 | tf_op jit(solution)/shard_map/all_to_all | solution.py:347
  143.9 11.0 %collective-permute-done.1.more_ref = bf16[12,2,128,128]{3,2,1,0:T(8,128)(2,1)} collective-permute-done((bf16[12,2,128,128]{3,2,1,0:T(8,128)(2,1)}, bf16[12,2,128,128]{3,2,1,0:T(8,128)(2,1)}, u32[]{:S(2)}, u32[]{:S(2)}) %collective-permute-start.1) | collective-permute-done | bytes 786464 | tf_op jit(solution)/shard_map/ppermute | solution.py:352
  154.9 0.0 collective-permute-done.less_ref
  154.9 0.0 copy-start.1
  154.9 1.6 copy-done.1
  156.5 0.0 copy-start.3
  156.5 13.8 %shard_map.68 = bf16[16,128,128]{2,1,0:T(8,128)(2,1)S(1)} custom-call(s32[1]{0:T(128)} %bitcast.3.base_ref, s32[128,6]{1,0:T(8,128)S(1)} %copy.7.kb_ref, s32[128]{0:T(128)S(1)} %copy-done.4, f32[2]{0:T(128)S(1)} %get-tuple-element.16.stat_ref, bf16[16,3,128,128]{3,2,1,0:T(8,128)(2,1)S(1)} %all-to-all-done.in_ref, ...), custom_call_target="tpu_custom_call" | custom-call | tf_op jit(solution)/shard_map/pallas_call | solution.py:311
  170.3 0.0 all-to-all-done.2.t_ref
  170.3 14.9 %all_to_all.20.s_ref = bf16[16,128,128]{2,1,0:T(8,128)(2,1)S(1)} all-to-all(bf16[16,128,128]{2,1,0:T(8,128)(2,1)S(1)} %shard_map.68), channel_id=1, replica_groups=mesh['grp'=8,'yh'=4,'yl'=2,'zl'=2,'x'=4] {'yl','zl','x'}, dimensions={0} | all-to-all | bytes 1048576 | tf_op jit(solution)/shard_map/all_to_all | solution.py:347
  185.2 0.0 copy-done.3
  185.2 1.6 shard_map.69
Async XLA Ops:
  49.9 33.6 %all-to-all-start = ((bf16[16,3,128,128]{3,2,1,0:T(8,128)(2,1)}), bf16[16,3,128,128]{3,2,1,0:T(8,128)(2,1)S(1)}, u32[]{:S(2)}, u32[]{:S(2)}) async-start(bf16[16,3,128,128]{3,2,1,0:T(8,128)(2,1)} %shard_map.64), calls=%async_computation | async-start | bytes 3145728 | tf_op jit(solution)/shard_map/all_to_all | solution.py:347
  83.5 16.6 %copy-start.5 = (s32[128,6]{0,1:T(8,128)S(1)}, s32[128,6]{0,1:T(8,128)}, u32[]{:S(2)}) copy-start(s32[128,6]{0,1:T(8,128)} %param.10) | copy-start | bytes 9220
  83.5 48.6 %all-to-all-start.1 = ((bf16[128,3,8,128]{3,2,1,0:T(8,128)(2,1)}), bf16[128,3,8,128]{3,2,1,0:T(8,128)(2,1)S(1)}, u32[]{:S(2)}, u32[]{:S(2)}) async-start(bf16[128,3,8,128]{3,2,1,0:T(8,128)(2,1)} %shard_map.65), calls=%async_computation.1 | async-start | bytes 1572864 | tf_op jit(solution)/shard_map/all_to_all | solution.py:347
  100.2 9.1 %copy-start.4 = (s32[128]{0:T(128)S(1)}, s32[128]{0:T(128)}, u32[]{:S(2)}) copy-start(s32[128]{0:T(128)} %bc_ref.3) | copy-start | bytes 1540
  101.7 53.2 %collective-permute-start.1 = (bf16[12,2,128,128]{3,2,1,0:T(8,128)(2,1)}, bf16[12,2,128,128]{3,2,1,0:T(8,128)(2,1)}, u32[]{:S(2)}, u32[]{:S(2)}) collective-permute-start(bf16[12,2,128,128]{3,2,1,0:T(8,128)(2,1)} %get-tuple-element.19), channel_id=1, source_target_pairs={{16,0},{32,16},{48,32},{64,48},{80,64},{96,80},{112,96},{128,112},... | collective-permute-start | bytes 2359304 | tf_op jit(solution)/shard_map/ppermute | solution.py:352
  107.3 47.6 %collective-permute-start = (bf16[12,2,128,128]{3,2,1,0:T(8,128)(2,1)}, bf16[12,2,128,128]{3,2,1,0:T(8,128)(2,1)}, u32[]{:S(2)}, u32[]{:S(2)}) collective-permute-start(bf16[12,2,128,128]{3,2,1,0:T(8,128)(2,1)} %get-tuple-element.20), channel_id=1, source_target_pairs={{496,0},{0,16},{16,32},{32,48},{48,64},{64,80},{80,96},{96,112},{1... | collective-permute-start | bytes 2359304 | tf_op jit(solution)/shard_map/ppermute | solution.py:352
  130.7 1.3 copy-start
  134.2 0.7 copy-start.2
  134.9 35.3 %all-to-all-start.2 = ((bf16[128,8,128]{2,1,0:T(8,128)(2,1)}), bf16[128,8,128]{2,1,0:T(8,128)(2,1)S(1)}, u32[]{:S(2)}, u32[]{:S(2)}) async-start(bf16[128,8,128]{2,1,0:T(8,128)(2,1)} %copy-done.2), calls=%async_computation.2 | async-start | bytes 524288 | tf_op jit(solution)/shard_map/all_to_all | solution.py:347
  154.9 1.6 copy-start.1
  156.5 28.8 %copy-start.3 = (s32[24]{0:T(128)S(1)}, s32[24]{0:T(128)}, u32[]{:S(2)}) copy-start(s32[24]{0:T(128)} %order_ref.5) | copy-start | bytes 292
where the time goes:
time: 188 us; the launch traced here: 187 us
  Pallas kernels  115 us (61%)
  starting transfers between devices  40.9 us (22%)
  blocking collectives  14.9 us (8%)
  waiting for transfers between devices  11 us (6%)
  local copies, waits for them, and re-layouts  5.22 us (3%)
    pallas_call x1, Pallas kernels, pack_spatial(): pl.pallas_call(pack_spatial_kernel, out_shape=jax.ShapeDtypeStruct((heads...  49.8 us
    all_to_all x3, starting transfers between devices, exchange(): return lax.all_to_all(array, axes, 0, 0, tiled=True)  33.3 us
    pallas_call x1, Pallas kernels, pack_temporal(): pl.pallas_call(pack_temporal_kernel, out_shape=jax.ShapeDtypeStruct((HT *...  25.8 us
    pallas_call x1, Pallas kernels, attend_own(): pl.pallas_call(functools.partial(own_kernel, frames), out_shape=[jax.Shap...  21.5 us
    all_to_all x1, blocking collectives, exchange(): return lax.all_to_all(array, axes, 0, 0, tiled=True)  14.9 us
    pallas_call x1, Pallas kernels, attend_near(): pl.pallas_call(functools.partial(near_kernel, frames), out_shape=jax.Shap...  13.8 us
    ppermute x2, waiting for transfers between devices, from_block(): lax.ppermute(array, ('grp', 'yh'), [((i + by) % count, i) for i in range(...  11 us
    ppermute x2, starting transfers between devices, from_block(): lax.ppermute(array, ('grp', 'yh'), [((i + by) % count, i) for i in range(...  7.56 us
  transfers between devices with their start and end apart: 5, of which 1 were waited for; matrix products, arithmetic and copies ran while one was open for 1% of the time, Pallas kernels for 34%

commit v1 on v0

--- a/solution.py
+++ b/solution.py
@@ -58,73 +58,87 @@
         pack_spatial_kernel,
         out_shape=jax.ShapeDtypeStruct((heads, len(arrays), rows, DEPTH), BF),
         in_specs=[SMEM] + [ANY] * len(arrays),
-        out_specs=ANY,
+        out_specs=VMEM,
         scratch_shapes=[pltpu.SemaphoreType.DMA((len(arrays), heads))],
         compiler_params=PACK_PARAMS,
     )(order, *arrays)
 
 
-def pack_temporal_kernel(order_ref, *refs):
-    dst, sems = refs[-2:]
-    pieces = refs[0].shape[0]
-    copies = []
-    for which, src in enumerate(refs[:-2]):
-        for head in range(HT):
-            copies.append(
-                pltpu.make_async_copy(
-                    src.at[:, :, columns_of(order_ref, head)],
-                    dst.at[pl.ds(head * pieces, pieces), which],
-                    sems.at[which, head],
-                )
-            )
-    run_copies(copies)
-
-
-def pack_temporal(order, arrays, items):
-    rows, width = arrays[0].shape
-    pieces = rows // items
+def pack_temporal_kernel(order_ref, y_ref, q_ref, k_ref, v_ref, *outs):
+    _, side, _, items, _ = outs[0].shape
+    for away, out in enumerate(outs):
+        to = lax.rem(y_ref[0] + away, len(outs))
+        here = pl.ds(pl.multiple_of(to * (side * items), side * items), side * items)
+        for which, src in enumerate((q_ref, k_ref, v_ref)):
+            for head in range(HT):
+                block = src[here, columns_of(order_ref, head)]
+                out[head, :, which] = block.reshape(side, items, DEPTH)
+
+
+def pack_temporal(order, y, arrays, items, steps):
+    side = arrays[0].shape[0] // items // steps
+    out = jax.ShapeDtypeStruct((HT, side, len(arrays), items, DEPTH), BF)
     return pl.pallas_call(
         pack_temporal_kernel,
-        out_shape=jax.ShapeDtypeStruct((HT * pieces, len(arrays), items, DEPTH), BF),
-        in_specs=[SMEM] + [ANY] * len(arrays),
-        out_specs=ANY,
-        scratch_shapes=[pltpu.SemaphoreType.DMA((len(arrays), HT))],
-        compiler_params=PACK_PARAMS,
-        cost_estimate=estimate(10),
-    )(order, *[array.reshape(pieces, items, width) for array in arrays])
-
-
-def temporal_kernel(in_ref, out_ref):
-    frames, _, items, depth = in_ref.shape
-    total = frames * items
-    step = 256
-    factor = depth ** (-0.5) * math.log2(math.e)
-    k = in_ref[:, 1].reshape(total, depth)
-    v = in_ref[:, 2].reshape(total, depth)
+        out_shape=[out] * steps,
+        in_specs=[SMEM, SMEM] + [VMEM] * len(arrays),
+        out_specs=[VMEM] * steps,
+        compiler_params=PARAMS,
+    )(order, y, *arrays)
+
+
+def regroup_kernel(*refs):
+    dst = refs[-1]
+    for away, src in enumerate(refs[:-1]):
+        dst[:, away] = src[...].reshape(dst.shape[0], *dst.shape[2:])
+
+
+def regroup(parts):
+    heads, side, *rest = parts[0].shape
+    return pl.pallas_call(
+        regroup_kernel,
+        out_shape=jax.ShapeDtypeStruct((heads * side, len(parts), *rest), BF),
+        in_specs=[VMEM] * len(parts),
+        out_specs=VMEM,
+        compiler_params=PARAMS,
+    )(*parts)
+
+
+def temporal_kernel(y_ref, in_ref, out_ref):
+    planes, steps, _, items, depth = in_ref.shape
+    total = planes * steps * items
+    per = 4
+    step = per * steps * items
+    side = 2
+    k = in_ref[:, :, 1].reshape(total, depth)
+    v = in_ref[:, :, 2].reshape(total, depth)
     row_item = lax.broadcasted_iota(jnp.int32, (step, total), 0) % items
     col_item = lax.broadcasted_iota(jnp.int32, (step, total), 1) % items
     same = row_item == col_item
-    per = step // items
-    for at in range(frames // per):
-        q = in_ref[at * per : (at + 1) * per, 0].reshape(step, depth)
-        s = lax.dot_general(q, k, (((1,), (1,)), ((), ())), preferred_element_type=F32)
-        s = jnp.where(same, s * factor, -jnp.inf)
+    for at in range(planes // per):
+        q = in_ref[at * per : (at + 1) * per, :, 0].reshape(step, depth)
+        s = jnp.where(same, products(q, k) * score_factor(), -jnp.inf)
         p = jnp.exp2(s - jnp.max(s, axis=1, keepdims=True))
         total_p = jnp.sum(p, axis=1, keepdims=True)
         o = jnp.dot(p.astype(BF), v, preferred_element_type=F32) / total_p
-        out_ref[at * per : (at + 1) * per] = o.astype(BF).reshape(per, items, depth)
-
-
-def temporal_attend(arrived):
-    frames, _, items, depth = arrived.shape
+        o = o.astype(BF).reshape(per, steps, items, depth)
+        for plane in range(per):
+            grp, low = divmod(at * per + plane, side)
+            for away in range(steps):
+                y = lax.rem(y_ref[0] + steps - away, steps)
+                out_ref[(grp * steps + y) * side + low] = o[plane, away]
+
+
+def temporal_attend(y, arrived):
+    planes, steps, _, items, depth = arrived.shape
     return pl.pallas_call(
         temporal_kernel,
-        out_shape=jax.ShapeDtypeStruct((frames, items, depth), BF),
-        in_specs=[VMEM],
+        out_shape=jax.ShapeDtypeStruct((planes * steps, items, depth), BF),
+        in_specs=[SMEM, VMEM],
         out_specs=VMEM,
         compiler_params=PARAMS,
         cost_estimate=estimate(50),
-    )(arrived)
+    )(y, arrived)
 
 
 def row_norm(blocks):
@@ -352,6 +366,13 @@
     return lax.ppermute(array, ("grp", "yh"), [((i + by) % count, i) for i in range(count)])
 
 
+def along_y(array, by):
+    count = lax.axis_size("yh") * lax.axis_size("yl")
+    if by == 0:
+        return array
+    return lax.ppermute(array, ("yh", "yl"), [(i, (i + by) % count) for i in range(count)])
+
+
 def local(queries, keys, values, head_order, key_blocks, block_count):
     rows, width = queries.shape
     blocks = lax.axis_size("grp") * lax.axis_size("yh")
@@ -362,15 +383,18 @@
 
     block_axes = ("yl", "zl", "x")
     loop_axes = ("grp", "yh", "yl", "zl")
-    st = pack_temporal(head_order, (queries, keys, values), items)
+    steps = lax.axis_size("yh") * lax.axis_size("yl")
+    y = (lax.axis_index("yh") * lax.axis_size("yl") + lax.axis_index("yl")).astype(jnp.int32).reshape(1)
+    st = pack_temporal(head_order, y, (queries, keys, values), items, steps)
+    st = [along_y(part, away) for away, part in enumerate(st)]
     qkv = exchange(pack_spatial(head_order, (queries, keys, values)), block_axes)
     pieces = qkv.shape[0] // BLOCK
     less = from_block(qkv[(BLOCK - W) * pieces :, 1:], -1)
     more = from_block(qkv[: W * pieces, 1:], 1)
     qkv, st = lax.optimization_barrier((qkv, st))
-    at = exchange(st, loop_axes)
+    at = exchange(regroup(st), ("grp", "zl"))
     acc, top, stat = attend_own(base, key_blocks, block_count, qkv, frames)
-    to, stat = lax.optimization_barrier((temporal_attend(at), stat))
+    to, stat = lax.optimization_barrier((temporal_attend(y, at), stat))
     tr = exchange(to, loop_axes)
     so = attend_near(base, key_blocks, block_count, stat, qkv, less, more, acc, top, frames)
     sr = exchange(so, block_axes)

time: 188 us -> 142 us (0.76)
  Pallas kernels: 115 us -> 32.4 us
  starting transfers between devices: 40.9 us -> 72.1 us
  waiting for transfers between devices: 11 us -> 14.9 us
    pallas_call x1, Pallas kernels: 49.8 us -> 3.64 us  [pack_spatial(): pl.pallas_call(pack_spatial_kernel, out_shape=jax.ShapeDtypeStruct((heads...]
    ppermute x0 -> x7, starting transfers between devices: none -> 29.8 us  [along_y(): lax.ppermute(array, ('yh', 'yl'), [(i, (i + by) % count) for i in range(c...]
    pallas_call x2 -> x3, Pallas kernels: 27.9 us -> 3.85 us  [the longest x1 2.13 us: temporal_attend(): pl.pallas_call(temporal_kernel, out_shape=jax.ShapeDtypeStruct((planes *...]
    ppermute x2, waiting for transfers between devices: 11 us -> 0.01 us  [from_block(): lax.ppermute(array, ('grp', 'yh'), [((i + by) % count, i) for i in range(...]
    all_to_all x3, waiting for transfers between devices: 0.01 us -> 9.57 us  [exchange(): return lax.all_to_all(array, axes, 0, 0, tiled=True)]
    pallas_call x1, Pallas kernels: 21.5 us -> 13.1 us  [attend_own(): pl.pallas_call(functools.partial(own_kernel, frames), out_shape=[jax.Shap...]
    ppermute x0 -> x7, waiting for transfers between devices: none -> 5.29 us  [along_y(): lax.ppermute(array, ('yh', 'yl'), [(i, (i + by) % count) for i in range(c...]
    pallas_call x1, Pallas kernels: 13.8 us -> 10.2 us  [attend_near(): pl.pallas_call(functools.partial(near_kernel, frames), out_shape=jax.Shap...]
  transfers between devices with their start and end apart: 5 -> 12, of which waited for: 1 -> 6; matrix products, arithmetic and copies ran while one was open for 1% -> 1% of each run, Pallas kernels for 34% -> 19%
where the time goes in v1:
time: 142 us; the launch traced here: 141 us
  starting transfers between devices  72.1 us (51%)
  Pallas kernels  32.4 us (23%)
  blocking collectives  15.5 us (11%)
  waiting for transfers between devices  14.9 us (10%)
  local copies, waits for them, and re-layouts  6.39 us (4%)
    all_to_all x3, starting transfers between devices, exchange(): return lax.all_to_all(array, axes, 0, 0, tiled=True)  36 us
    ppermute x7, starting transfers between devices, along_y(): lax.ppermute(array, ('yh', 'yl'), [(i, (i + by) % count) for i in range(c...  29.8 us
    all_to_all x1, blocking collectives, exchange(): return lax.all_to_all(array, axes, 0, 0, tiled=True)  15.5 us
    pallas_call x1, Pallas kernels, attend_own(): pl.pallas_call(functools.partial(own_kernel, frames), out_shape=[jax.Shap...  13.1 us
    pallas_call x1, Pallas kernels, attend_near(): pl.pallas_call(functools.partial(near_kernel, frames), out_shape=jax.Shap...  10.2 us
    all_to_all x3, waiting for transfers between devices, exchange(): return lax.all_to_all(array, axes, 0, 0, tiled=True)  9.57 us
    ppermute x2, starting transfers between devices, from_block(): lax.ppermute(array, ('grp', 'yh'), [((i + by) % count, i) for i in range(...  6.2 us
    ppermute x7, waiting for transfers between devices, along_y(): lax.ppermute(array, ('yh', 'yl'), [(i, (i + by) % count) for i in range(c...  5.29 us
  transfers between devices with their start and end apart: 12, of which 6 were waited for; matrix products, arithmetic and copies ran while one was open for 1% of the time, Pallas kernels for 19%

profile of v1, /device:TPU:1, one launch (start us, length us, event | category | flops | bytes accessed | tf_op | source)
XLA Modules:
  0.0 141.5 jit_solution(190761839472776795)
XLA Ops:
  0.0 3.6 %shard_map.64 = bf16[16,3,128,128]{3,2,1,0:T(8,128)(2,1)} custom-call(s32[24]{0:T(128)} %order_ref.5, bf16[128,3072]{1,0:T(8,128)(2,1)} %q_ref.1, bf16[128,3072]{1,0:T(8,128)(2,1)} %k_ref.1, bf16[128,3072]{1,0:T(8,128)(2,1)} %v_ref.1), custom_call_target="tpu_custom_call" | custom-call | tf_op jit(solution)/shard_map/pallas_call | solution.py:57
  3.6 0.0 copy-start
  3.7 0.0 copy-start.1
  3.7 0.0 copy-start.6
  3.7 7.9 %all-to-all-start = ((bf16[16,3,128,128]{3,2,1,0:T(8,128)(2,1)}), bf16[16,3,128,128]{3,2,1,0:T(8,128)(2,1)S(1)}, u32[]{:S(2)}, u32[]{:S(2)}) async-start(bf16[16,3,128,128]{3,2,1,0:T(8,128)(2,1)} %shard_map.64), calls=%async_computation | async-start | bytes 3145728 | tf_op jit(solution)/shard_map/all_to_all | solution.py:361
  11.6 0.0 copy-done
  11.6 0.0 copy-done.1
  11.6 0.0 copy-done.6
  11.7 0.0 copy-start.2
  11.7 1.1 copy-done.2
  12.8 0.8 shard_map.65
  13.6 3.3 %collective-permute-start = (bf16[8,2,3,8,128]{4,3,2,1,0:T(8,128)(2,1)S(1)}, bf16[8,2,3,8,128]{4,3,2,1,0:T(8,128)(2,1)S(1)}, u32[]{:S(2)}, u32[]{:S(2)}) collective-permute-start(bf16[8,2,3,8,128]{4,3,2,1,0:T(8,128)(2,1)S(1)} %get-tuple-element.28), channel_id=1, source_target_pairs={{0,8},{8,16},{16,24},{24,32},{32,40},{40,48},{48,56},{56,0},{1,9},... | collective-permute-start | bytes 294920 | tf_op jit(solution)/shard_map/ppermute | solution.py:373
  16.8 4.2 %collective-permute-start.1 = (bf16[8,2,3,8,128]{4,3,2,1,0:T(8,128)(2,1)S(1)}, bf16[8,2,3,8,128]{4,3,2,1,0:T(8,128)(2,1)S(1)}, u32[]{:S(2)}, u32[]{:S(2)}) collective-permute-start(bf16[8,2,3,8,128]{4,3,2,1,0:T(8,128)(2,1)S(1)} %get-tuple-element.29), channel_id=1, source_target_pairs={{0,16},{8,24},{16,32},{24,40},{32,48},{40,56},{48,0},{56,8},{1,17}... | collective-permute-start | bytes 294920 | tf_op jit(solution)/shard_map/ppermute | solution.py:373
  21.1 4.3 %collective-permute-start.2 = (bf16[8,2,3,8,128]{4,3,2,1,0:T(8,128)(2,1)S(1)}, bf16[8,2,3,8,128]{4,3,2,1,0:T(8,128)(2,1)S(1)}, u32[]{:S(2)}, u32[]{:S(2)}) collective-permute-start(bf16[8,2,3,8,128]{4,3,2,1,0:T(8,128)(2,1)S(1)} %get-tuple-element.30), channel_id=1, source_target_pairs={{0,24},{8,32},{16,40},{24,48},{32,56},{40,0},{48,8},{56,16},{1,25}... | collective-permute-start | bytes 294920 | tf_op jit(solution)/shard_map/ppermute | solution.py:373
  25.3 3.9 %collective-permute-start.3 = (bf16[8,2,3,8,128]{4,3,2,1,0:T(8,128)(2,1)S(1)}, bf16[8,2,3,8,128]{4,3,2,1,0:T(8,128)(2,1)S(1)}, u32[]{:S(2)}, u32[]{:S(2)}) collective-permute-start(bf16[8,2,3,8,128]{4,3,2,1,0:T(8,128)(2,1)S(1)} %get-tuple-element.31), channel_id=1, source_target_pairs={{0,32},{8,40},{16,48},{24,56},{32,0},{40,8},{48,16},{56,24},{1,33}... | collective-permute-start | bytes 294920 | tf_op jit(solution)/shard_map/ppermute | solution.py:373
  29.2 4.9 %collective-permute-start.4 = (bf16[8,2,3,8,128]{4,3,2,1,0:T(8,128)(2,1)S(1)}, bf16[8,2,3,8,128]{4,3,2,1,0:T(8,128)(2,1)S(1)}, u32[]{:S(2)}, u32[]{:S(2)}) collective-permute-start(bf16[8,2,3,8,128]{4,3,2,1,0:T(8,128)(2,1)S(1)} %get-tuple-element.32), channel_id=1, source_target_pairs={{0,40},{8,48},{16,56},{24,0},{32,8},{40,16},{48,24},{56,32},{1,41}... | collective-permute-start | bytes 294920 | tf_op jit(solution)/shard_map/ppermute | solution.py:373
  34.1 0.0 collective-permute-done.refs_1_
  34.1 5.1 %collective-permute-start.5 = (bf16[8,2,3,8,128]{4,3,2,1,0:T(8,128)(2,1)S(1)}, bf16[8,2,3,8,128]{4,3,2,1,0:T(8,128)(2,1)S(1)}, u32[]{:S(2)}, u32[]{:S(2)}) collective-permute-start(bf16[8,2,3,8,128]{4,3,2,1,0:T(8,128)(2,1)S(1)} %get-tuple-element.33), channel_id=1, source_target_pairs={{0,48},{8,56},{16,0},{24,8},{32,16},{40,24},{48,32},{56,40},{1,49}... | collective-permute-start | bytes 294920 | tf_op jit(solution)/shard_map/ppermute | solution.py:373
  39.3 0.6 collective-permute-done.1.refs_2_
  39.9 4.1 %collective-permute-start.6 = (bf16[8,2,3,8,128]{4,3,2,1,0:T(8,128)(2,1)S(1)}, bf16[8,2,3,8,128]{4,3,2,1,0:T(8,128)(2,1)S(1)}, u32[]{:S(2)}, u32[]{:S(2)}) collective-permute-start(bf16[8,2,3,8,128]{4,3,2,1,0:T(8,128)(2,1)S(1)} %get-tuple-element.34), channel_id=1, source_target_pairs={{0,56},{8,0},{16,8},{24,16},{32,24},{40,32},{48,40},{56,48},{1,57}... | collective-permute-start | bytes 294920 | tf_op jit(solution)/shard_map/ppermute | solution.py:373
  44.1 0.0 collective-permute-done.2.refs_3_
  44.1 2.7 %collective-permute-done.3.refs_4_ = bf16[8,2,3,8,128]{4,3,2,1,0:T(8,128)(2,1)S(1)} collective-permute-done((bf16[8,2,3,8,128]{4,3,2,1,0:T(8,128)(2,1)S(1)}, bf16[8,2,3,8,128]{4,3,2,1,0:T(8,128)(2,1)S(1)}, u32[]{:S(2)}, u32[]{:S(2)}) %collective-permute-start.3) | collective-permute-done | bytes 98336 | tf_op jit(solution)/shard_map/ppermute | solution.py:373
  46.8 0.0 collective-permute-done.4.refs_5_
  46.8 1.1 collective-permute-done.5.refs_6_
  47.9 0.9 collective-permute-done.6.refs_7_
  48.7 0.0 all-to-all-done.in_ref
  48.7 0.9 shard_map.66
  49.7 11.7 %all-to-all-start.1 = ((bf16[16,8,3,8,128]{4,3,2,1,0:T(8,128)(2,1)}), bf16[16,8,3,8,128]{4,3,2,1,0:T(8,128)(2,1)S(1)}, u32[]{:S(2)}, u32[]{:S(2)}) async-start(bf16[16,8,3,8,128]{4,3,2,1,0:T(8,128)(2,1)} %shard_map.66), calls=%async_computation.1 | async-start | bytes 1572864 | tf_op jit(solution)/shard_map/all_to_all | solution.py:361
  61.4 0.0 copy-done.8
  61.4 0.1 copy.7.kb_ref
  61.5 1.5 %fusion = (bf16[12,2,128,128]{3,2,1,0:T(8,128)(2,1)}, bf16[12,2,128,128]{3,2,1,0:T(8,128)(2,1)}) fusion(bf16[16,3,128,128]{3,2,1,0:T(8,128)(2,1)S(1)} %all-to-all-done.in_ref), kind=kLoop, calls=%fused_computation | loop fusion | bytes 3145728 | tf_op jit(solution)/shard_map/slice | solution.py:393
  63.0 3.9 %collective-permute-start.8 = (bf16[12,2,128,128]{3,2,1,0:T(8,128)(2,1)}, bf16[12,2,128,128]{3,2,1,0:T(8,128)(2,1)}, u32[]{:S(2)}, u32[]{:S(2)}) collective-permute-start(bf16[12,2,128,128]{3,2,1,0:T(8,128)(2,1)} %get-tuple-element.49), channel_id=1, source_target_pairs={{16,0},{32,16},{48,32},{64,48},{80,64},{96,80},{112,96},{128,112},... | collective-permute-start | bytes 2359304 | tf_op jit(solution)/shard_map/ppermute | solution.py:366
  66.9 2.3 %collective-permute-start.7 = (bf16[12,2,128,128]{3,2,1,0:T(8,128)(2,1)}, bf16[12,2,128,128]{3,2,1,0:T(8,128)(2,1)}, u32[]{:S(2)}, u32[]{:S(2)}) collective-permute-start(bf16[12,2,128,128]{3,2,1,0:T(8,128)(2,1)} %get-tuple-element.50), channel_id=1, source_target_pairs={{496,0},{0,16},{16,32},{32,48},{48,64},{64,80},{80,96},{96,112},{1... | collective-permute-start | bytes 2359304 | tf_op jit(solution)/shard_map/ppermute | solution.py:366
  69.2 0.0 copy-done.7
  69.3 13.1 %shard_map.68 = (f32[4,512,256]{2,1,0:T(8,128)S(1)}, f32[4,512,128]{2,1,0:T(8,128)S(1)}, f32[2]{0:T(128)S(1)}) custom-call(s32[1]{0:T(128)} %bitcast.1.base_ref, s32[128,6]{1,0:T(8,128)S(1)} %copy.7.kb_ref, s32[128]{0:T(128)S(1)} %copy-done.7, bf16[16,3,128,128]{3,2,1,0:T(8,128)(2,1)S(1)} %all-to-all-done.in_ref), custom_call_target="tpu_custom_call" | custom-call | flops 10000000000 | bytes 1048576 | tf_op jit(solution)/shard_map/pallas_call | solution.py:308
  82.4 1.3 copy-done.3
  83.7 6.9 %all-to-all-done.1.in_ref = bf16[16,8,3,8,128]{4,3,2,1,0:T(8,128)(2,1)S(1)} async-done(((bf16[16,8,3,8,128]{4,3,2,1,0:T(8,128)(2,1)}), bf16[16,8,3,8,128]{4,3,2,1,0:T(8,128)(2,1)S(1)}, u32[]{:S(2)}, u32[]{:S(2)}) %all-to-all-start.1) | async-done | bytes 786464 | tf_op jit(solution)/shard_map/all_to_all | solution.py:361
  90.6 2.1 %shard_map.67 = bf16[128,8,128]{2,1,0:T(8,128)(2,1)S(1)} custom-call(s32[1]{0:T(128)} %bitcast.y_ref, bf16[16,8,3,8,128]{4,3,2,1,0:T(8,128)(2,1)S(1)} %all-to-all-done.1.in_ref), custom_call_target="tpu_custom_call" | custom-call | flops 49999998976 | bytes 1048576 | tf_op jit(solution)/shard_map/pallas_call | solution.py:134
  92.7 0.0 copy-start.5
  92.8 0.7 copy-done.5
  93.5 16.4 %all-to-all-start.2 = ((bf16[128,8,128]{2,1,0:T(8,128)(2,1)}), bf16[128,8,128]{2,1,0:T(8,128)(2,1)S(1)}, u32[]{:S(2)}, u32[]{:S(2)}) async-start(bf16[128,8,128]{2,1,0:T(8,128)(2,1)} %copy-done.5), calls=%async_computation.2 | async-start | bytes 524288 | tf_op jit(solution)/shard_map/all_to_all | solution.py:361
  109.9 0.0 collective-permute-done.8.more_ref
  109.9 0.0 collective-permute-done.7.less_ref
  109.9 1.6 %copy-done.4 = f32[4,512,256]{2,1,0:T(8,128)S(1)} copy-done((f32[4,512,256]{2,1,0:T(8,128)S(1)}, f32[4,512,256]{2,1,0:T(8,128)}, u32[]{:S(2)}) %copy-start.4) | copy-done | bytes 2097176
  111.5 10.2 %shard_map.69 = bf16[16,128,128]{2,1,0:T(8,128)(2,1)S(1)} custom-call(s32[1]{0:T(128)} %bitcast.1.base_ref, s32[128,6]{1,0:T(8,128)S(1)} %copy.7.kb_ref, s32[128]{0:T(128)S(1)} %copy-done.7, f32[2]{0:T(128)S(1)} %get-tuple-element.46.stat_ref, bf16[16,3,128,128]{3,2,1,0:T(8,128)(2,1)S(1)} %all-to-all-done.in_ref, ...), custom_call_target="tpu_custom_call" | custom-call | tf_op jit(solution)/shard_map/pallas_call | solution.py:325
  121.7 2.7 %all-to-all-done.2.t_ref = bf16[128,8,128]{2,1,0:T(8,128)(2,1)S(1)} async-done(((bf16[128,8,128]{2,1,0:T(8,128)(2,1)}), bf16[128,8,128]{2,1,0:T(8,128)(2,1)S(1)}, u32[]{:S(2)}, u32[]{:S(2)}) %all-to-all-start.2) | async-done | bytes 262176 | tf_op jit(solution)/shard_map/all_to_all | solution.py:361
  124.4 15.5 %all_to_all.20.s_ref = bf16[16,128,128]{2,1,0:T(8,128)(2,1)S(1)} all-to-all(bf16[16,128,128]{2,1,0:T(8,128)(2,1)S(1)} %shard_map.69), channel_id=1, replica_groups=mesh['grp'=8,'yh'=4,'yl'=2,'zl'=2,'x'=4] {'yl','zl','x'}, dimensions={0} | all-to-all | bytes 1048576 | tf_op jit(solution)/shard_map/all_to_all | solution.py:361
  139.9 1.6 %shard_map.70 = bf16[128,3072]{1,0:T(8,128)(2,1)} custom-call(s32[24]{0:T(128)S(1)} %copy-done.6, bf16[128,8,128]{2,1,0:T(8,128)(2,1)S(1)} %all-to-all-done.2.t_ref, bf16[16,128,128]{2,1,0:T(8,128)(2,1)S(1)} %all_to_all.20.s_ref), custom_call_target="tpu_custom_call" | custom-call | tf_op jit(solution)/shard_map/pallas_call | solution.py:351
  (4 shorter events, 0.0 us)
Async XLA Ops:
  3.6 8.0 %copy-start = (bf16[128,3072]{1,0:T(8,128)(2,1)S(1)}, bf16[128,3072]{1,0:T(8,128)(2,1)}, u32[]{:S(2)}) copy-start(bf16[128,3072]{1,0:T(8,128)(2,1)} %q_ref.1) | copy-start | bytes 2359300
  3.7 8.0 %copy-start.1 = (bf16[128,3072]{1,0:T(8,128)(2,1)S(1)}, bf16[128,3072]{1,0:T(8,128)(2,1)}, u32[]{:S(2)}) copy-start(bf16[128,3072]{1,0:T(8,128)(2,1)} %k_ref.1) | copy-start | bytes 2359300
  3.7 8.0 %copy-start.6 = (s32[24]{0:T(128)S(1)}, s32[24]{0:T(128)}, u32[]{:S(2)}) copy-start(s32[24]{0:T(128)} %order_ref.5) | copy-start | bytes 292
  3.7 45.1 %all-to-all-start = ((bf16[16,3,128,128]{3,2,1,0:T(8,128)(2,1)}), bf16[16,3,128,128]{3,2,1,0:T(8,128)(2,1)S(1)}, u32[]{:S(2)}, u32[]{:S(2)}) async-start(bf16[16,3,128,128]{3,2,1,0:T(8,128)(2,1)} %shard_map.64), calls=%async_computation | async-start | bytes 3145728 | tf_op jit(solution)/shard_map/all_to_all | solution.py:361
  11.7 1.1 copy-start.2
  13.6 20.6 %collective-permute-start = (bf16[8,2,3,8,128]{4,3,2,1,0:T(8,128)(2,1)S(1)}, bf16[8,2,3,8,128]{4,3,2,1,0:T(8,128)(2,1)S(1)}, u32[]{:S(2)}, u32[]{:S(2)}) collective-permute-start(bf16[8,2,3,8,128]{4,3,2,1,0:T(8,128)(2,1)S(1)} %get-tuple-element.28), channel_id=1, source_target_pairs={{0,8},{8,16},{16,24},{24,32},{32,40},{40,48},{48,56},{56,0},{1,9},... | collective-permute-start | bytes 294920 | tf_op jit(solution)/shard_map/ppermute | solution.py:373
  16.8 23.1 %collective-permute-start.1 = (bf16[8,2,3,8,128]{4,3,2,1,0:T(8,128)(2,1)S(1)}, bf16[8,2,3,8,128]{4,3,2,1,0:T(8,128)(2,1)S(1)}, u32[]{:S(2)}, u32[]{:S(2)}) collective-permute-start(bf16[8,2,3,8,128]{4,3,2,1,0:T(8,128)(2,1)S(1)} %get-tuple-element.29), channel_id=1, source_target_pairs={{0,16},{8,24},{16,32},{24,40},{32,48},{40,56},{48,0},{56,8},{1,17}... | collective-permute-start | bytes 294920 | tf_op jit(solution)/shard_map/ppermute | solution.py:373
  21.1 23.0 %collective-permute-start.2 = (bf16[8,2,3,8,128]{4,3,2,1,0:T(8,128)(2,1)S(1)}, bf16[8,2,3,8,128]{4,3,2,1,0:T(8,128)(2,1)S(1)}, u32[]{:S(2)}, u32[]{:S(2)}) collective-permute-start(bf16[8,2,3,8,128]{4,3,2,1,0:T(8,128)(2,1)S(1)} %get-tuple-element.30), channel_id=1, source_target_pairs={{0,24},{8,32},{16,40},{24,48},{32,56},{40,0},{48,8},{56,16},{1,25}... | collective-permute-start | bytes 294920 | tf_op jit(solution)/shard_map/ppermute | solution.py:373
  25.3 21.4 %collective-permute-start.3 = (bf16[8,2,3,8,128]{4,3,2,1,0:T(8,128)(2,1)S(1)}, bf16[8,2,3,8,128]{4,3,2,1,0:T(8,128)(2,1)S(1)}, u32[]{:S(2)}, u32[]{:S(2)}) collective-permute-start(bf16[8,2,3,8,128]{4,3,2,1,0:T(8,128)(2,1)S(1)} %get-tuple-element.31), channel_id=1, source_target_pairs={{0,32},{8,40},{16,48},{24,56},{32,0},{40,8},{48,16},{56,24},{1,33}... | collective-permute-start | bytes 294920 | tf_op jit(solution)/shard_map/ppermute | solution.py:373
  29.2 17.6 %collective-permute-start.4 = (bf16[8,2,3,8,128]{4,3,2,1,0:T(8,128)(2,1)S(1)}, bf16[8,2,3,8,128]{4,3,2,1,0:T(8,128)(2,1)S(1)}, u32[]{:S(2)}, u32[]{:S(2)}) collective-permute-start(bf16[8,2,3,8,128]{4,3,2,1,0:T(8,128)(2,1)S(1)} %get-tuple-element.32), channel_id=1, source_target_pairs={{0,40},{8,48},{16,56},{24,0},{32,8},{40,16},{48,24},{56,32},{1,41}... | collective-permute-start | bytes 294920 | tf_op jit(solution)/shard_map/ppermute | solution.py:373
  34.1 13.7 %collective-permute-start.5 = (bf16[8,2,3,8,128]{4,3,2,1,0:T(8,128)(2,1)S(1)}, bf16[8,2,3,8,128]{4,3,2,1,0:T(8,128)(2,1)S(1)}, u32[]{:S(2)}, u32[]{:S(2)}) collective-permute-start(bf16[8,2,3,8,128]{4,3,2,1,0:T(8,128)(2,1)S(1)} %get-tuple-element.33), channel_id=1, source_target_pairs={{0,48},{8,56},{16,0},{24,8},{32,16},{40,24},{48,32},{56,40},{1,49}... | collective-permute-start | bytes 294920 | tf_op jit(solution)/shard_map/ppermute | solution.py:373
  39.9 8.8 %collective-permute-start.6 = (bf16[8,2,3,8,128]{4,3,2,1,0:T(8,128)(2,1)S(1)}, bf16[8,2,3,8,128]{4,3,2,1,0:T(8,128)(2,1)S(1)}, u32[]{:S(2)}, u32[]{:S(2)}) collective-permute-start(bf16[8,2,3,8,128]{4,3,2,1,0:T(8,128)(2,1)S(1)} %get-tuple-element.34), channel_id=1, source_target_pairs={{0,56},{8,0},{16,8},{24,16},{32,24},{40,32},{48,40},{56,48},{1,57}... | collective-permute-start | bytes 294920 | tf_op jit(solution)/shard_map/ppermute | solution.py:373
  48.7 12.6 %copy-start.8 = (s32[128,6]{0,1:T(8,128)S(1)}, s32[128,6]{0,1:T(8,128)}, u32[]{:S(2)}) copy-start(s32[128,6]{0,1:T(8,128)} %param.10) | copy-start | bytes 9220
  49.7 40.9 %all-to-all-start.1 = ((bf16[16,8,3,8,128]{4,3,2,1,0:T(8,128)(2,1)}), bf16[16,8,3,8,128]{4,3,2,1,0:T(8,128)(2,1)S(1)}, u32[]{:S(2)}, u32[]{:S(2)}) async-start(bf16[16,8,3,8,128]{4,3,2,1,0:T(8,128)(2,1)} %shard_map.66), calls=%async_computation.1 | async-start | bytes 1572864 | tf_op jit(solution)/shard_map/all_to_all | solution.py:361
  61.5 7.7 %copy-start.7 = (s32[128]{0:T(128)S(1)}, s32[128]{0:T(128)}, u32[]{:S(2)}) copy-start(s32[128]{0:T(128)} %bc_ref.3) | copy-start | bytes 1540
  63.0 46.9 %collective-permute-start.8 = (bf16[12,2,128,128]{3,2,1,0:T(8,128)(2,1)}, bf16[12,2,128,128]{3,2,1,0:T(8,128)(2,1)}, u32[]{:S(2)}, u32[]{:S(2)}) collective-permute-start(bf16[12,2,128,128]{3,2,1,0:T(8,128)(2,1)} %get-tuple-element.49), channel_id=1, source_target_pairs={{16,0},{32,16},{48,32},{64,48},{80,64},{96,80},{112,96},{128,112},... | collective-permute-start | bytes 2359304 | tf_op jit(solution)/shard_map/ppermute | solution.py:366
  66.9 43.0 %collective-permute-start.7 = (bf16[12,2,128,128]{3,2,1,0:T(8,128)(2,1)}, bf16[12,2,128,128]{3,2,1,0:T(8,128)(2,1)}, u32[]{:S(2)}, u32[]{:S(2)}) collective-permute-start(bf16[12,2,128,128]{3,2,1,0:T(8,128)(2,1)} %get-tuple-element.50), channel_id=1, source_target_pairs={{496,0},{0,16},{16,32},{32,48},{48,64},{64,80},{80,96},{96,112},{1... | collective-permute-start | bytes 2359304 | tf_op jit(solution)/shard_map/ppermute | solution.py:366
  82.4 1.3 copy-start.3
  92.7 0.7 copy-start.5
  93.5 30.9 %all-to-all-start.2 = ((bf16[128,8,128]{2,1,0:T(8,128)(2,1)}), bf16[128,8,128]{2,1,0:T(8,128)(2,1)S(1)}, u32[]{:S(2)}, u32[]{:S(2)}) async-start(bf16[128,8,128]{2,1,0:T(8,128)(2,1)} %copy-done.5), calls=%async_computation.2 | async-start | bytes 524288 | tf_op jit(solution)/shard_map/all_to_all | solution.py:361
  109.9 1.6 %copy-start.4 = (f32[4,512,256]{2,1,0:T(8,128)S(1)}, f32[4,512,256]{2,1,0:T(8,128)}, u32[]{:S(2)}) copy-start(f32[4,512,256]{2,1,0:T(8,128)} %copy-done.3) | copy-start | bytes 6291460

commit v2 on v0

--- a/solution.py
+++ b/solution.py
@@ -58,40 +58,29 @@
         pack_spatial_kernel,
         out_shape=jax.ShapeDtypeStruct((heads, len(arrays), rows, DEPTH), BF),
         in_specs=[SMEM] + [ANY] * len(arrays),
-        out_specs=ANY,
+        out_specs=VMEM,
         scratch_shapes=[pltpu.SemaphoreType.DMA((len(arrays), heads))],
         compiler_params=PACK_PARAMS,
     )(order, *arrays)
 
 
-def pack_temporal_kernel(order_ref, *refs):
-    dst, sems = refs[-2:]
-    pieces = refs[0].shape[0]
-    copies = []
-    for which, src in enumerate(refs[:-2]):
+def pack_temporal_kernel(items, order_ref, q_ref, k_ref, v_ref, out_ref):
+    pieces = q_ref.shape[0] // items
+    for which, src in enumerate((q_ref, k_ref, v_ref)):
         for head in range(HT):
-            copies.append(
-                pltpu.make_async_copy(
-                    src.at[:, :, columns_of(order_ref, head)],
-                    dst.at[pl.ds(head * pieces, pieces), which],
-                    sems.at[which, head],
-                )
-            )
-    run_copies(copies)
-
-
-def pack_temporal(order, arrays, items):
-    rows, width = arrays[0].shape
-    pieces = rows // items
-    return pl.pallas_call(
-        pack_temporal_kernel,
-        out_shape=jax.ShapeDtypeStruct((HT * pieces, len(arrays), items, DEPTH), BF),
-        in_specs=[SMEM] + [ANY] * len(arrays),
-        out_specs=ANY,
-        scratch_shapes=[pltpu.SemaphoreType.DMA((len(arrays), HT))],
-        compiler_params=PACK_PARAMS,
-        cost_estimate=estimate(10),
-    )(order, *[array.reshape(pieces, items, width) for array in arrays])
+            block = src[:, columns_of(order_ref, head)]
+            out_ref[head * pieces : (head + 1) * pieces, which] = block.reshape(pieces, items, DEPTH)
+
+
+def pack_temporal(order, q, k, v, items):
+    dests = HT * q.shape[0] // items
+    return pl.pallas_call(
+        functools.partial(pack_temporal_kernel, items),
+        out_shape=jax.ShapeDtypeStruct((dests, 3, items, DEPTH), BF),
+        in_specs=[SMEM] + [VMEM] * 3,
+        out_specs=VMEM,
+        compiler_params=PARAMS,
+    )(order, q, k, v)
 
 
 def temporal_kernel(in_ref, out_ref):
@@ -186,11 +175,14 @@
     return block.reshape(pieces * block.shape[1], DEPTH)
 
 
-def own_kernel(frames, base_ref, kb_ref, bc_ref, in_ref, acc_ref, m_ref, stat_ref):
-    pieces = in_ref.shape[0] // BLOCK
-    size = pieces * in_ref.shape[2]
+def own_kernel(frames, base_ref, kb_ref, bc_ref, q_ref, kv_ref, acc_ref, m_ref, stat_ref):
+    pieces = q_ref.shape[0] // BLOCK
+    size = pieces * q_ref.shape[2]
     base = base_ref[0]
-    part = functools.partial(frame_at, in_ref, pieces=pieces)
+
+    def part(which, at):
+        return frame_at(kv_ref, which - 1, at, pieces) if which else frame_at(q_ref, 0, at, pieces)
+
     q_norm = row_norm([part(0, at) for at in range(BLOCK)])
     k_norm = row_norm([part(1, at) for at in range(BLOCK)])
     fast = small_scores(q_norm, k_norm)
@@ -230,24 +222,32 @@
 
 
 def near_kernel(
-    frames, base_ref, kb_ref, bc_ref, stat_ref, in_ref, less_ref, more_ref, acc_in, m_in, o_ref,
-    acc_ref, m_ref, near_ref, sems
+    frames, base_ref, kb_ref, bc_ref, stat_ref, q_ref, less_ref, more_ref, acc_hbm, m_hbm, o_ref,
+    acc_ref, m_ref, near_ref, sems, acc_sems, m_sem
 ):
-    pieces = in_ref.shape[0] // BLOCK
-    rows = in_ref.shape[2]
+    pieces = q_ref.shape[0] // BLOCK
+    rows = q_ref.shape[2]
     base = base_ref[0]
-    run_copies(
-        [
-            pltpu.make_async_copy(less_ref, near_ref.at[pl.ds(0, W * pieces)], sems.at[0]),
-            pltpu.make_async_copy(more_ref, near_ref.at[pl.ds(W * pieces, W * pieces)], sems.at[1]),
-        ]
-    )
+    sums = [
+        pltpu.make_async_copy(acc_hbm.at[mine], acc_ref.at[mine], acc_sems.at[mine])
+        for mine in range(BLOCK)
+    ]
+    frames_in = [
+        pltpu.make_async_copy(less_ref, near_ref.at[pl.ds(0, W * pieces)], sems.at[0]),
+        pltpu.make_async_copy(more_ref, near_ref.at[pl.ds(W * pieces, W * pieces)], sems.at[1]),
+    ]
+    for copy in frames_in + sums:
+        copy.start()
+    for copy in frames_in:
+        copy.wait()
     part = functools.partial(frame_at, near_ref, pieces=pieces)
     k_norm = row_norm([part(0, at) for at in range(2 * W)])
     fast = small_scores(stat_ref[0], k_norm) & (stat_ref[1] > 0.5)
+    for copy in sums:
+        copy.wait()
 
     def query(mine):
-        return frame_at(in_ref, 0, mine, pieces)
+        return frame_at(q_ref, 0, mine, pieces)
 
     def used(mine, at):
         slot = jnp.where(at < W, at - W, at - W + BLOCK)
@@ -263,7 +263,7 @@
             pairs = [
                 (part(0, mine + j), part(1, mine + j), used(mine, mine + j)) for j in range(W)
             ]
-            finish(mine, add_frames(acc_in[mine], query(mine), pairs))
+            finish(mine, add_frames(acc_ref[mine], query(mine), pairs))
             return carry
 
         lax.fori_loop(0, BLOCK, frame, 0)
@@ -271,25 +271,24 @@
     @pl.when(jnp.logical_not(fast))
     def _():
         def frame(mine, carry):
-            acc_ref[...] = acc_in[mine]
-            m_ref[...] = m_in[mine]
+            run_copies([pltpu.make_async_copy(m_hbm.at[mine], m_ref, m_sem)])
 
             def pair(j, inner):
                 @pl.when(used(mine, mine + j))
                 def _():
-                    fold_frame(query(mine), part(0, mine + j), part(1, mine + j), acc_ref, m_ref)
+                    fold_frame(query(mine), part(0, mine + j), part(1, mine + j), acc_ref.at[mine], m_ref)
 
                 return inner
 
             lax.fori_loop(0, W, pair, 0)
-            finish(mine, acc_ref[...])
+            finish(mine, acc_ref[mine])
             return carry
 
         lax.fori_loop(0, BLOCK, frame, 0)
 
 
-def attend_own(base, kb, bc, arrived, frames):
-    dests, _, rows, depth = arrived.shape
+def attend_own(base, kb, bc, q, kv, frames):
+    dests, _, rows, depth = q.shape
     size = dests // BLOCK * rows
     return pl.pallas_call(
         functools.partial(own_kernel, frames),
@@ -298,29 +297,31 @@
             jax.ShapeDtypeStruct((BLOCK, size, LANES), F32),
             jax.ShapeDtypeStruct((2,), F32),
         ],
-        in_specs=[SMEM] * 3 + [VMEM],
+        in_specs=[SMEM] * 3 + [VMEM] * 2,
         out_specs=[VMEM, VMEM, SMEM],
         compiler_params=PARAMS,
         cost_estimate=estimate(10),
-    )(base, kb, bc, arrived)
-
-
-def attend_near(base, kb, bc, stat, arrived, less, more, acc, top, frames):
-    dests, _, rows, depth = arrived.shape
+    )(base, kb, bc, q, kv)
+
+
+def attend_near(base, kb, bc, stat, q, less, more, acc, top, frames):
+    dests, _, rows, depth = q.shape
     size = dests // BLOCK * rows
     return pl.pallas_call(
         functools.partial(near_kernel, frames),
         out_shape=jax.ShapeDtypeStruct((dests, rows, depth), BF),
-        in_specs=[SMEM] * 4 + [VMEM, ANY, ANY, VMEM, VMEM],
+        in_specs=[SMEM] * 4 + [VMEM] + [ANY] * 4,
         out_specs=VMEM,
         scratch_shapes=[
-            pltpu.VMEM((size, 2 * depth), F32),
+            pltpu.VMEM((BLOCK, size, 2 * depth), F32),
             pltpu.VMEM((size, LANES), F32),
             pltpu.VMEM((2 * less.shape[0], *less.shape[1:]), BF),
             pltpu.SemaphoreType.DMA((2,)),
+            pltpu.SemaphoreType.DMA((BLOCK,)),
+            pltpu.SemaphoreType.DMA,
         ],
         compiler_params=PARAMS,
-    )(base, kb, bc, stat, arrived, less, more, acc, top)
+    )(base, kb, bc, stat, q, less, more, acc, top)
 
 
 def assemble_kernel(order_ref, t_ref, s_ref, out_ref):
@@ -362,17 +363,20 @@
 
     block_axes = ("yl", "zl", "x")
     loop_axes = ("grp", "yh", "yl", "zl")
-    st = pack_temporal(head_order, (queries, keys, values), items)
-    qkv = exchange(pack_spatial(head_order, (queries, keys, values)), block_axes)
-    pieces = qkv.shape[0] // BLOCK
-    less = from_block(qkv[(BLOCK - W) * pieces :, 1:], -1)
-    more = from_block(qkv[: W * pieces, 1:], 1)
-    qkv, st = lax.optimization_barrier((qkv, st))
+    st = pack_temporal(head_order, queries, keys, values, items)
+    sq = pack_spatial(head_order, (queries,))
+    kv = exchange(pack_spatial(head_order, (keys, values)), block_axes)
+    pieces = kv.shape[0] // BLOCK
+    less = from_block(kv[(BLOCK - W) * pieces :], -1)
+    more = from_block(kv[: W * pieces], 1)
+    kv, st = lax.optimization_barrier((kv, st))
     at = exchange(st, loop_axes)
-    acc, top, stat = attend_own(base, key_blocks, block_count, qkv, frames)
-    to, stat = lax.optimization_barrier((temporal_attend(at), stat))
+    at, sq = lax.optimization_barrier((at, sq))
+    q = exchange(sq, block_axes)
+    to, q = lax.optimization_barrier((temporal_attend(at), q))
     tr = exchange(to, loop_axes)
-    so = attend_near(base, key_blocks, block_count, stat, qkv, less, more, acc, top, frames)
+    acc, top, stat = attend_own(base, key_blocks, block_count, q, kv, frames)
+    so = attend_near(base, key_blocks, block_count, stat, q, less, more, acc, top, frames)
     sr = exchange(so, block_axes)
     return assemble(head_order, tr, sr, rows, width)
 

time: 188 us -> 164 us (0.87)
  the two profiles are of different devices: /device:TPU:1 before, /device:TPU:2 now
where the time goes in v2:
time: 164 us; the launch traced here: 163 us
  starting transfers between devices  53.8 us (33%)
  waiting for transfers between devices  45.9 us (28%)
  Pallas kernels  44.1 us (27%)
  blocking collectives  14.6 us (9%)
  local copies, waits for them, and re-layouts  4.34 us (3%)
    all_to_all x4, waiting for transfers between devices, exchange(): return lax.all_to_all(array, axes, 0, 0, tiled=True)  45.8 us
    all_to_all x4, starting transfers between devices, exchange(): return lax.all_to_all(array, axes, 0, 0, tiled=True)  43.3 us
    pallas_call x1, Pallas kernels, attend_own(): pl.pallas_call(functools.partial(own_kernel, frames), out_shape=[jax.Shap...  19.1 us
    all_to_all x1, blocking collectives, exchange(): return lax.all_to_all(array, axes, 0, 0, tiled=True)  14.6 us
    pallas_call x1, Pallas kernels, attend_near(): pl.pallas_call(functools.partial(near_kernel, frames), out_shape=jax.Shap...  13.8 us
    ppermute x2, starting transfers between devices, from_block(): lax.ppermute(array, ('grp', 'yh'), [((i + by) % count, i) for i in range(...  10.5 us
    pallas_call x2, Pallas kernels, pack_spatial(): pl.pallas_call(pack_spatial_kernel, out_shape=jax.ShapeDtypeStruct((heads...  5.9 us
  transfers between devices with their start and end apart: 6, of which 3 were waited for; matrix products, arithmetic and copies ran while one was open for 1% of the time, Pallas kernels for 24%

profile of v2, /device:TPU:2, one launch (start us, length us, event | category | flops | bytes accessed | tf_op | source)
XLA Modules:
  0.0 163.0 jit_solution(6168944240852345161)
XLA Ops:
  0.0 0.0 copy-start.6
  0.0 0.0 copy-start.2
  0.0 0.0 copy-start.1
  0.0 0.0 copy-start
  0.0 3.3 %shard_map.64 = bf16[16,2,128,128]{3,2,1,0:T(8,128)(2,1)} custom-call(s32[24]{0:T(128)} %order_ref.7, bf16[128,3072]{1,0:T(8,128)(2,1)} %k_ref.1, bf16[128,3072]{1,0:T(8,128)(2,1)} %v_ref.1), custom_call_target="tpu_custom_call" | custom-call | tf_op jit(solution)/shard_map/pallas_call | solution.py:57
  3.3 9.3 %all-to-all-start = ((bf16[16,2,128,128]{3,2,1,0:T(8,128)(2,1)}), bf16[16,2,128,128]{3,2,1,0:T(8,128)(2,1)S(1)}, u32[]{:S(2)}, u32[]{:S(2)}) async-start(bf16[16,2,128,128]{3,2,1,0:T(8,128)(2,1)} %shard_map.64), calls=%async_computation | async-start | bytes 2097152 | tf_op jit(solution)/shard_map/all_to_all | solution.py:348
  12.6 0.0 copy-done.6
  12.6 0.0 copy-done.2
  12.7 0.0 copy-done.1
  12.7 0.0 copy-done
  12.7 1.6 shard_map.65
  14.3 0.0 copy-start.9
  14.3 12.2 %all-to-all-done.kv_ref = bf16[16,2,128,128]{3,2,1,0:T(8,128)(2,1)S(1)} async-done(((bf16[16,2,128,128]{3,2,1,0:T(8,128)(2,1)}), bf16[16,2,128,128]{3,2,1,0:T(8,128)(2,1)S(1)}, u32[]{:S(2)}, u32[]{:S(2)}) %all-to-all-start) | async-done | bytes 1048608 | tf_op jit(solution)/shard_map/all_to_all | solution.py:348
  26.5 15.9 %all-to-all-start.1 = ((bf16[128,3,8,128]{3,2,1,0:T(8,128)(2,1)}), bf16[128,3,8,128]{3,2,1,0:T(8,128)(2,1)S(1)}, u32[]{:S(2)}, u32[]{:S(2)}) async-start(bf16[128,3,8,128]{3,2,1,0:T(8,128)(2,1)} %shard_map.65), calls=%async_computation.1 | async-start | bytes 1572864 | tf_op jit(solution)/shard_map/all_to_all | solution.py:348
  42.4 2.6 %shard_map.66 = bf16[16,1,128,128]{3,2,1,0:T(8,128)(2,1)} custom-call(s32[24]{0:T(128)} %order_ref.7, bf16[128,3072]{1,0:T(8,128)(2,1)} %refs_0_.3), custom_call_target="tpu_custom_call" | custom-call | tf_op jit(solution)/shard_map/pallas_call | solution.py:57
  45.1 0.0 copy-done.9
  45.1 0.1 copy.8.kb_ref
  45.2 1.5 fusion
  46.7 8.6 %collective-permute-start.1 = (bf16[12,2,128,128]{3,2,1,0:T(8,128)(2,1)}, bf16[12,2,128,128]{3,2,1,0:T(8,128)(2,1)S(1)}, u32[]{:S(2)}, u32[]{:S(2)}) collective-permute-start(bf16[12,2,128,128]{3,2,1,0:T(8,128)(2,1)} %get-tuple-element.23), channel_id=1, source_target_pairs={{16,0},{32,16},{48,32},{64,48},{80,64},{96,80},{112,96},{128,112},... | collective-permute-start | bytes 2359304 | tf_op jit(solution)/shard_map/ppermute | solution.py:353
  55.3 1.9 %collective-permute-start = (bf16[12,2,128,128]{3,2,1,0:T(8,128)(2,1)}, bf16[12,2,128,128]{3,2,1,0:T(8,128)(2,1)S(1)}, u32[]{:S(2)}, u32[]{:S(2)}) collective-permute-start(bf16[12,2,128,128]{3,2,1,0:T(8,128)(2,1)} %get-tuple-element.24), channel_id=1, source_target_pairs={{496,0},{0,16},{16,32},{32,48},{48,64},{64,80},{80,96},{96,112},{1... | collective-permute-start | bytes 2359304 | tf_op jit(solution)/shard_map/ppermute | solution.py:353
  57.2 10.5 %all-to-all-done.1.in_ref = bf16[128,3,8,128]{3,2,1,0:T(8,128)(2,1)S(1)} async-done(((bf16[128,3,8,128]{3,2,1,0:T(8,128)(2,1)}), bf16[128,3,8,128]{3,2,1,0:T(8,128)(2,1)S(1)}, u32[]{:S(2)}, u32[]{:S(2)}) %all-to-all-start.1) | async-done | bytes 786464 | tf_op jit(solution)/shard_map/all_to_all | solution.py:348
  67.8 0.0 copy-start.3
  67.8 0.9 copy-done.3
  68.6 5.0 %all-to-all-start.2 = ((bf16[16,1,128,128]{3,2,1,0:T(8,128)(2,1)}), bf16[16,1,128,128]{3,2,1,0:T(8,128)(2,1)S(1)}, u32[]{:S(2)}, u32[]{:S(2)}) async-start(bf16[16,1,128,128]{3,2,1,0:T(8,128)(2,1)} %shard_map.66), calls=%async_computation.2 | async-start | bytes 1048576 | tf_op jit(solution)/shard_map/all_to_all | solution.py:348
  73.7 0.0 copy-start.4
  73.7 1.1 copy-done.4
  74.8 0.0 copy-start.8
  74.8 2.1 %shard_map.67 = bf16[128,8,128]{2,1,0:T(8,128)(2,1)S(1)} custom-call(bf16[128,3,8,128]{3,2,1,0:T(8,128)(2,1)S(1)} %copy-done.4), custom_call_target="tpu_custom_call" | custom-call | flops 49999998976 | bytes 1048576 | tf_op jit(solution)/shard_map/pallas_call | solution.py:109
  76.9 0.0 copy-start.5
  77.0 0.7 copy-done.5
  77.7 23.1 %all-to-all-done.2.q_ref = bf16[16,1,128,128]{3,2,1,0:T(8,128)(2,1)S(1)} async-done(((bf16[16,1,128,128]{3,2,1,0:T(8,128)(2,1)}), bf16[16,1,128,128]{3,2,1,0:T(8,128)(2,1)S(1)}, u32[]{:S(2)}, u32[]{:S(2)}) %all-to-all-start.2) | async-done | bytes 524320 | tf_op jit(solution)/shard_map/all_to_all | solution.py:348
  100.8 13.0 %all-to-all-start.3 = ((bf16[128,8,128]{2,1,0:T(8,128)(2,1)}), bf16[128,8,128]{2,1,0:T(8,128)(2,1)S(1)}, u32[]{:S(2)}, u32[]{:S(2)}) async-start(bf16[128,8,128]{2,1,0:T(8,128)(2,1)} %copy-done.5), calls=%async_computation.3 | async-start | bytes 524288 | tf_op jit(solution)/shard_map/all_to_all | solution.py:348
  113.8 0.0 copy-done.8
  113.8 19.1 %shard_map.68 = (f32[4,512,256]{2,1,0:T(8,128)S(1)}, f32[4,512,128]{2,1,0:T(8,128)S(1)}, f32[2]{0:T(128)S(1)}) custom-call(s32[1]{0:T(128)} %bitcast.base_ref, s32[128,6]{1,0:T(8,128)S(1)} %copy.8.kb_ref, s32[128]{0:T(128)S(1)} %copy-done.8, bf16[16,1,128,128]{3,2,1,0:T(8,128)(2,1)S(1)} %all-to-all-done.2.q_ref, ...), custom_call_target="tpu_custom_call" | custom-call | flops 10000000000 | bytes 1048576 | tf_op jit(solution)/shard_map/pallas_call | solution.py:293
  132.9 0.0 collective-permute-done.1.more_ref
  132.9 0.0 collective-permute-done.less_ref
  132.9 0.0 copy-start.7
  132.9 13.8 %shard_map.69 = bf16[16,128,128]{2,1,0:T(8,128)(2,1)S(1)} custom-call(s32[1]{0:T(128)} %bitcast.base_ref, s32[128,6]{1,0:T(8,128)S(1)} %copy.8.kb_ref, s32[128]{0:T(128)S(1)} %copy-done.8, f32[2]{0:T(128)S(1)} %get-tuple-element.20.stat_ref, bf16[16,1,128,128]{3,2,1,0:T(8,128)(2,1)S(1)} %all-to-all-done.2.q_ref, ...), custom_call_target="tpu_custom_call" | custom-call | tf_op jit(solution)/shard_map/pallas_call | solution.py:310
  146.7 0.0 all-to-all-done.3.t_ref
  146.8 14.6 %all_to_all.25.s_ref = bf16[16,128,128]{2,1,0:T(8,128)(2,1)S(1)} all-to-all(bf16[16,128,128]{2,1,0:T(8,128)(2,1)S(1)} %shard_map.69), channel_id=1, replica_groups=mesh['grp'=8,'yh'=4,'yl'=2,'zl'=2,'x'=4] {'yl','zl','x'}, dimensions={0} | all-to-all | bytes 1048576 | tf_op jit(solution)/shard_map/all_to_all | solution.py:348
  161.4 0.0 copy-done.7
  161.4 1.6 shard_map.70
Async XLA Ops:
  0.0 12.6 %copy-start.6 = (s32[24]{0:T(128)S(1)}, s32[24]{0:T(128)}, u32[]{:S(2)}) copy-start(s32[24]{0:T(128)} %order_ref.7) | copy-start | bytes 292
  0.0 12.6 %copy-start.2 = (bf16[128,3072]{1,0:T(8,128)(2,1)S(1)}, bf16[128,3072]{1,0:T(8,128)(2,1)}, u32[]{:S(2)}) copy-start(bf16[128,3072]{1,0:T(8,128)(2,1)} %v_ref.1) | copy-start | bytes 2359300
  0.0 12.7 %copy-start.1 = (bf16[128,3072]{1,0:T(8,128)(2,1)S(1)}, bf16[128,3072]{1,0:T(8,128)(2,1)}, u32[]{:S(2)}) copy-start(bf16[128,3072]{1,0:T(8,128)(2,1)} %k_ref.1) | copy-start | bytes 2359300
  0.0 12.7 %copy-start = (bf16[128,3072]{1,0:T(8,128)(2,1)S(1)}, bf16[128,3072]{1,0:T(8,128)(2,1)}, u32[]{:S(2)}) copy-start(bf16[128,3072]{1,0:T(8,128)(2,1)} %refs_0_.3) | copy-start | bytes 2359300
  3.3 23.2 %all-to-all-start = ((bf16[16,2,128,128]{3,2,1,0:T(8,128)(2,1)}), bf16[16,2,128,128]{3,2,1,0:T(8,128)(2,1)S(1)}, u32[]{:S(2)}, u32[]{:S(2)}) async-start(bf16[16,2,128,128]{3,2,1,0:T(8,128)(2,1)} %shard_map.64), calls=%async_computation | async-start | bytes 2097152 | tf_op jit(solution)/shard_map/all_to_all | solution.py:348
  14.3 30.8 %copy-start.9 = (s32[128,6]{0,1:T(8,128)S(1)}, s32[128,6]{0,1:T(8,128)}, u32[]{:S(2)}) copy-start(s32[128,6]{0,1:T(8,128)} %param.10) | copy-start | bytes 9220
  26.5 41.3 %all-to-all-start.1 = ((bf16[128,3,8,128]{3,2,1,0:T(8,128)(2,1)}), bf16[128,3,8,128]{3,2,1,0:T(8,128)(2,1)S(1)}, u32[]{:S(2)}, u32[]{:S(2)}) async-start(bf16[128,3,8,128]{3,2,1,0:T(8,128)(2,1)} %shard_map.65), calls=%async_computation.1 | async-start | bytes 1572864 | tf_op jit(solution)/shard_map/all_to_all | solution.py:348
  46.7 86.2 %collective-permute-start.1 = (bf16[12,2,128,128]{3,2,1,0:T(8,128)(2,1)}, bf16[12,2,128,128]{3,2,1,0:T(8,128)(2,1)S(1)}, u32[]{:S(2)}, u32[]{:S(2)}) collective-permute-start(bf16[12,2,128,128]{3,2,1,0:T(8,128)(2,1)} %get-tuple-element.23), channel_id=1, source_target_pairs={{16,0},{32,16},{48,32},{64,48},{80,64},{96,80},{112,96},{128,112},... | collective-permute-start | bytes 2359304 | tf_op jit(solution)/shard_map/ppermute | solution.py:353
  55.3 77.6 %collective-permute-start = (bf16[12,2,128,128]{3,2,1,0:T(8,128)(2,1)}, bf16[12,2,128,128]{3,2,1,0:T(8,128)(2,1)S(1)}, u32[]{:S(2)}, u32[]{:S(2)}) collective-permute-start(bf16[12,2,128,128]{3,2,1,0:T(8,128)(2,1)} %get-tuple-element.24), channel_id=1, source_target_pairs={{496,0},{0,16},{16,32},{32,48},{48,64},{64,80},{80,96},{96,112},{1... | collective-permute-start | bytes 2359304 | tf_op jit(solution)/shard_map/ppermute | solution.py:353
  67.8 0.9 copy-start.3
  68.6 32.1 %all-to-all-start.2 = ((bf16[16,1,128,128]{3,2,1,0:T(8,128)(2,1)}), bf16[16,1,128,128]{3,2,1,0:T(8,128)(2,1)S(1)}, u32[]{:S(2)}, u32[]{:S(2)}) async-start(bf16[16,1,128,128]{3,2,1,0:T(8,128)(2,1)} %shard_map.66), calls=%async_computation.2 | async-start | bytes 1048576 | tf_op jit(solution)/shard_map/all_to_all | solution.py:348
  73.7 1.1 copy-start.4
  74.8 39.0 %copy-start.8 = (s32[128]{0:T(128)S(1)}, s32[128]{0:T(128)}, u32[]{:S(2)}) copy-start(s32[128]{0:T(128)} %bc_ref.3) | copy-start | bytes 1540
  76.9 0.7 copy-start.5
  100.8 46.0 %all-to-all-start.3 = ((bf16[128,8,128]{2,1,0:T(8,128)(2,1)}), bf16[128,8,128]{2,1,0:T(8,128)(2,1)S(1)}, u32[]{:S(2)}, u32[]{:S(2)}) async-start(bf16[128,8,128]{2,1,0:T(8,128)(2,1)} %copy-done.5), calls=%async_computation.3 | async-start | bytes 524288 | tf_op jit(solution)/shard_map/all_to_all | solution.py:348
  132.9 28.4 %copy-start.7 = (s32[24]{0:T(128)S(1)}, s32[24]{0:T(128)}, u32[]{:S(2)}) copy-start(s32[24]{0:T(128)} %order_ref.7) | copy-start | bytes 292

commit v3 on v2

--- a/solution.py
+++ b/solution.py
@@ -64,56 +64,75 @@
     )(order, *arrays)
 
 
-def pack_temporal_kernel(items, order_ref, q_ref, k_ref, v_ref, out_ref):
+def pack_temporal_kernel(items, core_ref, order_ref, q_ref, k_ref, v_ref, mine_ref, other_ref):
     pieces = q_ref.shape[0] // items
-    for which, src in enumerate((q_ref, k_ref, v_ref)):
-        for head in range(HT):
-            block = src[:, columns_of(order_ref, head)]
-            out_ref[head * pieces : (head + 1) * pieces, which] = block.reshape(pieces, items, DEPTH)
-
-
-def pack_temporal(order, q, k, v, items):
-    dests = HT * q.shape[0] // items
+    for out, core in ((mine_ref, core_ref[0]), (other_ref, 1 - core_ref[0])):
+        for which, src in enumerate((q_ref, k_ref, v_ref)):
+            for pair in range(HT // 2):
+                block = src[:, columns_of(order_ref, 2 * pair + core)]
+                out[pair * pieces : (pair + 1) * pieces, which] = block.reshape(pieces, items, DEPTH)
+
+
+def pack_temporal(order, core, q, k, v, items):
+    out = jax.ShapeDtypeStruct((HT // 2 * q.shape[0] // items, 3, items, DEPTH), BF)
     return pl.pallas_call(
         functools.partial(pack_temporal_kernel, items),
-        out_shape=jax.ShapeDtypeStruct((dests, 3, items, DEPTH), BF),
-        in_specs=[SMEM] + [VMEM] * 3,
+        out_shape=[out, out],
+        in_specs=[SMEM, SMEM] + [VMEM] * 3,
+        out_specs=[VMEM, VMEM],
+        compiler_params=PARAMS,
+    )(core, order, q, k, v)
+
+
+def join_kernel(a_ref, b_ref, out_ref):
+    out_ref[:, 0] = a_ref[...]
+    out_ref[:, 1] = b_ref[...]
+
+
+def join(mine, other):
+    return pl.pallas_call(
+        join_kernel,
+        out_shape=jax.ShapeDtypeStruct((mine.shape[0], 2, *mine.shape[1:]), BF),
+        in_specs=[VMEM] * 2,
         out_specs=VMEM,
         compiler_params=PARAMS,
-    )(order, q, k, v)
-
-
-def temporal_kernel(in_ref, out_ref):
-    frames, _, items, depth = in_ref.shape
-    total = frames * items
-    step = 256
-    factor = depth ** (-0.5) * math.log2(math.e)
-    k = in_ref[:, 1].reshape(total, depth)
-    v = in_ref[:, 2].reshape(total, depth)
+    )(mine, other)
+
+
+def temporal_kernel(core_ref, in_ref, out_ref):
+    places, cores, _, items, depth = in_ref.shape
+    total = places * cores * items
+    per = 16
+    step = per * cores * items
+    inner = out_ref.shape[0] // HT
+    k = in_ref[:, :, 1].reshape(total, depth)
+    v = in_ref[:, :, 2].reshape(total, depth)
     row_item = lax.broadcasted_iota(jnp.int32, (step, total), 0) % items
     col_item = lax.broadcasted_iota(jnp.int32, (step, total), 1) % items
     same = row_item == col_item
-    per = step // items
-    for at in range(frames // per):
-        q = in_ref[at * per : (at + 1) * per, 0].reshape(step, depth)
-        s = lax.dot_general(q, k, (((1,), (1,)), ((), ())), preferred_element_type=F32)
-        s = jnp.where(same, s * factor, -jnp.inf)
+    for at in range(places // per):
+        q = in_ref[at * per : (at + 1) * per, :, 0].reshape(step, depth)
+        s = jnp.where(same, products(q, k) * score_factor(), -jnp.inf)
         p = jnp.exp2(s - jnp.max(s, axis=1, keepdims=True))
         total_p = jnp.sum(p, axis=1, keepdims=True)
         o = jnp.dot(p.astype(BF), v, preferred_element_type=F32) / total_p
-        out_ref[at * per : (at + 1) * per] = o.astype(BF).reshape(per, items, depth)
-
-
-def temporal_attend(arrived):
-    frames, _, items, depth = arrived.shape
+        o = o.astype(BF).reshape(per, cores, items, depth)
+        high, low = divmod(at * per, inner)
+        for which, core in enumerate((core_ref[0], 1 - core_ref[0])):
+            first = (high * cores + core) * inner + low
+            out_ref[pl.ds(first, per)] = o[:, which]
+
+
+def temporal_attend(core, arrived):
+    places, cores, _, items, depth = arrived.shape
     return pl.pallas_call(
         temporal_kernel,
-        out_shape=jax.ShapeDtypeStruct((frames, items, depth), BF),
-        in_specs=[VMEM],
+        out_shape=jax.ShapeDtypeStruct((places * cores, items, depth), BF),
+        in_specs=[SMEM, VMEM],
         out_specs=VMEM,
         compiler_params=PARAMS,
         cost_estimate=estimate(50),
-    )(arrived)
+    )(core, arrived)
 
 
 def row_norm(blocks):
@@ -175,14 +194,11 @@
     return block.reshape(pieces * block.shape[1], DEPTH)
 
 
-def own_kernel(frames, base_ref, kb_ref, bc_ref, q_ref, kv_ref, acc_ref, m_ref, stat_ref):
-    pieces = q_ref.shape[0] // BLOCK
-    size = pieces * q_ref.shape[2]
+def own_kernel(frames, base_ref, kb_ref, bc_ref, in_ref, acc_ref, m_ref, stat_ref):
+    pieces = in_ref.shape[0] // BLOCK
+    size = pieces * in_ref.shape[2]
     base = base_ref[0]
-
-    def part(which, at):
-        return frame_at(kv_ref, which - 1, at, pieces) if which else frame_at(q_ref, 0, at, pieces)
-
+    part = functools.partial(frame_at, in_ref, pieces=pieces)
     q_norm = row_norm([part(0, at) for at in range(BLOCK)])
     k_norm = row_norm([part(1, at) for at in range(BLOCK)])
     fast = small_scores(q_norm, k_norm)
@@ -287,8 +303,8 @@
         lax.fori_loop(0, BLOCK, frame, 0)
 
 
-def attend_own(base, kb, bc, q, kv, frames):
-    dests, _, rows, depth = q.shape
+def attend_own(base, kb, bc, arrived, frames):
+    dests, _, rows, depth = arrived.shape
     size = dests // BLOCK * rows
     return pl.pallas_call(
         functools.partial(own_kernel, frames),
@@ -297,11 +313,11 @@
             jax.ShapeDtypeStruct((BLOCK, size, LANES), F32),
             jax.ShapeDtypeStruct((2,), F32),
         ],
-        in_specs=[SMEM] * 3 + [VMEM] * 2,
+        in_specs=[SMEM] * 3 + [VMEM],
         out_specs=[VMEM, VMEM, SMEM],
         compiler_params=PARAMS,
         cost_estimate=estimate(10),
-    )(base, kb, bc, q, kv)
+    )(base, kb, bc, arrived)
 
 
 def attend_near(base, kb, bc, stat, q, less, more, acc, top, frames):
@@ -349,42 +365,42 @@
 
 
 def from_block(array, by):
-    count = lax.axis_size("grp") * lax.axis_size("yh")
-    return lax.ppermute(array, ("grp", "yh"), [((i + by) % count, i) for i in range(count)])
+    count = lax.axis_size("zh") * lax.axis_size("core") * lax.axis_size("yh")
+    return lax.ppermute(array, ("zh", "core", "yh"), [((i + by) % count, i) for i in range(count)])
 
 
 def local(queries, keys, values, head_order, key_blocks, block_count):
     rows, width = queries.shape
-    blocks = lax.axis_size("grp") * lax.axis_size("yh")
+    blocks = lax.axis_size("zh") * lax.axis_size("core") * lax.axis_size("yh")
     frames = blocks * BLOCK
     items = HT * rows // frames
-    base = (lax.axis_index("grp") * lax.axis_size("yh") + lax.axis_index("yh")) * BLOCK
+    base = lax.axis_index(("zh", "core", "yh")) * BLOCK
     base = base.astype(jnp.int32).reshape(1)
 
     block_axes = ("yl", "zl", "x")
-    loop_axes = ("grp", "yh", "yl", "zl")
-    st = pack_temporal(head_order, queries, keys, values, items)
-    sq = pack_spatial(head_order, (queries,))
-    kv = exchange(pack_spatial(head_order, (keys, values)), block_axes)
-    pieces = kv.shape[0] // BLOCK
-    less = from_block(kv[(BLOCK - W) * pieces :], -1)
-    more = from_block(kv[: W * pieces], 1)
-    kv, st = lax.optimization_barrier((kv, st))
-    at = exchange(st, loop_axes)
-    at, sq = lax.optimization_barrier((at, sq))
-    q = exchange(sq, block_axes)
-    to, q = lax.optimization_barrier((temporal_attend(at), q))
+    loop_axes = ("zh", "core", "yh", "yl", "zl")
+    core = lax.axis_index("core").astype(jnp.int32).reshape(1)
+    mine, other = pack_temporal(head_order, core, queries, keys, values, items)
+    st = join(mine, lax.ppermute(other, "core", [(0, 1), (1, 0)]))
+    qkv = exchange(pack_spatial(head_order, (queries, keys, values)), block_axes)
+    pieces = qkv.shape[0] // BLOCK
+    less = from_block(qkv[(BLOCK - W) * pieces :, 1:], -1)
+    more = from_block(qkv[: W * pieces, 1:], 1)
+    qkv, st = lax.optimization_barrier((qkv, st))
+    at = exchange(st, ("zh", "yh", "yl", "zl"))
+    acc, top, stat = attend_own(base, key_blocks, block_count, qkv, frames)
+    to, stat = lax.optimization_barrier((temporal_attend(core, at), stat))
     tr = exchange(to, loop_axes)
-    acc, top, stat = attend_own(base, key_blocks, block_count, q, kv, frames)
-    so = attend_near(base, key_blocks, block_count, stat, q, less, more, acc, top, frames)
+    so = attend_near(base, key_blocks, block_count, stat, qkv, less, more, acc, top, frames)
     sr = exchange(so, block_axes)
     return assemble(head_order, tr, sr, rows, width)
 
 
 def solution(mesh):
     grp, seq = mesh.shape["grp"], mesh.shape["seq"]
-    fine = Mesh(mesh.devices.reshape(grp, seq // 16, 2, 2, 4), ("grp", "yh", "yl", "zl", "x"))
-    tokens = P(("grp", "yh", "yl", "zl", "x"), None)
+    names = ("zh", "core", "yh", "yl", "zl", "x")
+    fine = Mesh(mesh.devices.reshape(grp // 2, 2, seq // 16, 2, 2, 4), names)
+    tokens = P(names, None)
     return jax.shard_map(
         local,
         mesh=fine,

time: 164 us -> 136 us (0.83)
  the two profiles are of different devices: /device:TPU:2 before, /device:TPU:16 now
where the time goes in v3:
time: 136 us
  starting transfers between devices  46.2 us (34%)
  Pallas kernels  38.3 us (28%)
  waiting for transfers between devices  29.6 us (22%)
  blocking collectives  14.9 us (11%)
  local copies, waits for them, and re-layouts  6.39 us (5%)
    all_to_all x3, starting transfers between devices, exchange(): return lax.all_to_all(array, axes, 0, 0, tiled=True)  36.3 us
    all_to_all x3, waiting for transfers between devices, exchange(): return lax.all_to_all(array, axes, 0, 0, tiled=True)  15.9 us
    pallas_call x1, Pallas kernels, attend_own(): pl.pallas_call(functools.partial(own_kernel, frames), out_shape=[jax.Shap...  15.5 us
    all_to_all x1, blocking collectives, exchange(): return lax.all_to_all(array, axes, 0, 0, tiled=True)  14.9 us
    pallas_call x1, Pallas kernels, attend_near(): pl.pallas_call(functools.partial(near_kernel, frames), out_shape=jax.Shap...  13.7 us
    ppermute x2, waiting for transfers between devices, from_block(): lax.ppermute(array, ('zh', 'core', 'yh'), [((i + by) % count, i) for i in...  12 us
    ppermute x2, starting transfers between devices, from_block(): lax.ppermute(array, ('zh', 'core', 'yh'), [((i + by) % count, i) for i in...  7.94 us
    unnamed x19, local copies, waits for them, and re-layouts  4.89 us
  transfers between devices with their start and end apart: 6, of which 3 were waited for; matrix products, arithmetic and copies ran while one was open for 1% of the time, Pallas kernels for 24%

profile of v3, /device:TPU:16, one launch (start us, length us, event | category | flops | bytes accessed | tf_op | source)
XLA Modules:
  0.0 135.6 jit_solution(17914975304410779278)
XLA Ops:
  0.0 3.6 %shard_map.64 = bf16[16,3,128,128]{3,2,1,0:T(8,128)(2,1)} custom-call(s32[24]{0:T(128)} %order_ref.5, bf16[128,3072]{1,0:T(8,128)(2,1)} %q_ref.1, bf16[128,3072]{1,0:T(8,128)(2,1)} %k_ref.1, bf16[128,3072]{1,0:T(8,128)(2,1)} %v_ref.1), custom_call_target="tpu_custom_call" | custom-call | tf_op jit(solution)/shard_map/pallas_call | solution.py:57
  3.6 0.0 copy-start
  3.7 0.0 copy-start.1
  3.7 0.0 copy-start.6
  3.7 7.4 %all-to-all-start = ((bf16[16,3,128,128]{3,2,1,0:T(8,128)(2,1)}), bf16[16,3,128,128]{3,2,1,0:T(8,128)(2,1)S(1)}, u32[]{:S(2)}, u32[]{:S(2)}) async-start(bf16[16,3,128,128]{3,2,1,0:T(8,128)(2,1)} %shard_map.64), calls=%async_computation | async-start | bytes 3145728 | tf_op jit(solution)/shard_map/all_to_all | solution.py:364
  11.1 0.0 copy-done
  11.1 0.0 copy-done.1
  11.1 0.0 copy-done.6
  11.1 0.0 copy-start.2
  11.1 1.1 copy-done.2
  12.2 0.7 shard_map.65
  13.0 1.9 %collective-permute-start = (bf16[64,3,8,128]{3,2,1,0:T(8,128)(2,1)S(1)}, bf16[64,3,8,128]{3,2,1,0:T(8,128)(2,1)S(1)}, u32[]{:S(2)}, u32[]{:S(2)}) collective-permute-start(bf16[64,3,8,128]{3,2,1,0:T(8,128)(2,1)S(1)} %get-tuple-element.15), channel_id=1, source_target_pairs={{0,64},{64,0},{1,65},{65,1},{2,66},{66,2},{3,67},{67,3},{4,68},{68... | collective-permute-start | bytes 1179656 | tf_op jit(solution)/shard_map/ppermute | solution.py:384
  14.9 1.7 %collective-permute-done.b_ref = bf16[64,3,8,128]{3,2,1,0:T(8,128)(2,1)S(1)} collective-permute-done((bf16[64,3,8,128]{3,2,1,0:T(8,128)(2,1)S(1)}, bf16[64,3,8,128]{3,2,1,0:T(8,128)(2,1)S(1)}, u32[]{:S(2)}, u32[]{:S(2)}) %collective-permute-start) | collective-permute-done | bytes 393248 | tf_op jit(solution)/shard_map/ppermute | solution.py:384
  16.6 0.0 copy-start.8
  16.6 0.9 shard_map.66
  17.5 15.9 %all-to-all-done.in_ref.q_ref = bf16[16,3,128,128]{3,2,1,0:T(8,128)(2,1)S(1)} async-done(((bf16[16,3,128,128]{3,2,1,0:T(8,128)(2,1)}), bf16[16,3,128,128]{3,2,1,0:T(8,128)(2,1)S(1)}, u32[]{:S(2)}, u32[]{:S(2)}) %all-to-all-start) | async-done | bytes 1572896 | tf_op jit(solution)/shard_map/all_to_all | solution.py:364
  33.5 14.7 %all-to-all-start.1 = ((bf16[64,2,3,8,128]{4,3,2,1,0:T(8,128)(2,1)}), bf16[64,2,3,8,128]{4,3,2,1,0:T(8,128)(2,1)S(1)}, u32[]{:S(2)}, u32[]{:S(2)}) async-start(bf16[64,2,3,8,128]{4,3,2,1,0:T(8,128)(2,1)} %shard_map.66), calls=%async_computation.1 | async-start | bytes 1572864 | tf_op jit(solution)/shard_map/all_to_all | solution.py:364
  48.1 0.0 copy-done.8
  48.2 0.1 copy.7.kb_ref
  48.3 0.0 copy-start.7
  48.3 1.5 %fusion = (bf16[12,2,128,128]{3,2,1,0:T(8,128)(2,1)}, bf16[12,2,128,128]{3,2,1,0:T(8,128)(2,1)}) fusion(bf16[16,3,128,128]{3,2,1,0:T(8,128)(2,1)S(1)} %all-to-all-done.in_ref.q_ref), kind=kLoop, calls=%fused_computation | loop fusion | bytes 3145728 | tf_op jit(solution)/shard_map/slice | solution.py:388
  49.8 2.4 %collective-permute-start.2 = (bf16[12,2,128,128]{3,2,1,0:T(8,128)(2,1)}, bf16[12,2,128,128]{3,2,1,0:T(8,128)(2,1)}, u32[]{:S(2)}, u32[]{:S(2)}) collective-permute-start(bf16[12,2,128,128]{3,2,1,0:T(8,128)(2,1)} %get-tuple-element.23), channel_id=1, source_target_pairs={{16,0},{32,16},{48,32},{64,48},{80,64},{96,80},{112,96},{128,112},... | collective-permute-start | bytes 2359304 | tf_op jit(solution)/shard_map/ppermute | solution.py:369
  52.1 5.6 %collective-permute-start.1 = (bf16[12,2,128,128]{3,2,1,0:T(8,128)(2,1)}, bf16[12,2,128,128]{3,2,1,0:T(8,128)(2,1)}, u32[]{:S(2)}, u32[]{:S(2)}) collective-permute-start(bf16[12,2,128,128]{3,2,1,0:T(8,128)(2,1)} %get-tuple-element.24), channel_id=1, source_target_pairs={{496,0},{0,16},{16,32},{32,48},{48,64},{64,80},{80,96},{96,112},{1... | collective-permute-start | bytes 2359304 | tf_op jit(solution)/shard_map/ppermute | solution.py:369
  57.7 0.0 copy-done.7
  57.8 15.5 %shard_map.68 = (f32[4,512,256]{2,1,0:T(8,128)S(1)}, f32[4,512,128]{2,1,0:T(8,128)S(1)}, f32[2]{0:T(128)S(1)}) custom-call(s32[1]{0:T(128)} %bitcast.1.base_ref, s32[128,6]{1,0:T(8,128)S(1)} %copy.7.kb_ref, s32[128]{0:T(128)S(1)} %copy-done.7, bf16[16,3,128,128]{3,2,1,0:T(8,128)(2,1)S(1)} %all-to-all-done.in_ref.q_ref), custom_call_target="tpu_custom_call" | custom-call | flops 10000000000 | bytes 1048576 | tf_op jit(solution)/shard_map/pallas_call | solution.py:309
  73.3 0.0 copy-start.3
  73.3 1.3 copy-done.3
  74.6 0.0 all-to-all-done.1.in_ref
  74.6 2.2 %shard_map.67 = bf16[128,8,128]{2,1,0:T(8,128)(2,1)S(1)} custom-call(s32[1]{0:T(128)} %bitcast.core_ref, bf16[64,2,3,8,128]{4,3,2,1,0:T(8,128)(2,1)S(1)} %all-to-all-done.1.in_ref), custom_call_target="tpu_custom_call" | custom-call | flops 49999998976 | bytes 1048576 | tf_op jit(solution)/shard_map/pallas_call | solution.py:128
  76.8 0.0 copy-start.5
  76.8 0.7 copy-done.5
  77.5 14.3 %all-to-all-start.2 = ((bf16[128,8,128]{2,1,0:T(8,128)(2,1)}), bf16[128,8,128]{2,1,0:T(8,128)(2,1)S(1)}, u32[]{:S(2)}, u32[]{:S(2)}) async-start(bf16[128,8,128]{2,1,0:T(8,128)(2,1)} %copy-done.5), calls=%async_computation.2 | async-start | bytes 524288 | tf_op jit(solution)/shard_map/all_to_all | solution.py:364
  91.8 12.0 %collective-permute-done.2.more_ref = bf16[12,2,128,128]{3,2,1,0:T(8,128)(2,1)} collective-permute-done((bf16[12,2,128,128]{3,2,1,0:T(8,128)(2,1)}, bf16[12,2,128,128]{3,2,1,0:T(8,128)(2,1)}, u32[]{:S(2)}, u32[]{:S(2)}) %collective-permute-start.2) | collective-permute-done | bytes 786464 | tf_op jit(solution)/shard_map/ppermute | solution.py:369
  103.8 0.0 collective-permute-done.1.less_ref
  103.8 0.0 copy-start.4
  103.8 1.6 %copy-done.4 = f32[4,512,256]{2,1,0:T(8,128)S(1)} copy-done((f32[4,512,256]{2,1,0:T(8,128)S(1)}, f32[4,512,256]{2,1,0:T(8,128)}, u32[]{:S(2)}) %copy-start.4) | copy-done | bytes 2097176
  105.4 13.7 %shard_map.69 = bf16[16,128,128]{2,1,0:T(8,128)(2,1)S(1)} custom-call(s32[1]{0:T(128)} %bitcast.1.base_ref, s32[128,6]{1,0:T(8,128)S(1)} %copy.7.kb_ref, s32[128]{0:T(128)S(1)} %copy-done.7, f32[2]{0:T(128)S(1)} %get-tuple-element.20.stat_ref, bf16[16,3,128,128]{3,2,1,0:T(8,128)(2,1)S(1)} %all-to-all-done.in_ref.q_ref, ...), custom_call_target="tpu_custom_call" | custom-call | tf_op jit(solution)/shard_map/pallas_call | solution.py:326
  119.1 0.0 all-to-all-done.2.t_ref
  119.1 14.9 %all_to_all.20.s_ref = bf16[16,128,128]{2,1,0:T(8,128)(2,1)S(1)} all-to-all(bf16[16,128,128]{2,1,0:T(8,128)(2,1)S(1)} %shard_map.69), channel_id=1, replica_groups=mesh['zh'=4,'core'=2,'yh'=4,'yl'=2,'zl'=2,'x'=4] {'yl','zl','x'}, dimensions={0} | all-to-all | bytes 1048576 | tf_op jit(solution)/shard_map/all_to_all | solution.py:364
  134.0 1.6 %shard_map.70 = bf16[128,3072]{1,0:T(8,128)(2,1)} custom-call(s32[24]{0:T(128)S(1)} %copy-done.6, bf16[128,8,128]{2,1,0:T(8,128)(2,1)S(1)} %all-to-all-done.2.t_ref, bf16[16,128,128]{2,1,0:T(8,128)(2,1)S(1)} %all_to_all.20.s_ref), custom_call_target="tpu_custom_call" | custom-call | tf_op jit(solution)/shard_map/pallas_call | solution.py:354
Async XLA Ops:
  3.6 7.4 %copy-start = (bf16[128,3072]{1,0:T(8,128)(2,1)S(1)}, bf16[128,3072]{1,0:T(8,128)(2,1)}, u32[]{:S(2)}) copy-start(bf16[128,3072]{1,0:T(8,128)(2,1)} %q_ref.1) | copy-start | bytes 2359300
  3.7 7.4 %copy-start.1 = (bf16[128,3072]{1,0:T(8,128)(2,1)S(1)}, bf16[128,3072]{1,0:T(8,128)(2,1)}, u32[]{:S(2)}) copy-start(bf16[128,3072]{1,0:T(8,128)(2,1)} %k_ref.1) | copy-start | bytes 2359300
  3.7 7.4 %copy-start.6 = (s32[24]{0:T(128)S(1)}, s32[24]{0:T(128)}, u32[]{:S(2)}) copy-start(s32[24]{0:T(128)} %order_ref.5) | copy-start | bytes 292
  3.7 29.8 %all-to-all-start = ((bf16[16,3,128,128]{3,2,1,0:T(8,128)(2,1)}), bf16[16,3,128,128]{3,2,1,0:T(8,128)(2,1)S(1)}, u32[]{:S(2)}, u32[]{:S(2)}) async-start(bf16[16,3,128,128]{3,2,1,0:T(8,128)(2,1)} %shard_map.64), calls=%async_computation | async-start | bytes 3145728 | tf_op jit(solution)/shard_map/all_to_all | solution.py:364
  11.1 1.1 copy-start.2
  13.0 3.6 %collective-permute-start = (bf16[64,3,8,128]{3,2,1,0:T(8,128)(2,1)S(1)}, bf16[64,3,8,128]{3,2,1,0:T(8,128)(2,1)S(1)}, u32[]{:S(2)}, u32[]{:S(2)}) collective-permute-start(bf16[64,3,8,128]{3,2,1,0:T(8,128)(2,1)S(1)} %get-tuple-element.15), channel_id=1, source_target_pairs={{0,64},{64,0},{1,65},{65,1},{2,66},{66,2},{3,67},{67,3},{4,68},{68... | collective-permute-start | bytes 1179656 | tf_op jit(solution)/shard_map/ppermute | solution.py:384
  16.6 31.6 %copy-start.8 = (s32[128,6]{0,1:T(8,128)S(1)}, s32[128,6]{0,1:T(8,128)}, u32[]{:S(2)}) copy-start(s32[128,6]{0,1:T(8,128)} %param.10) | copy-start | bytes 9220
  33.5 41.2 %all-to-all-start.1 = ((bf16[64,2,3,8,128]{4,3,2,1,0:T(8,128)(2,1)}), bf16[64,2,3,8,128]{4,3,2,1,0:T(8,128)(2,1)S(1)}, u32[]{:S(2)}, u32[]{:S(2)}) async-start(bf16[64,2,3,8,128]{4,3,2,1,0:T(8,128)(2,1)} %shard_map.66), calls=%async_computation.1 | async-start | bytes 1572864 | tf_op jit(solution)/shard_map/all_to_all | solution.py:364
  48.3 9.5 %copy-start.7 = (s32[128]{0:T(128)S(1)}, s32[128]{0:T(128)}, u32[]{:S(2)}) copy-start(s32[128]{0:T(128)} %bc_ref.3) | copy-start | bytes 1540
  49.8 54.0 %collective-permute-start.2 = (bf16[12,2,128,128]{3,2,1,0:T(8,128)(2,1)}, bf16[12,2,128,128]{3,2,1,0:T(8,128)(2,1)}, u32[]{:S(2)}, u32[]{:S(2)}) collective-permute-start(bf16[12,2,128,128]{3,2,1,0:T(8,128)(2,1)} %get-tuple-element.23), channel_id=1, source_target_pairs={{16,0},{32,16},{48,32},{64,48},{80,64},{96,80},{112,96},{128,112},... | collective-permute-start | bytes 2359304 | tf_op jit(solution)/shard_map/ppermute | solution.py:369
  52.1 51.6 %collective-permute-start.1 = (bf16[12,2,128,128]{3,2,1,0:T(8,128)(2,1)}, bf16[12,2,128,128]{3,2,1,0:T(8,128)(2,1)}, u32[]{:S(2)}, u32[]{:S(2)}) collective-permute-start(bf16[12,2,128,128]{3,2,1,0:T(8,128)(2,1)} %get-tuple-element.24), channel_id=1, source_target_pairs={{496,0},{0,16},{16,32},{32,48},{48,64},{64,80},{80,96},{96,112},{1... | collective-permute-start | bytes 2359304 | tf_op jit(solution)/shard_map/ppermute | solution.py:369
  73.3 1.3 copy-start.3
  76.8 0.7 copy-start.5
  77.5 41.6 %all-to-all-start.2 = ((bf16[128,8,128]{2,1,0:T(8,128)(2,1)}), bf16[128,8,128]{2,1,0:T(8,128)(2,1)S(1)}, u32[]{:S(2)}, u32[]{:S(2)}) async-start(bf16[128,8,128]{2,1,0:T(8,128)(2,1)} %copy-done.5), calls=%async_computation.2 | async-start | bytes 524288 | tf_op jit(solution)/shard_map/all_to_all | solution.py:364
  103.8 1.6 %copy-start.4 = (f32[4,512,256]{2,1,0:T(8,128)S(1)}, f32[4,512,256]{2,1,0:T(8,128)}, u32[]{:S(2)}) copy-start(f32[4,512,256]{2,1,0:T(8,128)} %copy-done.3) | copy-start | bytes 6291460

commit v4 on v3

--- a/solution.py
+++ b/solution.py
@@ -84,6 +84,23 @@
     )(core, order, q, k, v)
 
 
+def part_kernel(low_ref, a_ref, b_ref, mine_ref, other_ref):
+    for out, low in ((mine_ref, low_ref[0]), (other_ref, 1 - low_ref[0])):
+        for which, src in enumerate((a_ref, b_ref)):
+            out[:, pl.ds(which, 1)] = src[:, pl.ds(low, 1)]
+
+
+def part(low, a, b):
+    out = jax.ShapeDtypeStruct(a.shape, BF)
+    return pl.pallas_call(
+        part_kernel,
+        out_shape=[out, out],
+        in_specs=[SMEM, VMEM, VMEM],
+        out_specs=[VMEM, VMEM],
+        compiler_params=PARAMS,
+    )(low, a, b)
+
+
 def join_kernel(a_ref, b_ref, out_ref):
     out_ref[:, 0] = a_ref[...]
     out_ref[:, 1] = b_ref[...]
@@ -99,40 +116,40 @@
     )(mine, other)
 
 
-def temporal_kernel(core_ref, in_ref, out_ref):
-    places, cores, _, items, depth = in_ref.shape
-    total = places * cores * items
-    per = 16
-    step = per * cores * items
-    inner = out_ref.shape[0] // HT
-    k = in_ref[:, :, 1].reshape(total, depth)
-    v = in_ref[:, :, 2].reshape(total, depth)
+def temporal_kernel(core_ref, low_ref, in_ref, out_ref):
+    places, lows, cores, _, items, depth = in_ref.shape
+    total = places * lows * cores * items
+    per = out_ref.shape[1]
+    step = per * lows * cores * items
+    k = in_ref[:, :, :, 1].reshape(total, depth)
+    v = in_ref[:, :, :, 2].reshape(total, depth)
     row_item = lax.broadcasted_iota(jnp.int32, (step, total), 0) % items
     col_item = lax.broadcasted_iota(jnp.int32, (step, total), 1) % items
     same = row_item == col_item
-    for at in range(places // per):
-        q = in_ref[at * per : (at + 1) * per, :, 0].reshape(step, depth)
+    for high in range(places // per):
+        q = in_ref[high * per : (high + 1) * per, :, :, 0].reshape(step, depth)
         s = jnp.where(same, products(q, k) * score_factor(), -jnp.inf)
         p = jnp.exp2(s - jnp.max(s, axis=1, keepdims=True))
         total_p = jnp.sum(p, axis=1, keepdims=True)
         o = jnp.dot(p.astype(BF), v, preferred_element_type=F32) / total_p
-        o = o.astype(BF).reshape(per, cores, items, depth)
-        high, low = divmod(at * per, inner)
-        for which, core in enumerate((core_ref[0], 1 - core_ref[0])):
-            first = (high * cores + core) * inner + low
-            out_ref[pl.ds(first, per)] = o[:, which]
-
-
-def temporal_attend(core, arrived):
-    places, cores, _, items, depth = arrived.shape
-    return pl.pallas_call(
+        o = o.astype(BF).reshape(per, lows, cores, items, depth)
+        for i, low in enumerate((low_ref[0], 1 - low_ref[0])):
+            for j, core in enumerate((core_ref[0], 1 - core_ref[0])):
+                out_ref[pl.ds(high * cores + core, 1), :, pl.ds(low, 1)] = o[:, i, j][None, :, None]
+
+
+def temporal_attend(core, low, arrived, ys):
+    places, lows, cores, _, items, depth = arrived.shape
+    frames = places * lows * cores
+    out = pl.pallas_call(
         temporal_kernel,
-        out_shape=jax.ShapeDtypeStruct((places * cores, items, depth), BF),
-        in_specs=[SMEM, VMEM],
+        out_shape=jax.ShapeDtypeStruct((frames // (ys * lows), ys, lows, items, depth), BF),
+        in_specs=[SMEM, SMEM, VMEM],
         out_specs=VMEM,
         compiler_params=PARAMS,
         cost_estimate=estimate(50),
-    )(core, arrived)
+    )(core, low, arrived)
+    return out.reshape(frames, items, depth)
 
 
 def row_norm(blocks):
@@ -238,11 +255,11 @@
 
 
 def near_kernel(
-    frames, base_ref, kb_ref, bc_ref, stat_ref, q_ref, less_ref, more_ref, acc_hbm, m_hbm, o_ref,
-    acc_ref, m_ref, near_ref, sems, acc_sems, m_sem
+    frames, base_ref, kb_ref, bc_ref, stat_ref, in_ref, less_ref, more_ref, acc_hbm, m_hbm, o_ref,
+    acc_ref, m_ref, near_ref, q_ref, sems, acc_sems, m_sem
 ):
-    pieces = q_ref.shape[0] // BLOCK
-    rows = q_ref.shape[2]
+    pieces = in_ref.shape[0] // BLOCK
+    rows = in_ref.shape[2]
     base = base_ref[0]
     sums = [
         pltpu.make_async_copy(acc_hbm.at[mine], acc_ref.at[mine], acc_sems.at[mine])
@@ -251,6 +268,7 @@
     frames_in = [
         pltpu.make_async_copy(less_ref, near_ref.at[pl.ds(0, W * pieces)], sems.at[0]),
         pltpu.make_async_copy(more_ref, near_ref.at[pl.ds(W * pieces, W * pieces)], sems.at[1]),
+        pltpu.make_async_copy(in_ref.at[:, pl.ds(0, 1)], q_ref, sems.at[2]),
     ]
     for copy in frames_in + sums:
         copy.start()
@@ -326,13 +344,14 @@
     return pl.pallas_call(
         functools.partial(near_kernel, frames),
         out_shape=jax.ShapeDtypeStruct((dests, rows, depth), BF),
-        in_specs=[SMEM] * 4 + [VMEM] + [ANY] * 4,
+        in_specs=[SMEM] * 4 + [ANY] * 5,
         out_specs=VMEM,
         scratch_shapes=[
             pltpu.VMEM((BLOCK, size, 2 * depth), F32),
             pltpu.VMEM((size, LANES), F32),
             pltpu.VMEM((2 * less.shape[0], *less.shape[1:]), BF),
-            pltpu.SemaphoreType.DMA((2,)),
+            pltpu.VMEM((dests, 1, rows, depth), BF),
+            pltpu.SemaphoreType.DMA((3,)),
             pltpu.SemaphoreType.DMA((BLOCK,)),
             pltpu.SemaphoreType.DMA,
         ],
@@ -380,16 +399,21 @@
     block_axes = ("yl", "zl", "x")
     loop_axes = ("zh", "core", "yh", "yl", "zl")
     core = lax.axis_index("core").astype(jnp.int32).reshape(1)
+    low = lax.axis_index("zl").astype(jnp.int32).reshape(1)
+    ys = lax.axis_size("yh") * lax.axis_size("yl")
     mine, other = pack_temporal(head_order, core, queries, keys, values, items)
-    st = join(mine, lax.ppermute(other, "core", [(0, 1), (1, 0)]))
+    other = lax.ppermute(other, "core", [(0, 1), (1, 0)])
+    by_low = (mine.shape[0] // 2, 2, *mine.shape[1:])
+    mine, other = part(low, mine.reshape(by_low), other.reshape(by_low))
+    st = join(mine, lax.ppermute(other, "zl", [(0, 1), (1, 0)]))
     qkv = exchange(pack_spatial(head_order, (queries, keys, values)), block_axes)
     pieces = qkv.shape[0] // BLOCK
     less = from_block(qkv[(BLOCK - W) * pieces :, 1:], -1)
     more = from_block(qkv[: W * pieces, 1:], 1)
     qkv, st = lax.optimization_barrier((qkv, st))
-    at = exchange(st, ("zh", "yh", "yl", "zl"))
+    at = exchange(st, ("zh", "yh", "yl"))
     acc, top, stat = attend_own(base, key_blocks, block_count, qkv, frames)
-    to, stat = lax.optimization_barrier((temporal_attend(core, at), stat))
+    to, stat = lax.optimization_barrier((temporal_attend(core, low, at, ys), stat))
     tr = exchange(to, loop_axes)
     so = attend_near(base, key_blocks, block_count, stat, qkv, less, more, acc, top, frames)
     sr = exchange(so, block_axes)

time: 136 us -> 142 us (1.044)
  the two profiles are of different devices: /device:TPU:16 before, /device:TPU:272 now
where the time goes in v4:
time: 142 us
  starting transfers between devices  47.9 us (34%)
  Pallas kernels  42.8 us (30%)
  waiting for transfers between devices  30.9 us (22%)
  blocking collectives  13.3 us (9%)
  local copies, waits for them, and re-layouts  6.37 us (4%)
    all_to_all x3, starting transfers between devices, exchange(): return lax.all_to_all(array, axes, 0, 0, tiled=True)  34.3 us
    ppermute x1, waiting for transfers between devices, local(): st = join(mine, lax.ppermute(other, 'zl', [(0, 1), (1, 0)]))  17.8 us
    pallas_call x1, Pallas kernels, attend_near(): pl.pallas_call(functools.partial(near_kernel, frames), out_shape=jax.Shap...  17.3 us
    pallas_call x1, Pallas kernels, attend_own(): pl.pallas_call(functools.partial(own_kernel, frames), out_shape=[jax.Shap...  15.5 us
    all_to_all x1, blocking collectives, exchange(): return lax.all_to_all(array, axes, 0, 0, tiled=True)  13.3 us
    ppermute x2, waiting for transfers between devices, from_block(): lax.ppermute(array, ('zh', 'core', 'yh'), [((i + by) % count, i) for i in...  11.2 us
    ppermute x2, starting transfers between devices, from_block(): lax.ppermute(array, ('zh', 'core', 'yh'), [((i + by) % count, i) for i in...  7.94 us
    unnamed x19, local copies, waits for them, and re-layouts  4.88 us
  transfers between devices with their start and end apart: 7, of which 3 were waited for; matrix products, arithmetic and copies ran while one was open for 1% of the time, Pallas kernels for 27%

profile of v4, /device:TPU:272, one launch (start us, length us, event | category | flops | bytes accessed | tf_op | source)
XLA Modules:
  0.0 141.6 jit_solution(18384143561724171815)
XLA Ops:
  0.0 3.6 %shard_map.64 = bf16[16,3,128,128]{3,2,1,0:T(8,128)(2,1)} custom-call(s32[24]{0:T(128)} %order_ref.5, bf16[128,3072]{1,0:T(8,128)(2,1)} %q_ref.1, bf16[128,3072]{1,0:T(8,128)(2,1)} %k_ref.1, bf16[128,3072]{1,0:T(8,128)(2,1)} %v_ref.1), custom_call_target="tpu_custom_call" | custom-call | tf_op jit(solution)/shard_map/pallas_call | solution.py:57
  3.6 0.0 copy-start
  3.6 0.0 copy-start.1
  3.7 0.0 copy-start.6
  3.7 6.5 %all-to-all-start = ((bf16[16,3,128,128]{3,2,1,0:T(8,128)(2,1)}), bf16[16,3,128,128]{3,2,1,0:T(8,128)(2,1)S(1)}, u32[]{:S(2)}, u32[]{:S(2)}) async-start(bf16[16,3,128,128]{3,2,1,0:T(8,128)(2,1)} %shard_map.64), calls=%async_computation | async-start | bytes 3145728 | tf_op jit(solution)/shard_map/all_to_all | solution.py:383
  10.2 0.0 copy-done
  10.2 0.0 copy-done.1
  10.2 0.0 copy-done.6
  10.2 0.0 copy-start.2
  10.2 1.1 copy-done.2
  11.3 1.5 %shard_map.65 = (bf16[64,3,8,128]{3,2,1,0:T(8,128)(2,1)S(1)}, bf16[64,3,8,128]{3,2,1,0:T(8,128)(2,1)}) custom-call(s32[1]{0:T(128)} %bitcast.core_ref, s32[24]{0:T(128)S(1)} %copy-done.6, bf16[128,3072]{1,0:T(8,128)(2,1)S(1)} %copy-done, bf16[128,3072]{1,0:T(8,128)(2,1)S(1)} %copy-done.1, bf16[128,3072]{1,0:T(8,128)(2,1)S(1)} %copy-done.2), custom_call_target="tpu_custom_call" | custom-call | tf_op jit(solution)/shard_map/pallas_call | solution.py:78
  12.8 1.9 %collective-permute-start = (bf16[64,3,8,128]{3,2,1,0:T(8,128)(2,1)}, bf16[64,3,8,128]{3,2,1,0:T(8,128)(2,1)S(1)}, u32[]{:S(2)}, u32[]{:S(2)}) collective-permute-start(bf16[64,3,8,128]{3,2,1,0:T(8,128)(2,1)} %get-tuple-element.17), channel_id=1, source_target_pairs={{0,64},{64,0},{1,65},{65,1},{2,66},{66,2},{3,67},{67,3},{4,68},{68... | collective-permute-start | bytes 1179656 | tf_op jit(solution)/shard_map/ppermute | solution.py:405
  14.7 1.9 %collective-permute-done = bf16[64,3,8,128]{3,2,1,0:T(8,128)(2,1)S(1)} collective-permute-done((bf16[64,3,8,128]{3,2,1,0:T(8,128)(2,1)}, bf16[64,3,8,128]{3,2,1,0:T(8,128)(2,1)S(1)}, u32[]{:S(2)}, u32[]{:S(2)}) %collective-permute-start) | collective-permute-done | bytes 393248 | tf_op jit(solution)/shard_map/ppermute | solution.py:405
  16.6 0.1 shard_map.66
  16.7 3.8 %collective-permute-start.1 = (bf16[32,2,3,8,128]{4,3,2,1,0:T(8,128)(2,1)S(1)}, bf16[32,2,3,8,128]{4,3,2,1,0:T(8,128)(2,1)S(1)}, u32[]{:S(2)}, u32[]{:S(2)}) collective-permute-start(bf16[32,2,3,8,128]{4,3,2,1,0:T(8,128)(2,1)S(1)} %get-tuple-element.19), channel_id=1, source_target_pairs={{0,4},{4,0},{1,5},{5,1},{2,6},{6,2},{3,7},{7,3},{8,12},{12,8},{9,1... | collective-permute-start | bytes 1179656 | tf_op jit(solution)/shard_map/ppermute | solution.py:408
  20.5 17.8 %collective-permute-done.1.b_ref = bf16[32,2,3,8,128]{4,3,2,1,0:T(8,128)(2,1)S(1)} collective-permute-done((bf16[32,2,3,8,128]{4,3,2,1,0:T(8,128)(2,1)S(1)}, bf16[32,2,3,8,128]{4,3,2,1,0:T(8,128)(2,1)S(1)}, u32[]{:S(2)}, u32[]{:S(2)}) %collective-permute-start.1) | collective-permute-done | bytes 393248 | tf_op jit(solution)/shard_map/ppermute | solution.py:408
  38.3 0.0 copy-start.8
  38.3 0.9 shard_map.67
  39.2 0.0 all-to-all-done.in_ref
  39.3 12.0 %all-to-all-start.1 = ((bf16[32,2,2,3,8,128]{5,4,3,2,1,0:T(8,128)(2,1)}), bf16[32,2,2,3,8,128]{5,4,3,2,1,0:T(8,128)(2,1)S(1)}, u32[]{:S(2)}, u32[]{:S(2)}) async-start(bf16[32,2,2,3,8,128]{5,4,3,2,1,0:T(8,128)(2,1)} %shard_map.67), calls=%async_computation.1 | async-start | bytes 1572864 | tf_op jit(solution)/shard_map/all_to_all | solution.py:383
  51.2 0.0 copy-done.8
  51.2 0.1 copy.7.kb_ref
  51.4 0.0 copy-start.7
  51.4 1.5 %fusion = (bf16[12,2,128,128]{3,2,1,0:T(8,128)(2,1)}, bf16[12,2,128,128]{3,2,1,0:T(8,128)(2,1)}) fusion(bf16[16,3,128,128]{3,2,1,0:T(8,128)(2,1)S(1)} %all-to-all-done.in_ref), kind=kLoop, calls=%fused_computation | loop fusion | bytes 3145728 | tf_op jit(solution)/shard_map/slice | solution.py:412
  52.9 2.5 %collective-permute-start.3 = (bf16[12,2,128,128]{3,2,1,0:T(8,128)(2,1)}, bf16[12,2,128,128]{3,2,1,0:T(8,128)(2,1)}, u32[]{:S(2)}, u32[]{:S(2)}) collective-permute-start(bf16[12,2,128,128]{3,2,1,0:T(8,128)(2,1)} %get-tuple-element.27), channel_id=1, source_target_pairs={{16,0},{32,16},{48,32},{64,48},{80,64},{96,80},{112,96},{128,112},... | collective-permute-start | bytes 2359304 | tf_op jit(solution)/shard_map/ppermute | solution.py:388
  55.3 5.5 %collective-permute-start.2 = (bf16[12,2,128,128]{3,2,1,0:T(8,128)(2,1)}, bf16[12,2,128,128]{3,2,1,0:T(8,128)(2,1)}, u32[]{:S(2)}, u32[]{:S(2)}) collective-permute-start(bf16[12,2,128,128]{3,2,1,0:T(8,128)(2,1)} %get-tuple-element.28), channel_id=1, source_target_pairs={{496,0},{0,16},{16,32},{32,48},{48,64},{64,80},{80,96},{96,112},{1... | collective-permute-start | bytes 2359304 | tf_op jit(solution)/shard_map/ppermute | solution.py:388
  60.8 0.0 copy-done.7
  60.8 15.5 %shard_map.69 = (f32[4,512,256]{2,1,0:T(8,128)S(1)}, f32[4,512,128]{2,1,0:T(8,128)S(1)}, f32[2]{0:T(128)S(1)}) custom-call(s32[1]{0:T(128)} %bitcast.5.base_ref, s32[128,6]{1,0:T(8,128)S(1)} %copy.7.kb_ref, s32[128]{0:T(128)S(1)} %copy-done.7, bf16[16,3,128,128]{3,2,1,0:T(8,128)(2,1)S(1)} %all-to-all-done.in_ref), custom_call_target="tpu_custom_call" | custom-call | flops 10000000000 | bytes 1048576 | tf_op jit(solution)/shard_map/pallas_call | solution.py:327
  76.4 0.0 copy-start.3
  76.4 1.3 copy-done.3
  77.7 0.0 all-to-all-done.1.in_ref
  77.7 2.2 %shard_map.68 = bf16[8,8,2,8,128]{4,3,2,1,0:T(8,128)(2,1)S(1)} custom-call(s32[1]{0:T(128)} %bitcast.core_ref, s32[1]{0:T(128)} %bitcast.1.low_ref, bf16[32,2,2,3,8,128]{5,4,3,2,1,0:T(8,128)(2,1)S(1)} %all-to-all-done.1.in_ref), custom_call_target="tpu_custom_call" | custom-call | flops 49999998976 | bytes 1048576 | tf_op jit(solution)/shard_map/pallas_call | solution.py:144
  79.9 0.0 copy-start.5
  79.9 0.7 copy-done.5
  80.6 15.8 %all-to-all-start.2 = ((bf16[128,8,128]{2,1,0:T(8,128)(2,1)}), bf16[128,8,128]{2,1,0:T(8,128)(2,1)S(1)}, u32[]{:S(2)}, u32[]{:S(2)}) async-start(bf16[128,8,128]{2,1,0:T(8,128)(2,1)} %bitcast.8), calls=%async_computation.2 | async-start | bytes 524288 | tf_op jit(solution)/shard_map/all_to_all | solution.py:383
  96.4 11.2 %collective-permute-done.3.more_ref = bf16[12,2,128,128]{3,2,1,0:T(8,128)(2,1)} collective-permute-done((bf16[12,2,128,128]{3,2,1,0:T(8,128)(2,1)}, bf16[12,2,128,128]{3,2,1,0:T(8,128)(2,1)}, u32[]{:S(2)}, u32[]{:S(2)}) %collective-permute-start.3) | collective-permute-done | bytes 786464 | tf_op jit(solution)/shard_map/ppermute | solution.py:388
  107.7 0.0 collective-permute-done.2.less_ref
  107.7 0.0 copy-start.4
  107.7 1.6 %copy-done.4 = f32[4,512,256]{2,1,0:T(8,128)S(1)} copy-done((f32[4,512,256]{2,1,0:T(8,128)S(1)}, f32[4,512,256]{2,1,0:T(8,128)}, u32[]{:S(2)}) %copy-start.4) | copy-done | bytes 2097176
  109.3 17.3 %shard_map.70 = bf16[16,128,128]{2,1,0:T(8,128)(2,1)S(1)} custom-call(s32[1]{0:T(128)} %bitcast.5.base_ref, s32[128,6]{1,0:T(8,128)S(1)} %copy.7.kb_ref, s32[128]{0:T(128)S(1)} %copy-done.7, f32[2]{0:T(128)S(1)} %get-tuple-element.24.stat_ref, bf16[16,3,128,128]{3,2,1,0:T(8,128)(2,1)S(1)} %all-to-all-done.in_ref, ...), custom_call_target="tpu_custom_call" | custom-call | tf_op jit(solution)/shard_map/pallas_call | solution.py:344
  126.6 0.0 all-to-all-done.2.t_ref
  126.6 13.3 %all_to_all.20.s_ref = bf16[16,128,128]{2,1,0:T(8,128)(2,1)S(1)} all-to-all(bf16[16,128,128]{2,1,0:T(8,128)(2,1)S(1)} %shard_map.70), channel_id=1, replica_groups=mesh['zh'=4,'core'=2,'yh'=4,'yl'=2,'zl'=2,'x'=4] {'yl','zl','x'}, dimensions={0} | all-to-all | bytes 1048576 | tf_op jit(solution)/shard_map/all_to_all | solution.py:383
  139.9 1.6 %shard_map.71 = bf16[128,3072]{1,0:T(8,128)(2,1)} custom-call(s32[24]{0:T(128)S(1)} %copy-done.6, bf16[128,8,128]{2,1,0:T(8,128)(2,1)S(1)} %all-to-all-done.2.t_ref, bf16[16,128,128]{2,1,0:T(8,128)(2,1)S(1)} %all_to_all.20.s_ref), custom_call_target="tpu_custom_call" | custom-call | tf_op jit(solution)/shard_map/pallas_call | solution.py:373
Async XLA Ops:
  3.6 6.5 %copy-start = (bf16[128,3072]{1,0:T(8,128)(2,1)S(1)}, bf16[128,3072]{1,0:T(8,128)(2,1)}, u32[]{:S(2)}) copy-start(bf16[128,3072]{1,0:T(8,128)(2,1)} %q_ref.1) | copy-start | bytes 2359300
  3.6 6.5 %copy-start.1 = (bf16[128,3072]{1,0:T(8,128)(2,1)S(1)}, bf16[128,3072]{1,0:T(8,128)(2,1)}, u32[]{:S(2)}) copy-start(bf16[128,3072]{1,0:T(8,128)(2,1)} %k_ref.1) | copy-start | bytes 2359300
  3.7 6.5 %copy-start.6 = (s32[24]{0:T(128)S(1)}, s32[24]{0:T(128)}, u32[]{:S(2)}) copy-start(s32[24]{0:T(128)} %order_ref.5) | copy-start | bytes 292
  3.7 35.6 %all-to-all-start = ((bf16[16,3,128,128]{3,2,1,0:T(8,128)(2,1)}), bf16[16,3,128,128]{3,2,1,0:T(8,128)(2,1)S(1)}, u32[]{:S(2)}, u32[]{:S(2)}) async-start(bf16[16,3,128,128]{3,2,1,0:T(8,128)(2,1)} %shard_map.64), calls=%async_computation | async-start | bytes 3145728 | tf_op jit(solution)/shard_map/all_to_all | solution.py:383
  10.2 1.1 copy-start.2
  12.8 3.8 %collective-permute-start = (bf16[64,3,8,128]{3,2,1,0:T(8,128)(2,1)}, bf16[64,3,8,128]{3,2,1,0:T(8,128)(2,1)S(1)}, u32[]{:S(2)}, u32[]{:S(2)}) collective-permute-start(bf16[64,3,8,128]{3,2,1,0:T(8,128)(2,1)} %get-tuple-element.17), channel_id=1, source_target_pairs={{0,64},{64,0},{1,65},{65,1},{2,66},{66,2},{3,67},{67,3},{4,68},{68... | collective-permute-start | bytes 1179656 | tf_op jit(solution)/shard_map/ppermute | solution.py:405
  16.7 21.6 %collective-permute-start.1 = (bf16[32,2,3,8,128]{4,3,2,1,0:T(8,128)(2,1)S(1)}, bf16[32,2,3,8,128]{4,3,2,1,0:T(8,128)(2,1)S(1)}, u32[]{:S(2)}, u32[]{:S(2)}) collective-permute-start(bf16[32,2,3,8,128]{4,3,2,1,0:T(8,128)(2,1)S(1)} %get-tuple-element.19), channel_id=1, source_target_pairs={{0,4},{4,0},{1,5},{5,1},{2,6},{6,2},{3,7},{7,3},{8,12},{12,8},{9,1... | collective-permute-start | bytes 1179656 | tf_op jit(solution)/shard_map/ppermute | solution.py:408
  38.3 12.9 %copy-start.8 = (s32[128,6]{0,1:T(8,128)S(1)}, s32[128,6]{0,1:T(8,128)}, u32[]{:S(2)}) copy-start(s32[128,6]{0,1:T(8,128)} %param.10) | copy-start | bytes 9220
  39.3 38.5 %all-to-all-start.1 = ((bf16[32,2,2,3,8,128]{5,4,3,2,1,0:T(8,128)(2,1)}), bf16[32,2,2,3,8,128]{5,4,3,2,1,0:T(8,128)(2,1)S(1)}, u32[]{:S(2)}, u32[]{:S(2)}) async-start(bf16[32,2,2,3,8,128]{5,4,3,2,1,0:T(8,128)(2,1)} %shard_map.67), calls=%async_computation.1 | async-start | bytes 1572864 | tf_op jit(solution)/shard_map/all_to_all | solution.py:383
  51.4 9.5 %copy-start.7 = (s32[128]{0:T(128)S(1)}, s32[128]{0:T(128)}, u32[]{:S(2)}) copy-start(s32[128]{0:T(128)} %bc_ref.3) | copy-start | bytes 1540
  52.9 54.8 %collective-permute-start.3 = (bf16[12,2,128,128]{3,2,1,0:T(8,128)(2,1)}, bf16[12,2,128,128]{3,2,1,0:T(8,128)(2,1)}, u32[]{:S(2)}, u32[]{:S(2)}) collective-permute-start(bf16[12,2,128,128]{3,2,1,0:T(8,128)(2,1)} %get-tuple-element.27), channel_id=1, source_target_pairs={{16,0},{32,16},{48,32},{64,48},{80,64},{96,80},{112,96},{128,112},... | collective-permute-start | bytes 2359304 | tf_op jit(solution)/shard_map/ppermute | solution.py:388
  55.3 52.3 %collective-permute-start.2 = (bf16[12,2,128,128]{3,2,1,0:T(8,128)(2,1)}, bf16[12,2,128,128]{3,2,1,0:T(8,128)(2,1)}, u32[]{:S(2)}, u32[]{:S(2)}) collective-permute-start(bf16[12,2,128,128]{3,2,1,0:T(8,128)(2,1)} %get-tuple-element.28), channel_id=1, source_target_pairs={{496,0},{0,16},{16,32},{32,48},{48,64},{64,80},{80,96},{96,112},{1... | collective-permute-start | bytes 2359304 | tf_op jit(solution)/shard_map/ppermute | solution.py:388
  76.4 1.3 copy-start.3
  79.9 0.7 copy-start.5
  80.6 46.0 %all-to-all-start.2 = ((bf16[128,8,128]{2,1,0:T(8,128)(2,1)}), bf16[128,8,128]{2,1,0:T(8,128)(2,1)S(1)}, u32[]{:S(2)}, u32[]{:S(2)}) async-start(bf16[128,8,128]{2,1,0:T(8,128)(2,1)} %bitcast.8), calls=%async_computation.2 | async-start | bytes 524288 | tf_op jit(solution)/shard_map/all_to_all | solution.py:383
  107.7 1.6 %copy-start.4 = (f32[4,512,256]{2,1,0:T(8,128)S(1)}, f32[4,512,256]{2,1,0:T(8,128)}, u32[]{:S(2)}) copy-start(f32[4,512,256]{2,1,0:T(8,128)} %copy-done.3) | copy-start | bytes 6291460

commit v5 on v3

--- a/solution.py
+++ b/solution.py
@@ -194,11 +194,16 @@
     return block.reshape(pieces * block.shape[1], DEPTH)
 
 
-def own_kernel(frames, base_ref, kb_ref, bc_ref, in_ref, acc_ref, m_ref, stat_ref):
+def upper_lanes(rows):
+    return lax.broadcasted_iota(jnp.int32, (rows, LANES), 1) >= LANES // 2
+
+
+def own_kernel(frames, base_ref, kb_ref, bc_ref, in_ref, acc_ref, side_ref, q_ref, stat_ref, both_ref, m_ref):
     pieces = in_ref.shape[0] // BLOCK
     size = pieces * in_ref.shape[2]
     base = base_ref[0]
     part = functools.partial(frame_at, in_ref, pieces=pieces)
+    q_ref[...] = in_ref[:, pl.ds(0, 1)]
     q_norm = row_norm([part(0, at) for at in range(BLOCK)])
     k_norm = row_norm([part(1, at) for at in range(BLOCK)])
     fast = small_scores(q_norm, k_norm)
@@ -212,8 +217,9 @@
     def _():
         def frame(mine, carry):
             pairs = [(part(1, slot), part(2, slot), used(mine, slot)) for slot in range(BLOCK)]
-            acc_ref[mine] = add_frames(None, part(0, mine), pairs)
-            m_ref[mine] = jnp.zeros((size, LANES), F32)
+            acc = add_frames(None, part(0, mine), pairs)
+            acc_ref[mine] = acc[:, :DEPTH]
+            side_ref[mine] = acc[:, DEPTH:]
             return carry
 
         lax.fori_loop(0, BLOCK, frame, 0)
@@ -225,12 +231,17 @@
 
             @pl.when(slot == 0)
             def _():
-                acc_ref[mine] = jnp.zeros((size, 2 * DEPTH), F32)
-                m_ref[mine] = jnp.full((size, LANES), -jnp.inf, F32)
+                both_ref[...] = jnp.zeros((size, 2 * DEPTH), F32)
+                m_ref[...] = jnp.full((size, LANES), -jnp.inf, F32)
 
             @pl.when(used(mine, slot))
             def _():
-                fold_frame(part(0, mine), part(1, slot), part(2, slot), acc_ref.at[mine], m_ref.at[mine])
+                fold_frame(part(0, mine), part(1, slot), part(2, slot), both_ref, m_ref)
+
+            @pl.when(slot == BLOCK - 1)
+            def _():
+                acc_ref[mine] = both_ref[:, :DEPTH]
+                side_ref[mine] = jnp.where(upper_lanes(size), m_ref[...], both_ref[:, DEPTH:])
 
             return carry
 
@@ -238,29 +249,22 @@
 
 
 def near_kernel(
-    frames, base_ref, kb_ref, bc_ref, stat_ref, q_ref, less_ref, more_ref, acc_hbm, m_hbm, o_ref,
-    acc_ref, m_ref, near_ref, sems, acc_sems, m_sem
+    frames, base_ref, kb_ref, bc_ref, stat_ref, q_ref, less_ref, more_ref, acc_in, side_in, o_ref,
+    acc_ref, m_ref, near_ref, sems
 ):
     pieces = q_ref.shape[0] // BLOCK
     rows = q_ref.shape[2]
+    size = pieces * rows
     base = base_ref[0]
-    sums = [
-        pltpu.make_async_copy(acc_hbm.at[mine], acc_ref.at[mine], acc_sems.at[mine])
-        for mine in range(BLOCK)
-    ]
-    frames_in = [
-        pltpu.make_async_copy(less_ref, near_ref.at[pl.ds(0, W * pieces)], sems.at[0]),
-        pltpu.make_async_copy(more_ref, near_ref.at[pl.ds(W * pieces, W * pieces)], sems.at[1]),
-    ]
-    for copy in frames_in + sums:
-        copy.start()
-    for copy in frames_in:
-        copy.wait()
+    run_copies(
+        [
+            pltpu.make_async_copy(less_ref, near_ref.at[pl.ds(0, W * pieces)], sems.at[0]),
+            pltpu.make_async_copy(more_ref, near_ref.at[pl.ds(W * pieces, W * pieces)], sems.at[1]),
+        ]
+    )
     part = functools.partial(frame_at, near_ref, pieces=pieces)
     k_norm = row_norm([part(0, at) for at in range(2 * W)])
     fast = small_scores(stat_ref[0], k_norm) & (stat_ref[1] > 0.5)
-    for copy in sums:
-        copy.wait()
 
     def query(mine):
         return frame_at(q_ref, 0, mine, pieces)
@@ -279,7 +283,8 @@
             pairs = [
                 (part(0, mine + j), part(1, mine + j), used(mine, mine + j)) for j in range(W)
             ]
-            finish(mine, add_frames(acc_ref[mine], query(mine), pairs))
+            acc = jnp.concatenate([acc_in[mine], side_in[mine]], axis=1)
+            finish(mine, add_frames(acc, query(mine), pairs))
             return carry
 
         lax.fori_loop(0, BLOCK, frame, 0)
@@ -287,17 +292,22 @@
     @pl.when(jnp.logical_not(fast))
     def _():
         def frame(mine, carry):
-            run_copies([pltpu.make_async_copy(m_hbm.at[mine], m_ref, m_sem)])
+            side = side_in[mine]
+            quick = jnp.full((size, LANES), stat_ref[1], F32) > 0.5
+            top = jnp.broadcast_to(side[:, LANES - 1 :], (size, LANES))
+            m_ref[...] = jnp.where(quick, 0.0, top)
+            acc_ref[:, :DEPTH] = acc_in[mine]
+            acc_ref[:, DEPTH:] = jnp.broadcast_to(side[:, :1], (size, LANES))
 
             def pair(j, inner):
                 @pl.when(used(mine, mine + j))
                 def _():
-                    fold_frame(query(mine), part(0, mine + j), part(1, mine + j), acc_ref.at[mine], m_ref)
+                    fold_frame(query(mine), part(0, mine + j), part(1, mine + j), acc_ref, m_ref)
 
                 return inner
 
             lax.fori_loop(0, W, pair, 0)
-            finish(mine, acc_ref[mine])
+            finish(mine, acc_ref[...])
             return carry
 
         lax.fori_loop(0, BLOCK, frame, 0)
@@ -309,35 +319,35 @@
     return pl.pallas_call(
         functools.partial(own_kernel, frames),
         out_shape=[
-            jax.ShapeDtypeStruct((BLOCK, size, 2 * depth), F32),
+            jax.ShapeDtypeStruct((BLOCK, size, depth), F32),
             jax.ShapeDtypeStruct((BLOCK, size, LANES), F32),
+            jax.ShapeDtypeStruct((dests, 1, rows, depth), BF),
             jax.ShapeDtypeStruct((2,), F32),
         ],
         in_specs=[SMEM] * 3 + [VMEM],
-        out_specs=[VMEM, VMEM, SMEM],
+        out_specs=[VMEM, VMEM, VMEM, SMEM],
+        scratch_shapes=[pltpu.VMEM((size, 2 * depth), F32), pltpu.VMEM((size, LANES), F32)],
         compiler_params=PARAMS,
         cost_estimate=estimate(10),
     )(base, kb, bc, arrived)
 
 
-def attend_near(base, kb, bc, stat, q, less, more, acc, top, frames):
+def attend_near(base, kb, bc, stat, q, less, more, sums, frames):
     dests, _, rows, depth = q.shape
     size = dests // BLOCK * rows
     return pl.pallas_call(
         functools.partial(near_kernel, frames),
         out_shape=jax.ShapeDtypeStruct((dests, rows, depth), BF),
-        in_specs=[SMEM] * 4 + [VMEM] + [ANY] * 4,
+        in_specs=[SMEM] * 4 + [VMEM, ANY, ANY, VMEM, VMEM],
         out_specs=VMEM,
         scratch_shapes=[
-            pltpu.VMEM((BLOCK, size, 2 * depth), F32),
+            pltpu.VMEM((size, 2 * depth), F32),
             pltpu.VMEM((size, LANES), F32),
             pltpu.VMEM((2 * less.shape[0], *less.shape[1:]), BF),
             pltpu.SemaphoreType.DMA((2,)),
-            pltpu.SemaphoreType.DMA((BLOCK,)),
-            pltpu.SemaphoreType.DMA,
         ],
         compiler_params=PARAMS,
-    )(base, kb, bc, stat, q, less, more, acc, top)
+    )(base, kb, bc, stat, q, less, more, *sums)
 
 
 def assemble_kernel(order_ref, t_ref, s_ref, out_ref):
@@ -388,10 +398,10 @@
     more = from_block(qkv[: W * pieces, 1:], 1)
     qkv, st = lax.optimization_barrier((qkv, st))
     at = exchange(st, ("zh", "yh", "yl", "zl"))
-    acc, top, stat = attend_own(base, key_blocks, block_count, qkv, frames)
+    *sums, q, stat = attend_own(base, key_blocks, block_count, qkv, frames)
     to, stat = lax.optimization_barrier((temporal_attend(core, at), stat))
     tr = exchange(to, loop_axes)
-    so = attend_near(base, key_blocks, block_count, stat, qkv, less, more, acc, top, frames)
+    so = attend_near(base, key_blocks, block_count, stat, q, less, more, sums, frames)
     sr = exchange(so, block_axes)
     return assemble(head_order, tr, sr, rows, width)
 

time: 136 us -> 136 us (level)
  the two profiles are of different devices: /device:TPU:16 before, /device:TPU:1 now
where the time goes in v5:
time: 136 us
  starting transfers between devices  50.1 us (37%)
  Pallas kernels  42.4 us (31%)
  waiting for transfers between devices  20.3 us (15%)
  blocking collectives  17 us (12%)
  local copies, waits for them, and re-layouts  5.74 us (4%)
    all_to_all x3, starting transfers between devices, exchange(): return lax.all_to_all(array, axes, 0, 0, tiled=True)  35.9 us
    all_to_all x1, blocking collectives, exchange(): return lax.all_to_all(array, axes, 0, 0, tiled=True)  17 us
    pallas_call x1, Pallas kernels, attend_own(): pl.pallas_call(functools.partial(own_kernel, frames), out_shape=[jax.Shap...  16.9 us
    pallas_call x1, Pallas kernels, attend_near(): pl.pallas_call(functools.partial(near_kernel, frames), out_shape=jax.Shap...  15.6 us
    all_to_all x3, waiting for transfers between devices, exchange(): return lax.all_to_all(array, axes, 0, 0, tiled=True)  11.1 us
    ppermute x2, starting transfers between devices, from_block(): lax.ppermute(array, ('zh', 'core', 'yh'), [((i + by) % count, i) for i in...  9.51 us
    ppermute x2, waiting for transfers between devices, from_block(): lax.ppermute(array, ('zh', 'core', 'yh'), [((i + by) % count, i) for i in...  7.87 us
    ppermute x1, starting transfers between devices, local(): st = join(mine, lax.ppermute(other, 'core', [(0, 1), (1, 0)]))  4.72 us
  transfers between devices with their start and end apart: 6, of which 3 were waited for; matrix products, arithmetic and copies ran while one was open for 1% of the time, Pallas kernels for 27%

profile of v5, /device:TPU:1, one launch (start us, length us, event | category | flops | bytes accessed | tf_op | source)
XLA Modules:
  0.0 135.7 jit_solution(10891925254901574567)
XLA Ops:
  0.0 3.6 %shard_map.64 = bf16[16,3,128,128]{3,2,1,0:T(8,128)(2,1)} custom-call(s32[24]{0:T(128)} %order_ref.5, bf16[128,3072]{1,0:T(8,128)(2,1)} %q_ref.1, bf16[128,3072]{1,0:T(8,128)(2,1)} %k_ref.1, bf16[128,3072]{1,0:T(8,128)(2,1)} %v_ref.1), custom_call_target="tpu_custom_call" | custom-call | tf_op jit(solution)/shard_map/pallas_call | solution.py:57
  3.6 0.0 copy-start
  3.6 0.0 copy-start.1
  3.7 0.0 copy-start.7
  3.7 7.9 %all-to-all-start = ((bf16[16,3,128,128]{3,2,1,0:T(8,128)(2,1)}), bf16[16,3,128,128]{3,2,1,0:T(8,128)(2,1)S(1)}, u32[]{:S(2)}, u32[]{:S(2)}) async-start(bf16[16,3,128,128]{3,2,1,0:T(8,128)(2,1)} %shard_map.64), calls=%async_computation | async-start | bytes 3145728 | tf_op jit(solution)/shard_map/all_to_all | solution.py:374
  11.6 0.0 copy-done
  11.6 0.0 copy-done.1
  11.6 0.0 copy-done.7
  11.6 0.0 copy-start.2
  11.6 1.1 copy-done.2
  12.8 0.7 shard_map.65
  13.5 4.7 %collective-permute-start = (bf16[64,3,8,128]{3,2,1,0:T(8,128)(2,1)S(1)}, bf16[64,3,8,128]{3,2,1,0:T(8,128)(2,1)S(1)}, u32[]{:S(2)}, u32[]{:S(2)}) collective-permute-start(bf16[64,3,8,128]{3,2,1,0:T(8,128)(2,1)S(1)} %get-tuple-element.16), channel_id=1, source_target_pairs={{0,64},{64,0},{1,65},{65,1},{2,66},{66,2},{3,67},{67,3},{4,68},{68... | collective-permute-start | bytes 1179656 | tf_op jit(solution)/shard_map/ppermute | solution.py:394
  18.3 1.3 collective-permute-done.b_ref
  19.6 0.0 copy-start.9
  19.6 0.9 shard_map.66
  20.5 11.1 %all-to-all-done.in_ref = bf16[16,3,128,128]{3,2,1,0:T(8,128)(2,1)S(1)} async-done(((bf16[16,3,128,128]{3,2,1,0:T(8,128)(2,1)}), bf16[16,3,128,128]{3,2,1,0:T(8,128)(2,1)S(1)}, u32[]{:S(2)}, u32[]{:S(2)}) %all-to-all-start) | async-done | bytes 1572896 | tf_op jit(solution)/shard_map/all_to_all | solution.py:374
  31.7 15.7 %all-to-all-start.1 = ((bf16[64,2,3,8,128]{4,3,2,1,0:T(8,128)(2,1)}), bf16[64,2,3,8,128]{4,3,2,1,0:T(8,128)(2,1)S(1)}, u32[]{:S(2)}, u32[]{:S(2)}) async-start(bf16[64,2,3,8,128]{4,3,2,1,0:T(8,128)(2,1)} %shard_map.66), calls=%async_computation.1 | async-start | bytes 1572864 | tf_op jit(solution)/shard_map/all_to_all | solution.py:374
  47.4 0.0 copy-done.9
  47.4 0.1 copy.7.kb_ref
  47.5 0.0 copy-start.8
  47.5 1.5 %fusion = (bf16[12,2,128,128]{3,2,1,0:T(8,128)(2,1)}, bf16[12,2,128,128]{3,2,1,0:T(8,128)(2,1)}) fusion(bf16[16,3,128,128]{3,2,1,0:T(8,128)(2,1)S(1)} %all-to-all-done.in_ref), kind=kLoop, calls=%fused_computation | loop fusion | bytes 3145728 | tf_op jit(solution)/shard_map/slice | solution.py:398
  49.0 7.6 %collective-permute-start.2 = (bf16[12,2,128,128]{3,2,1,0:T(8,128)(2,1)}, bf16[12,2,128,128]{3,2,1,0:T(8,128)(2,1)}, u32[]{:S(2)}, u32[]{:S(2)}) collective-permute-start(bf16[12,2,128,128]{3,2,1,0:T(8,128)(2,1)} %get-tuple-element.25), channel_id=1, source_target_pairs={{16,0},{32,16},{48,32},{64,48},{80,64},{96,80},{112,96},{128,112},... | collective-permute-start | bytes 2359304 | tf_op jit(solution)/shard_map/ppermute | solution.py:379
  56.6 1.9 %collective-permute-start.1 = (bf16[12,2,128,128]{3,2,1,0:T(8,128)(2,1)}, bf16[12,2,128,128]{3,2,1,0:T(8,128)(2,1)}, u32[]{:S(2)}, u32[]{:S(2)}) collective-permute-start(bf16[12,2,128,128]{3,2,1,0:T(8,128)(2,1)} %get-tuple-element.26), channel_id=1, source_target_pairs={{496,0},{0,16},{16,32},{32,48},{48,64},{64,80},{80,96},{96,112},{1... | collective-permute-start | bytes 2359304 | tf_op jit(solution)/shard_map/ppermute | solution.py:379
  58.5 0.0 copy-done.8
  58.5 16.9 %shard_map.68 = (f32[4,512,128]{2,1,0:T(8,128)S(1)}, f32[4,512,128]{2,1,0:T(8,128)S(1)}, bf16[16,1,128,128]{3,2,1,0:T(8,128)(2,1)S(1)}, f32[2]{0:T(128)S(1)}) custom-call(s32[1]{0:T(128)} %bitcast.1.base_ref, s32[128,6]{1,0:T(8,128)S(1)} %copy.7.kb_ref, s32[128]{0:T(128)S(1)} %copy-done.8, bf16[16,3,128,128]{3,2,1,0:T(8,128)(2,1)S(1)} %all-to-all-done.in_ref), custom_call_target="tpu_custom_call" | custom-call | flops 10000000000 | bytes 1048576 | tf_op jit(solution)/shard_map/pallas_call | solution.py:319
  75.5 0.0 copy-start.3
  75.5 1.0 copy-done.3
  76.4 0.0 copy-start.5
  76.4 0.8 copy-done.5
  77.2 0.0 all-to-all-done.1.in_ref
  77.2 0.0 copy-start.6
  77.2 2.9 %shard_map.67 = bf16[128,8,128]{2,1,0:T(8,128)(2,1)} custom-call(s32[1]{0:T(128)} %bitcast.core_ref, bf16[64,2,3,8,128]{4,3,2,1,0:T(8,128)(2,1)S(1)} %all-to-all-done.1.in_ref), custom_call_target="tpu_custom_call" | custom-call | flops 49999998976 | bytes 1048576 | tf_op jit(solution)/shard_map/pallas_call | solution.py:128
  80.1 12.3 %all-to-all-start.2 = ((bf16[128,8,128]{2,1,0:T(8,128)(2,1)}), bf16[128,8,128]{2,1,0:T(8,128)(2,1)S(1)}, u32[]{:S(2)}, u32[]{:S(2)}) async-start(bf16[128,8,128]{2,1,0:T(8,128)(2,1)} %shard_map.67), calls=%async_computation.2 | async-start | bytes 524288 | tf_op jit(solution)/shard_map/all_to_all | solution.py:374
  92.4 7.9 %collective-permute-done.2.more_ref = bf16[12,2,128,128]{3,2,1,0:T(8,128)(2,1)} collective-permute-done((bf16[12,2,128,128]{3,2,1,0:T(8,128)(2,1)}, bf16[12,2,128,128]{3,2,1,0:T(8,128)(2,1)}, u32[]{:S(2)}, u32[]{:S(2)}) %collective-permute-start.2) | collective-permute-done | bytes 786464 | tf_op jit(solution)/shard_map/ppermute | solution.py:379
  100.3 0.0 collective-permute-done.1.less_ref
  100.3 0.0 copy-done.6
  100.3 0.0 copy-start.4
  100.3 1.2 copy-done.4
  101.5 15.6 %shard_map.69 = bf16[16,128,128]{2,1,0:T(8,128)(2,1)S(1)} custom-call(s32[1]{0:T(128)} %bitcast.1.base_ref, s32[128,6]{1,0:T(8,128)S(1)} %copy.7.kb_ref, s32[128]{0:T(128)S(1)} %copy-done.8, f32[2]{0:T(128)S(1)} %get-tuple-element.21.stat_ref, bf16[16,1,128,128]{3,2,1,0:T(8,128)(2,1)S(1)} %copy-done.6, ...), custom_call_target="tpu_custom_call" | custom-call | tf_op jit(solution)/shard_map/pallas_call | solution.py:338
  117.1 0.0 all-to-all-done.2.t_ref
  117.1 17.0 %all_to_all.20.s_ref = bf16[16,128,128]{2,1,0:T(8,128)(2,1)S(1)} all-to-all(bf16[16,128,128]{2,1,0:T(8,128)(2,1)S(1)} %shard_map.69), channel_id=1, replica_groups=mesh['zh'=4,'core'=2,'yh'=4,'yl'=2,'zl'=2,'x'=4] {'yl','zl','x'}, dimensions={0} | all-to-all | bytes 1048576 | tf_op jit(solution)/shard_map/all_to_all | solution.py:374
  134.1 1.6 %shard_map.70 = bf16[128,3072]{1,0:T(8,128)(2,1)} custom-call(s32[24]{0:T(128)S(1)} %copy-done.7, bf16[128,8,128]{2,1,0:T(8,128)(2,1)S(1)} %all-to-all-done.2.t_ref, bf16[16,128,128]{2,1,0:T(8,128)(2,1)S(1)} %all_to_all.20.s_ref), custom_call_target="tpu_custom_call" | custom-call | tf_op jit(solution)/shard_map/pallas_call | solution.py:364
Async XLA Ops:
  3.6 8.0 %copy-start = (bf16[128,3072]{1,0:T(8,128)(2,1)S(1)}, bf16[128,3072]{1,0:T(8,128)(2,1)}, u32[]{:S(2)}) copy-start(bf16[128,3072]{1,0:T(8,128)(2,1)} %q_ref.1) | copy-start | bytes 2359300
  3.6 8.0 %copy-start.1 = (bf16[128,3072]{1,0:T(8,128)(2,1)S(1)}, bf16[128,3072]{1,0:T(8,128)(2,1)}, u32[]{:S(2)}) copy-start(bf16[128,3072]{1,0:T(8,128)(2,1)} %k_ref.1) | copy-start | bytes 2359300
  3.7 8.0 %copy-start.7 = (s32[24]{0:T(128)S(1)}, s32[24]{0:T(128)}, u32[]{:S(2)}) copy-start(s32[24]{0:T(128)} %order_ref.5) | copy-start | bytes 292
  3.7 28.0 %all-to-all-start = ((bf16[16,3,128,128]{3,2,1,0:T(8,128)(2,1)}), bf16[16,3,128,128]{3,2,1,0:T(8,128)(2,1)S(1)}, u32[]{:S(2)}, u32[]{:S(2)}) async-start(bf16[16,3,128,128]{3,2,1,0:T(8,128)(2,1)} %shard_map.64), calls=%async_computation | async-start | bytes 3145728 | tf_op jit(solution)/shard_map/all_to_all | solution.py:374
  11.6 1.1 copy-start.2
  13.5 6.1 %collective-permute-start = (bf16[64,3,8,128]{3,2,1,0:T(8,128)(2,1)S(1)}, bf16[64,3,8,128]{3,2,1,0:T(8,128)(2,1)S(1)}, u32[]{:S(2)}, u32[]{:S(2)}) collective-permute-start(bf16[64,3,8,128]{3,2,1,0:T(8,128)(2,1)S(1)} %get-tuple-element.16), channel_id=1, source_target_pairs={{0,64},{64,0},{1,65},{65,1},{2,66},{66,2},{3,67},{67,3},{4,68},{68... | collective-permute-start | bytes 1179656 | tf_op jit(solution)/shard_map/ppermute | solution.py:394
  19.6 27.8 %copy-start.9 = (s32[128,6]{0,1:T(8,128)S(1)}, s32[128,6]{0,1:T(8,128)}, u32[]{:S(2)}) copy-start(s32[128,6]{0,1:T(8,128)} %param.10) | copy-start | bytes 9220
  31.7 45.6 %all-to-all-start.1 = ((bf16[64,2,3,8,128]{4,3,2,1,0:T(8,128)(2,1)}), bf16[64,2,3,8,128]{4,3,2,1,0:T(8,128)(2,1)S(1)}, u32[]{:S(2)}, u32[]{:S(2)}) async-start(bf16[64,2,3,8,128]{4,3,2,1,0:T(8,128)(2,1)} %shard_map.66), calls=%async_computation.1 | async-start | bytes 1572864 | tf_op jit(solution)/shard_map/all_to_all | solution.py:374
  47.5 11.0 %copy-start.8 = (s32[128]{0:T(128)S(1)}, s32[128]{0:T(128)}, u32[]{:S(2)}) copy-start(s32[128]{0:T(128)} %bc_ref.3) | copy-start | bytes 1540
  49.0 51.3 %collective-permute-start.2 = (bf16[12,2,128,128]{3,2,1,0:T(8,128)(2,1)}, bf16[12,2,128,128]{3,2,1,0:T(8,128)(2,1)}, u32[]{:S(2)}, u32[]{:S(2)}) collective-permute-start(bf16[12,2,128,128]{3,2,1,0:T(8,128)(2,1)} %get-tuple-element.25), channel_id=1, source_target_pairs={{16,0},{32,16},{48,32},{64,48},{80,64},{96,80},{112,96},{128,112},... | collective-permute-start | bytes 2359304 | tf_op jit(solution)/shard_map/ppermute | solution.py:379
  56.6 43.7 %collective-permute-start.1 = (bf16[12,2,128,128]{3,2,1,0:T(8,128)(2,1)}, bf16[12,2,128,128]{3,2,1,0:T(8,128)(2,1)}, u32[]{:S(2)}, u32[]{:S(2)}) collective-permute-start(bf16[12,2,128,128]{3,2,1,0:T(8,128)(2,1)} %get-tuple-element.26), channel_id=1, source_target_pairs={{496,0},{0,16},{16,32},{32,48},{48,64},{64,80},{80,96},{96,112},{1... | collective-permute-start | bytes 2359304 | tf_op jit(solution)/shard_map/ppermute | solution.py:379
  75.5 1.0 copy-start.3
  76.4 0.8 copy-start.5
  77.2 23.0 %copy-start.6 = (bf16[16,1,128,128]{3,2,1,0:T(8,128)(2,1)S(1)}, bf16[16,1,128,128]{3,2,1,0:T(8,128)(2,1)}, u32[]{:S(2)}) copy-start(bf16[16,1,128,128]{3,2,1,0:T(8,128)(2,1)} %copy-done.5) | copy-start | bytes 1572868
  80.1 37.0 %all-to-all-start.2 = ((bf16[128,8,128]{2,1,0:T(8,128)(2,1)}), bf16[128,8,128]{2,1,0:T(8,128)(2,1)S(1)}, u32[]{:S(2)}, u32[]{:S(2)}) async-start(bf16[128,8,128]{2,1,0:T(8,128)(2,1)} %shard_map.67), calls=%async_computation.2 | async-start | bytes 524288 | tf_op jit(solution)/shard_map/all_to_all | solution.py:374
  100.3 1.2 copy-start.4

commit v6 on v5

--- a/solution.py
+++ b/solution.py
@@ -40,26 +40,43 @@
 
 
 def pack_spatial_kernel(order_ref, *refs):
-    dst, sems = refs[-2:]
-    copies = []
-    for which, src in enumerate(refs[:-2]):
-        for head in range(dst.shape[0]):
-            column = columns_of(order_ref, HT + head)
-            copies.append(
-                pltpu.make_async_copy(src.at[:, column], dst.at[head, which], sems.at[which, head])
+    dst, held, sems, out_sems = refs[-4:]
+    heads = range(dst.shape[0])
+    inward = [
+        [
+            pltpu.make_async_copy(
+                src.at[:, columns_of(order_ref, HT + head)], held.at[head, which], sems.at[which, head]
             )
-    run_copies(copies)
+            for which, src in enumerate(refs[:-4])
+        ]
+        for head in heads
+    ]
+    outward = [pltpu.make_async_copy(held.at[head], dst.at[head], out_sems.at[head]) for head in heads]
+    for group in inward:
+        for copy in group:
+            copy.start()
+    for group, out in zip(inward, outward):
+        for copy in group:
+            copy.wait()
+        out.start()
+    for out in outward:
+        out.wait()
 
 
 def pack_spatial(order, arrays):
     rows, width = arrays[0].shape
     heads = width // DEPTH - HT
+    shape = (heads, len(arrays), rows, DEPTH)
     return pl.pallas_call(
         pack_spatial_kernel,
-        out_shape=jax.ShapeDtypeStruct((heads, len(arrays), rows, DEPTH), BF),
+        out_shape=jax.ShapeDtypeStruct(shape, BF),
         in_specs=[SMEM] + [ANY] * len(arrays),
-        out_specs=VMEM,
-        scratch_shapes=[pltpu.SemaphoreType.DMA((len(arrays), heads))],
+        out_specs=ANY,
+        scratch_shapes=[
+            pltpu.VMEM(shape, BF),
+            pltpu.SemaphoreType.DMA((len(arrays), heads)),
+            pltpu.SemaphoreType.DMA((heads,)),
+        ],
         compiler_params=PACK_PARAMS,
     )(order, *arrays)
 
@@ -350,24 +367,29 @@
     )(base, kb, bc, stat, q, less, more, *sums)
 
 
-def assemble_kernel(order_ref, t_ref, s_ref, out_ref):
-    rows = out_ref.shape[0]
-    pieces = t_ref.shape[0] // HT
-    for head in range(HT):
-        block = t_ref[head * pieces : (head + 1) * pieces].reshape(rows, DEPTH)
-        out_ref[:, columns_of(order_ref, head)] = block
-    for head in range(s_ref.shape[0]):
-        out_ref[:, columns_of(order_ref, HT + head)] = s_ref[head]
-
-
-def assemble(order, temporal, spatial, rows, width):
-    return pl.pallas_call(
-        assemble_kernel,
-        out_shape=jax.ShapeDtypeStruct((rows, width), BF),
-        in_specs=[SMEM, VMEM, VMEM],
-        out_specs=VMEM,
-        compiler_params=PARAMS,
-    )(order, temporal, spatial)
+def place_kernel(first, order_ref, src_ref, *refs):
+    out, sems = refs[-2:]
+    run_copies(
+        [
+            pltpu.make_async_copy(
+                src_ref.at[head], out.at[:, :, columns_of(order_ref, first + head)], sems.at[head]
+            )
+            for head in range(src_ref.shape[0])
+        ]
+    )
+
+
+def place(order, blocks, first, rows, width, before=()):
+    heads, pieces, items, _ = blocks.shape
+    return pl.pallas_call(
+        functools.partial(place_kernel, first),
+        out_shape=jax.ShapeDtypeStruct((pieces, items, width), BF),
+        in_specs=[SMEM, VMEM] + [ANY] * len(before),
+        out_specs=ANY,
+        scratch_shapes=[pltpu.SemaphoreType.DMA((heads,))],
+        input_output_aliases={2: 0} if before else {},
+        compiler_params=PARAMS if before else PACK_PARAMS,
+    )(order, blocks, *before)
 
 
 def exchange(array, axes):
@@ -403,7 +425,10 @@
     tr = exchange(to, loop_axes)
     so = attend_near(base, key_blocks, block_count, stat, q, less, more, sums, frames)
     sr = exchange(so, block_axes)
-    return assemble(head_order, tr, sr, rows, width)
+    by_head = (-1, rows // items, items, DEPTH)
+    partial = place(head_order, tr.reshape(by_head), 0, rows, width)
+    whole = place(head_order, sr.reshape(by_head), HT, rows, width, (partial,))
+    return whole.reshape(rows, width)
 
 
 def solution(mesh):

time: 136 us -> 137 us (level)
  blocking collectives: 17 us -> 0 us
  waiting for transfers between devices: 20.3 us -> 28.9 us
  Pallas kernels: 42.4 us -> 47.3 us
  starting transfers between devices: 50.1 us -> 55 us
    all_to_all x1 -> x0, blocking collectives: 17 us -> none  [exchange(): return lax.all_to_all(array, axes, 0, 0, tiled=True)]
    all_to_all x3 -> x4, waiting for transfers between devices: 11.1 us -> 18 us  [exchange(): return lax.all_to_all(array, axes, 0, 0, tiled=True)]
    all_to_all x3 -> x4, starting transfers between devices: 35.9 us -> 40.8 us  [exchange(): return lax.all_to_all(array, axes, 0, 0, tiled=True)]
    pallas_call x1, Pallas kernels: 16.9 us -> 19.3 us  [attend_own(): pl.pallas_call(functools.partial(own_kernel, frames), out_shape=[jax.Shap...]
    pallas_call x1, Pallas kernels: 15.6 us -> 17.6 us  [attend_near(): pl.pallas_call(functools.partial(near_kernel, frames), out_shape=jax.Shap...]
    ppermute x2, waiting for transfers between devices: 7.87 us -> 9.57 us  [from_block(): lax.ppermute(array, ('zh', 'core', 'yh'), [((i + by) % count, i) for i in...]
    pallas_call x2 -> x3, Pallas kernels: 5.25 us -> 6.49 us  [the longest x1 3.3 us: pack_spatial(): pl.pallas_call(pack_spatial_kernel, out_shape=jax.ShapeDtypeStruct(shape,...]
    unnamed x21 -> x25, local copies, waits for them, and re-layouts: 4.27 us -> 3.76 us
  transfers between devices with their start and end apart: 6 -> 7, of which waited for: 3 -> 4; matrix products, arithmetic and copies ran while one was open for 1% -> 1% of each run, Pallas kernels for 27% -> 31%
where the time goes in v6:
time: 137 us
  starting transfers between devices  55 us (40%)
  Pallas kernels  47.3 us (35%)
  waiting for transfers between devices  28.9 us (21%)
  local copies, waits for them, and re-layouts  5.21 us (4%)
    all_to_all x4, starting transfers between devices, exchange(): return lax.all_to_all(array, axes, 0, 0, tiled=True)  40.8 us
    pallas_call x1, Pallas kernels, attend_own(): pl.pallas_call(functools.partial(own_kernel, frames), out_shape=[jax.Shap...  19.3 us
    all_to_all x4, waiting for transfers between devices, exchange(): return lax.all_to_all(array, axes, 0, 0, tiled=True)  18 us
    pallas_call x1, Pallas kernels, attend_near(): pl.pallas_call(functools.partial(near_kernel, frames), out_shape=jax.Shap...  17.6 us
    ppermute x2, waiting for transfers between devices, from_block(): lax.ppermute(array, ('zh', 'core', 'yh'), [((i + by) % count, i) for i in...  9.57 us
    ppermute x2, starting transfers between devices, from_block(): lax.ppermute(array, ('zh', 'core', 'yh'), [((i + by) % count, i) for i in...  9.51 us
    ppermute x1, starting transfers between devices, local(): st = join(mine, lax.ppermute(other, 'core', [(0, 1), (1, 0)]))  4.72 us
    unnamed x25, local copies, waits for them, and re-layouts  3.76 us
  transfers between devices with their start and end apart: 7, of which 4 were waited for; matrix products, arithmetic and copies ran while one was open for 1% of the time, Pallas kernels for 31%

profile of v6, /device:TPU:1, one launch (start us, length us, event | category | flops | bytes accessed | tf_op | source)
XLA Modules:
  0.0 136.7 jit_solution(16375372011213699221)
XLA Ops:
  0.0 3.3 %shard_map.64 = bf16[16,3,128,128]{3,2,1,0:T(8,128)(2,1)} custom-call(s32[24]{0:T(128)} %order_ref.7, bf16[128,3072]{1,0:T(8,128)(2,1)} %q_ref.1, bf16[128,3072]{1,0:T(8,128)(2,1)} %k_ref.1, bf16[128,3072]{1,0:T(8,128)(2,1)} %v_ref.1), custom_call_target="tpu_custom_call" | custom-call | tf_op jit(solution)/shard_map/pallas_call | solution.py:70
  3.3 0.0 copy-start
  3.3 0.0 copy-start.1
  3.3 0.0 copy-start.8
  3.3 7.9 %all-to-all-start = ((bf16[16,3,128,128]{3,2,1,0:T(8,128)(2,1)}), bf16[16,3,128,128]{3,2,1,0:T(8,128)(2,1)S(1)}, u32[]{:S(2)}, u32[]{:S(2)}) async-start(bf16[16,3,128,128]{3,2,1,0:T(8,128)(2,1)} %shard_map.64), calls=%async_computation | async-start | bytes 3145728 | tf_op jit(solution)/shard_map/all_to_all | solution.py:396
  11.3 0.0 copy-done
  11.3 0.0 copy-done.1
  11.3 0.0 copy-done.8
  11.3 0.0 copy-start.2
  11.3 1.1 copy-done.2
  12.4 0.7 shard_map.65
  13.2 4.7 %collective-permute-start = (bf16[64,3,8,128]{3,2,1,0:T(8,128)(2,1)S(1)}, bf16[64,3,8,128]{3,2,1,0:T(8,128)(2,1)S(1)}, u32[]{:S(2)}, u32[]{:S(2)}) collective-permute-start(bf16[64,3,8,128]{3,2,1,0:T(8,128)(2,1)S(1)} %get-tuple-element.16), channel_id=1, source_target_pairs={{0,64},{64,0},{1,65},{65,1},{2,66},{66,2},{3,67},{67,3},{4,68},{68... | collective-permute-start | bytes 1179656 | tf_op jit(solution)/shard_map/ppermute | solution.py:416
  17.9 1.3 collective-permute-done.b_ref
  19.3 0.0 copy-start.11
  19.3 0.9 shard_map.66
  20.2 11.1 %all-to-all-done.in_ref = bf16[16,3,128,128]{3,2,1,0:T(8,128)(2,1)S(1)} async-done(((bf16[16,3,128,128]{3,2,1,0:T(8,128)(2,1)}), bf16[16,3,128,128]{3,2,1,0:T(8,128)(2,1)S(1)}, u32[]{:S(2)}, u32[]{:S(2)}) %all-to-all-start) | async-done | bytes 1572896 | tf_op jit(solution)/shard_map/all_to_all | solution.py:396
  31.3 15.7 %all-to-all-start.1 = ((bf16[64,2,3,8,128]{4,3,2,1,0:T(8,128)(2,1)}), bf16[64,2,3,8,128]{4,3,2,1,0:T(8,128)(2,1)S(1)}, u32[]{:S(2)}, u32[]{:S(2)}) async-start(bf16[64,2,3,8,128]{4,3,2,1,0:T(8,128)(2,1)} %shard_map.66), calls=%async_computation.1 | async-start | bytes 1572864 | tf_op jit(solution)/shard_map/all_to_all | solution.py:396
  47.0 0.0 copy-done.11
  47.1 0.1 copy.9.kb_ref
  47.2 0.0 copy-start.10
  47.2 1.5 %fusion = (bf16[12,2,128,128]{3,2,1,0:T(8,128)(2,1)}, bf16[12,2,128,128]{3,2,1,0:T(8,128)(2,1)}) fusion(bf16[16,3,128,128]{3,2,1,0:T(8,128)(2,1)S(1)} %all-to-all-done.in_ref), kind=kLoop, calls=%fused_computation | loop fusion | bytes 3145728 | tf_op jit(solution)/shard_map/slice | solution.py:420
  48.6 7.6 %collective-permute-start.2 = (bf16[12,2,128,128]{3,2,1,0:T(8,128)(2,1)}, bf16[12,2,128,128]{3,2,1,0:T(8,128)(2,1)}, u32[]{:S(2)}, u32[]{:S(2)}) collective-permute-start(bf16[12,2,128,128]{3,2,1,0:T(8,128)(2,1)} %get-tuple-element.25), channel_id=1, source_target_pairs={{16,0},{32,16},{48,32},{64,48},{80,64},{96,80},{112,96},{128,112},... | collective-permute-start | bytes 2359304 | tf_op jit(solution)/shard_map/ppermute | solution.py:401
  56.2 1.9 %collective-permute-start.1 = (bf16[12,2,128,128]{3,2,1,0:T(8,128)(2,1)}, bf16[12,2,128,128]{3,2,1,0:T(8,128)(2,1)}, u32[]{:S(2)}, u32[]{:S(2)}) collective-permute-start(bf16[12,2,128,128]{3,2,1,0:T(8,128)(2,1)} %get-tuple-element.26), channel_id=1, source_target_pairs={{496,0},{0,16},{16,32},{32,48},{48,64},{64,80},{80,96},{96,112},{1... | collective-permute-start | bytes 2359304 | tf_op jit(solution)/shard_map/ppermute | solution.py:401
  58.2 0.0 copy-done.10
  58.2 19.3 %shard_map.68 = (f32[4,512,128]{2,1,0:T(8,128)S(1)}, f32[4,512,128]{2,1,0:T(8,128)S(1)}, bf16[16,1,128,128]{3,2,1,0:T(8,128)(2,1)S(1)}, f32[2]{0:T(128)S(1)}) custom-call(s32[1]{0:T(128)} %bitcast.base_ref, s32[128,6]{1,0:T(8,128)S(1)} %copy.9.kb_ref, s32[128]{0:T(128)S(1)} %copy-done.10, bf16[16,3,128,128]{3,2,1,0:T(8,128)(2,1)S(1)} %all-to-all-done.in_ref), custom_call_target="tpu_custom_call" | custom-call | flops 10000000000 | bytes 1048576 | tf_op jit(solution)/shard_map/pallas_call | solution.py:336
  77.5 0.0 copy-start.3
  77.5 1.0 copy-done.3
  78.5 0.0 copy-start.5
  78.5 0.8 copy-done.5
  79.3 0.0 all-to-all-done.1.in_ref
  79.3 0.0 copy-start.4
  79.3 0.0 copy-start.6
  79.3 2.1 %shard_map.67 = bf16[128,8,128]{2,1,0:T(8,128)(2,1)S(1)} custom-call(s32[1]{0:T(128)} %bitcast.1.core_ref, bf16[64,2,3,8,128]{4,3,2,1,0:T(8,128)(2,1)S(1)} %all-to-all-done.1.in_ref), custom_call_target="tpu_custom_call" | custom-call | flops 49999998976 | bytes 1048576 | tf_op jit(solution)/shard_map/pallas_call | solution.py:145
  81.5 0.0 copy-start.7
  81.5 0.7 copy-done.7
  82.1 9.1 %all-to-all-start.3 = ((bf16[128,8,128]{2,1,0:T(8,128)(2,1)}), bf16[128,8,128]{2,1,0:T(8,128)(2,1)}, u32[]{:S(2)}, u32[]{:S(2)}) async-start(bf16[128,8,128]{2,1,0:T(8,128)(2,1)} %copy-done.7), calls=%async_computation.3 | async-start | bytes 524288 | tf_op jit(solution)/shard_map/all_to_all | solution.py:396
  91.2 9.6 %collective-permute-done.2.more_ref = bf16[12,2,128,128]{3,2,1,0:T(8,128)(2,1)} collective-permute-done((bf16[12,2,128,128]{3,2,1,0:T(8,128)(2,1)}, bf16[12,2,128,128]{3,2,1,0:T(8,128)(2,1)}, u32[]{:S(2)}, u32[]{:S(2)}) %collective-permute-start.2) | collective-permute-done | bytes 786464 | tf_op jit(solution)/shard_map/ppermute | solution.py:401
  100.8 0.0 collective-permute-done.1.less_ref
  100.8 0.0 copy-done.4
  100.8 0.0 copy-done.6
  100.8 17.6 %shard_map.69 = bf16[16,128,128]{2,1,0:T(8,128)(2,1)} custom-call(s32[1]{0:T(128)} %bitcast.base_ref, s32[128,6]{1,0:T(8,128)S(1)} %copy.9.kb_ref, s32[128]{0:T(128)S(1)} %copy-done.10, f32[2]{0:T(128)S(1)} %get-tuple-element.20.stat_ref, bf16[16,1,128,128]{3,2,1,0:T(8,128)(2,1)S(1)} %copy-done.6, bf16[12,2,128,128]{3,2,1,0:T(8,128)(2,1)} %collective-permute-done.1.less_ref, ...), custom_call_target="tpu_custom_call" | custom-call | tf_op jit(solution)/shard_map/pallas_call | solution.py:355
  118.4 0.0 copy-start.9
  118.4 0.0 all-to-all-done.3
  118.4 8.1 %all-to-all-start.2 = ((bf16[16,128,128]{2,1,0:T(8,128)(2,1)}), bf16[16,128,128]{2,1,0:T(8,128)(2,1)S(1)}, u32[]{:S(2)}, u32[]{:S(2)}) async-start(bf16[16,128,128]{2,1,0:T(8,128)(2,1)} %shard_map.69), calls=%async_computation.2 | async-start | bytes 1048576 | tf_op jit(solution)/shard_map/all_to_all | solution.py:396
  126.6 1.7 %shard_map.70.refs_0_ = bf16[16,8,3072]{2,1,0:T(8,128)(2,1)} custom-call(s32[24]{0:T(128)} %order_ref.7, bf16[8,16,8,128]{3,2,1,0:T(8,128)(2,1)} %bitcast.3.src_ref), custom_call_target="tpu_custom_call" | custom-call | tf_op jit(solution)/shard_map/pallas_call | solution.py:384
  128.3 6.9 %all-to-all-done.2 = bf16[16,128,128]{2,1,0:T(8,128)(2,1)S(1)} async-done(((bf16[16,128,128]{2,1,0:T(8,128)(2,1)}), bf16[16,128,128]{2,1,0:T(8,128)(2,1)S(1)}, u32[]{:S(2)}, u32[]{:S(2)}) %all-to-all-start.2) | async-done | bytes 524320 | tf_op jit(solution)/shard_map/all_to_all | solution.py:396
  135.2 0.0 copy-done.9
  135.2 1.5 %shard_map.71 = bf16[16,8,3072]{2,1,0:T(8,128)(2,1)} custom-call(s32[24]{0:T(128)S(1)} %copy-done.9, bf16[16,16,8,128]{3,2,1,0:T(8,128)(2,1)S(1)} %bitcast.5, bf16[16,8,3072]{2,1,0:T(8,128)(2,1)} %shard_map.70.refs_0_), custom_call_target="tpu_custom_call", output_to_operand_aliasing={{}: (2, {})} | custom-call | tf_op jit(solution)/shard_map/pallas_call | solution.py:384
Async XLA Ops:
  3.3 8.0 %copy-start = (bf16[128,3072]{1,0:T(8,128)(2,1)S(1)}, bf16[128,3072]{1,0:T(8,128)(2,1)}, u32[]{:S(2)}) copy-start(bf16[128,3072]{1,0:T(8,128)(2,1)} %q_ref.1) | copy-start | bytes 2359300
  3.3 8.0 %copy-start.1 = (bf16[128,3072]{1,0:T(8,128)(2,1)S(1)}, bf16[128,3072]{1,0:T(8,128)(2,1)}, u32[]{:S(2)}) copy-start(bf16[128,3072]{1,0:T(8,128)(2,1)} %k_ref.1) | copy-start | bytes 2359300
  3.3 8.0 %copy-start.8 = (s32[24]{0:T(128)S(1)}, s32[24]{0:T(128)}, u32[]{:S(2)}) copy-start(s32[24]{0:T(128)} %order_ref.7) | copy-start | bytes 292
  3.3 28.0 %all-to-all-start = ((bf16[16,3,128,128]{3,2,1,0:T(8,128)(2,1)}), bf16[16,3,128,128]{3,2,1,0:T(8,128)(2,1)S(1)}, u32[]{:S(2)}, u32[]{:S(2)}) async-start(bf16[16,3,128,128]{3,2,1,0:T(8,128)(2,1)} %shard_map.64), calls=%async_computation | async-start | bytes 3145728 | tf_op jit(solution)/shard_map/all_to_all | solution.py:396
  11.3 1.1 copy-start.2
  13.2 6.1 %collective-permute-start = (bf16[64,3,8,128]{3,2,1,0:T(8,128)(2,1)S(1)}, bf16[64,3,8,128]{3,2,1,0:T(8,128)(2,1)S(1)}, u32[]{:S(2)}, u32[]{:S(2)}) collective-permute-start(bf16[64,3,8,128]{3,2,1,0:T(8,128)(2,1)S(1)} %get-tuple-element.16), channel_id=1, source_target_pairs={{0,64},{64,0},{1,65},{65,1},{2,66},{66,2},{3,67},{67,3},{4,68},{68... | collective-permute-start | bytes 1179656 | tf_op jit(solution)/shard_map/ppermute | solution.py:416
  19.3 27.8 %copy-start.11 = (s32[128,6]{0,1:T(8,128)S(1)}, s32[128,6]{0,1:T(8,128)}, u32[]{:S(2)}) copy-start(s32[128,6]{0,1:T(8,128)} %param.10) | copy-start | bytes 9220
  31.3 48.0 %all-to-all-start.1 = ((bf16[64,2,3,8,128]{4,3,2,1,0:T(8,128)(2,1)}), bf16[64,2,3,8,128]{4,3,2,1,0:T(8,128)(2,1)S(1)}, u32[]{:S(2)}, u32[]{:S(2)}) async-start(bf16[64,2,3,8,128]{4,3,2,1,0:T(8,128)(2,1)} %shard_map.66), calls=%async_computation.1 | async-start | bytes 1572864 | tf_op jit(solution)/shard_map/all_to_all | solution.py:396
  47.2 11.0 %copy-start.10 = (s32[128]{0:T(128)S(1)}, s32[128]{0:T(128)}, u32[]{:S(2)}) copy-start(s32[128]{0:T(128)} %bc_ref.3) | copy-start | bytes 1540
  48.6 52.2 %collective-permute-start.2 = (bf16[12,2,128,128]{3,2,1,0:T(8,128)(2,1)}, bf16[12,2,128,128]{3,2,1,0:T(8,128)(2,1)}, u32[]{:S(2)}, u32[]{:S(2)}) collective-permute-start(bf16[12,2,128,128]{3,2,1,0:T(8,128)(2,1)} %get-tuple-element.25), channel_id=1, source_target_pairs={{16,0},{32,16},{48,32},{64,48},{80,64},{96,80},{112,96},{128,112},... | collective-permute-start | bytes 2359304 | tf_op jit(solution)/shard_map/ppermute | solution.py:401
  56.2 44.6 %collective-permute-start.1 = (bf16[12,2,128,128]{3,2,1,0:T(8,128)(2,1)}, bf16[12,2,128,128]{3,2,1,0:T(8,128)(2,1)}, u32[]{:S(2)}, u32[]{:S(2)}) collective-permute-start(bf16[12,2,128,128]{3,2,1,0:T(8,128)(2,1)} %get-tuple-element.26), channel_id=1, source_target_pairs={{496,0},{0,16},{16,32},{32,48},{48,64},{64,80},{80,96},{96,112},{1... | collective-permute-start | bytes 2359304 | tf_op jit(solution)/shard_map/ppermute | solution.py:401
  77.5 1.0 copy-start.3
  78.5 0.8 copy-start.5
  79.3 21.5 %copy-start.4 = (f32[4,512,128]{2,1,0:T(8,128)S(1)}, f32[4,512,128]{2,1,0:T(8,128)}, u32[]{:S(2)}) copy-start(f32[4,512,128]{2,1,0:T(8,128)} %copy-done.3) | copy-start | bytes 3145732
  79.3 21.5 %copy-start.6 = (bf16[16,1,128,128]{3,2,1,0:T(8,128)(2,1)S(1)}, bf16[16,1,128,128]{3,2,1,0:T(8,128)(2,1)}, u32[]{:S(2)}) copy-start(bf16[16,1,128,128]{3,2,1,0:T(8,128)(2,1)} %copy-done.5) | copy-start | bytes 1572868
  81.5 0.7 copy-start.7
  82.1 36.3 %all-to-all-start.3 = ((bf16[128,8,128]{2,1,0:T(8,128)(2,1)}), bf16[128,8,128]{2,1,0:T(8,128)(2,1)}, u32[]{:S(2)}, u32[]{:S(2)}) async-start(bf16[128,8,128]{2,1,0:T(8,128)(2,1)} %copy-done.7), calls=%async_computation.3 | async-start | bytes 524288 | tf_op jit(solution)/shard_map/all_to_all | solution.py:396
  118.4 16.8 %copy-start.9 = (s32[24]{0:T(128)S(1)}, s32[24]{0:T(128)}, u32[]{:S(2)}) copy-start(s32[24]{0:T(128)} %order_ref.7) | copy-start | bytes 292
  118.4 16.8 %all-to-all-start.2 = ((bf16[16,128,128]{2,1,0:T(8,128)(2,1)}), bf16[16,128,128]{2,1,0:T(8,128)(2,1)S(1)}, u32[]{:S(2)}, u32[]{:S(2)}) async-start(bf16[16,128,128]{2,1,0:T(8,128)(2,1)} %shard_map.69), calls=%async_computation.2 | async-start | bytes 1048576 | tf_op jit(solution)/shard_map/all_to_all | solution.py:396

commit v7 on v6

--- a/solution.py
+++ b/solution.py
@@ -267,21 +267,30 @@
 
 def near_kernel(
     frames, base_ref, kb_ref, bc_ref, stat_ref, q_ref, less_ref, more_ref, acc_in, side_in, o_ref,
-    acc_ref, m_ref, near_ref, sems
+    acc_ref, m_ref, near_ref, held_ref, sems, held_sems
 ):
     pieces = q_ref.shape[0] // BLOCK
     rows = q_ref.shape[2]
     size = pieces * rows
     base = base_ref[0]
-    run_copies(
-        [
-            pltpu.make_async_copy(less_ref, near_ref.at[pl.ds(0, W * pieces)], sems.at[0]),
-            pltpu.make_async_copy(more_ref, near_ref.at[pl.ds(W * pieces, W * pieces)], sems.at[1]),
-        ]
-    )
+    arriving = [
+        pltpu.make_async_copy(src, near_ref.at[pl.ds(at * W * pieces, W * pieces)], sems.at[at])
+        for at, src in enumerate((less_ref, more_ref))
+    ]
+    holding = [
+        pltpu.make_async_copy(src, held_ref.at[:, :, pl.ds(at * LANES, LANES)], held_sems.at[at])
+        for at, src in enumerate((acc_in, side_in))
+    ]
+    for copy in arriving + holding:
+        copy.start()
     part = functools.partial(frame_at, near_ref, pieces=pieces)
-    k_norm = row_norm([part(0, at) for at in range(2 * W)])
+    arriving[0].wait()
+    less_norm = row_norm([part(0, at) for at in range(W)])
+    arriving[1].wait()
+    k_norm = jnp.maximum(less_norm, row_norm([part(0, at) for at in range(W, 2 * W)]))
     fast = small_scores(stat_ref[0], k_norm) & (stat_ref[1] > 0.5)
+    for copy in holding:
+        copy.wait()
 
     def query(mine):
         return frame_at(q_ref, 0, mine, pieces)
@@ -300,8 +309,7 @@
             pairs = [
                 (part(0, mine + j), part(1, mine + j), used(mine, mine + j)) for j in range(W)
             ]
-            acc = jnp.concatenate([acc_in[mine], side_in[mine]], axis=1)
-            finish(mine, add_frames(acc, query(mine), pairs))
+            finish(mine, add_frames(held_ref[mine], query(mine), pairs))
             return carry
 
         lax.fori_loop(0, BLOCK, frame, 0)
@@ -309,11 +317,11 @@
     @pl.when(jnp.logical_not(fast))
     def _():
         def frame(mine, carry):
-            side = side_in[mine]
+            side = held_ref[mine, :, LANES:]
             quick = jnp.full((size, LANES), stat_ref[1], F32) > 0.5
             top = jnp.broadcast_to(side[:, LANES - 1 :], (size, LANES))
             m_ref[...] = jnp.where(quick, 0.0, top)
-            acc_ref[:, :DEPTH] = acc_in[mine]
+            acc_ref[:, :DEPTH] = held_ref[mine, :, :LANES]
             acc_ref[:, DEPTH:] = jnp.broadcast_to(side[:, :1], (size, LANES))
 
             def pair(j, inner):
@@ -355,12 +363,14 @@
     return pl.pallas_call(
         functools.partial(near_kernel, frames),
         out_shape=jax.ShapeDtypeStruct((dests, rows, depth), BF),
-        in_specs=[SMEM] * 4 + [VMEM, ANY, ANY, VMEM, VMEM],
+        in_specs=[SMEM] * 4 + [VMEM] + [ANY] * 4,
         out_specs=VMEM,
         scratch_shapes=[
             pltpu.VMEM((size, 2 * depth), F32),
             pltpu.VMEM((size, LANES), F32),
             pltpu.VMEM((2 * less.shape[0], *less.shape[1:]), BF),
+            pltpu.VMEM((BLOCK, size, 2 * LANES), F32),
+            pltpu.SemaphoreType.DMA((2,)),
             pltpu.SemaphoreType.DMA((2,)),
         ],
         compiler_params=PARAMS,

time: 137 us -> 135 us (0.985); the launches traced: 137 us -> 133 us
  waiting for transfers between devices: 28.9 us -> 21.8 us
  starting transfers between devices: 55 us -> 61.9 us
  Pallas kernels: 47.3 us -> 43.7 us
    ppermute x2, waiting for transfers between devices: 9.57 us -> 2.45 us  [from_block(): lax.ppermute(array, ('zh', 'core', 'yh'), [((i + by) % count, i) for i in...]
    all_to_all x4, starting transfers between devices: 40.8 us -> 47.7 us  [exchange(): return lax.all_to_all(array, axes, 0, 0, tiled=True)]
    pallas_call x1, Pallas kernels: 17.6 us -> 15.3 us  [attend_near(): pl.pallas_call(functools.partial(near_kernel, frames), out_shape=jax.Shap...]
  transfers between devices with their start and end apart: 7 -> 7, of which waited for: 4 -> 4; matrix products, arithmetic and copies ran while one was open for 1% -> 1% of each run, Pallas kernels for 31% -> 29%
where the time goes in v7:
time: 135 us; the launch traced here: 133 us
  starting transfers between devices  61.9 us (46%)
  Pallas kernels  43.7 us (32%)
  waiting for transfers between devices  21.8 us (16%)
  local copies, waits for them, and re-layouts  5.21 us (4%)
    all_to_all x4, starting transfers between devices, exchange(): return lax.all_to_all(array, axes, 0, 0, tiled=True)  47.7 us
    pallas_call x1, Pallas kernels, attend_own(): pl.pallas_call(functools.partial(own_kernel, frames), out_shape=[jax.Shap...  18.1 us
    all_to_all x4, waiting for transfers between devices, exchange(): return lax.all_to_all(array, axes, 0, 0, tiled=True)  18 us
    pallas_call x1, Pallas kernels, attend_near(): pl.pallas_call(functools.partial(near_kernel, frames), out_shape=jax.Shap...  15.3 us
    ppermute x2, starting transfers between devices, from_block(): lax.ppermute(array, ('zh', 'core', 'yh'), [((i + by) % count, i) for i in...  9.51 us
    ppermute x1, starting transfers between devices, local(): st = join(mine, lax.ppermute(other, 'core', [(0, 1), (1, 0)]))  4.72 us
    unnamed x25, local copies, waits for them, and re-layouts  3.76 us
    pallas_call x1, Pallas kernels, pack_spatial(): pl.pallas_call(pack_spatial_kernel, out_shape=jax.ShapeDtypeStruct(shape,...  3.3 us
  transfers between devices with their start and end apart: 7, of which 4 were waited for; matrix products, arithmetic and copies ran while one was open for 1% of the time, Pallas kernels for 29%

profile of v7, /device:TPU:1, one launch (start us, length us, event | category | flops | bytes accessed | tf_op | source)
XLA Modules:
  0.0 133.0 jit_solution(2590757979896350224)
XLA Ops:
  0.0 3.3 %shard_map.64 = bf16[16,3,128,128]{3,2,1,0:T(8,128)(2,1)} custom-call(s32[24]{0:T(128)} %order_ref.7, bf16[128,3072]{1,0:T(8,128)(2,1)} %q_ref.1, bf16[128,3072]{1,0:T(8,128)(2,1)} %k_ref.1, bf16[128,3072]{1,0:T(8,128)(2,1)} %v_ref.1), custom_call_target="tpu_custom_call" | custom-call | tf_op jit(solution)/shard_map/pallas_call | solution.py:70
  3.3 0.0 copy-start
  3.3 0.0 copy-start.1
  3.3 0.0 copy-start.8
  3.3 7.9 %all-to-all-start = ((bf16[16,3,128,128]{3,2,1,0:T(8,128)(2,1)}), bf16[16,3,128,128]{3,2,1,0:T(8,128)(2,1)S(1)}, u32[]{:S(2)}, u32[]{:S(2)}) async-start(bf16[16,3,128,128]{3,2,1,0:T(8,128)(2,1)} %shard_map.64), calls=%async_computation | async-start | bytes 3145728 | tf_op jit(solution)/shard_map/all_to_all | solution.py:406
  11.3 0.0 copy-done
  11.3 0.0 copy-done.1
  11.3 0.0 copy-done.8
  11.3 0.0 copy-start.2
  11.3 1.1 copy-done.2
  12.4 0.7 shard_map.65
  13.2 4.7 %collective-permute-start = (bf16[64,3,8,128]{3,2,1,0:T(8,128)(2,1)S(1)}, bf16[64,3,8,128]{3,2,1,0:T(8,128)(2,1)S(1)}, u32[]{:S(2)}, u32[]{:S(2)}) collective-permute-start(bf16[64,3,8,128]{3,2,1,0:T(8,128)(2,1)S(1)} %get-tuple-element.16), channel_id=1, source_target_pairs={{0,64},{64,0},{1,65},{65,1},{2,66},{66,2},{3,67},{67,3},{4,68},{68... | collective-permute-start | bytes 1179656 | tf_op jit(solution)/shard_map/ppermute | solution.py:426
  17.9 1.3 collective-permute-done.b_ref
  19.3 0.0 copy-start.11
  19.3 0.9 shard_map.66
  20.2 11.1 %all-to-all-done.in_ref = bf16[16,3,128,128]{3,2,1,0:T(8,128)(2,1)S(1)} async-done(((bf16[16,3,128,128]{3,2,1,0:T(8,128)(2,1)}), bf16[16,3,128,128]{3,2,1,0:T(8,128)(2,1)S(1)}, u32[]{:S(2)}, u32[]{:S(2)}) %all-to-all-start) | async-done | bytes 1572896 | tf_op jit(solution)/shard_map/all_to_all | solution.py:406
  31.3 15.7 %all-to-all-start.1 = ((bf16[64,2,3,8,128]{4,3,2,1,0:T(8,128)(2,1)}), bf16[64,2,3,8,128]{4,3,2,1,0:T(8,128)(2,1)S(1)}, u32[]{:S(2)}, u32[]{:S(2)}) async-start(bf16[64,2,3,8,128]{4,3,2,1,0:T(8,128)(2,1)} %shard_map.66), calls=%async_computation.1 | async-start | bytes 1572864 | tf_op jit(solution)/shard_map/all_to_all | solution.py:406
  47.0 0.0 copy-done.11
  47.1 0.1 copy.9.kb_ref
  47.2 0.0 copy-start.10
  47.2 1.5 %fusion = (bf16[12,2,128,128]{3,2,1,0:T(8,128)(2,1)}, bf16[12,2,128,128]{3,2,1,0:T(8,128)(2,1)}) fusion(bf16[16,3,128,128]{3,2,1,0:T(8,128)(2,1)S(1)} %all-to-all-done.in_ref), kind=kLoop, calls=%fused_computation | loop fusion | bytes 3145728 | tf_op jit(solution)/shard_map/slice | solution.py:430
  48.6 7.6 %collective-permute-start.2 = (bf16[12,2,128,128]{3,2,1,0:T(8,128)(2,1)}, bf16[12,2,128,128]{3,2,1,0:T(8,128)(2,1)}, u32[]{:S(2)}, u32[]{:S(2)}) collective-permute-start(bf16[12,2,128,128]{3,2,1,0:T(8,128)(2,1)} %get-tuple-element.25), channel_id=1, source_target_pairs={{16,0},{32,16},{48,32},{64,48},{80,64},{96,80},{112,96},{128,112},... | collective-permute-start | bytes 2359304 | tf_op jit(solution)/shard_map/ppermute | solution.py:411
  56.2 1.9 %collective-permute-start.1 = (bf16[12,2,128,128]{3,2,1,0:T(8,128)(2,1)}, bf16[12,2,128,128]{3,2,1,0:T(8,128)(2,1)}, u32[]{:S(2)}, u32[]{:S(2)}) collective-permute-start(bf16[12,2,128,128]{3,2,1,0:T(8,128)(2,1)} %get-tuple-element.26), channel_id=1, source_target_pairs={{496,0},{0,16},{16,32},{32,48},{48,64},{64,80},{80,96},{96,112},{1... | collective-permute-start | bytes 2359304 | tf_op jit(solution)/shard_map/ppermute | solution.py:411
  58.2 0.0 copy-done.10
  58.2 18.1 %shard_map.68 = (f32[4,512,128]{2,1,0:T(8,128)S(1)}, f32[4,512,128]{2,1,0:T(8,128)S(1)}, bf16[16,1,128,128]{3,2,1,0:T(8,128)(2,1)S(1)}, f32[2]{0:T(128)S(1)}) custom-call(s32[1]{0:T(128)} %bitcast.base_ref, s32[128,6]{1,0:T(8,128)S(1)} %copy.9.kb_ref, s32[128]{0:T(128)S(1)} %copy-done.10, bf16[16,3,128,128]{3,2,1,0:T(8,128)(2,1)S(1)} %all-to-all-done.in_ref), custom_call_target="tpu_custom_call" | custom-call | flops 10000000000 | bytes 1048576 | tf_op jit(solution)/shard_map/pallas_call | solution.py:344
  76.3 0.0 copy-start.3
  76.3 1.0 copy-done.3
  77.3 0.0 copy-start.5
  77.3 0.8 copy-done.5
  78.1 0.0 all-to-all-done.1.in_ref
  78.1 0.0 copy-start.4
  78.1 0.0 copy-start.6
  78.1 2.1 %shard_map.67 = bf16[128,8,128]{2,1,0:T(8,128)(2,1)S(1)} custom-call(s32[1]{0:T(128)} %bitcast.1.core_ref, bf16[64,2,3,8,128]{4,3,2,1,0:T(8,128)(2,1)S(1)} %all-to-all-done.1.in_ref), custom_call_target="tpu_custom_call" | custom-call | flops 49999998976 | bytes 1048576 | tf_op jit(solution)/shard_map/pallas_call | solution.py:145
  80.3 0.0 copy-start.7
  80.3 0.7 copy-done.7
  81.0 15.9 %all-to-all-start.3 = ((bf16[128,8,128]{2,1,0:T(8,128)(2,1)}), bf16[128,8,128]{2,1,0:T(8,128)(2,1)}, u32[]{:S(2)}, u32[]{:S(2)}) async-start(bf16[128,8,128]{2,1,0:T(8,128)(2,1)} %copy-done.7), calls=%async_computation.3 | async-start | bytes 524288 | tf_op jit(solution)/shard_map/all_to_all | solution.py:406
  96.9 2.5 %collective-permute-done.2.more_ref = bf16[12,2,128,128]{3,2,1,0:T(8,128)(2,1)} collective-permute-done((bf16[12,2,128,128]{3,2,1,0:T(8,128)(2,1)}, bf16[12,2,128,128]{3,2,1,0:T(8,128)(2,1)}, u32[]{:S(2)}, u32[]{:S(2)}) %collective-permute-start.2) | collective-permute-done | bytes 786464 | tf_op jit(solution)/shard_map/ppermute | solution.py:411
  99.3 0.0 collective-permute-done.1.less_ref
  99.3 0.0 copy-done.4
  99.3 0.0 copy-done.6
  99.3 15.3 %shard_map.69 = bf16[16,128,128]{2,1,0:T(8,128)(2,1)} custom-call(s32[1]{0:T(128)} %bitcast.base_ref, s32[128,6]{1,0:T(8,128)S(1)} %copy.9.kb_ref, s32[128]{0:T(128)S(1)} %copy-done.10, f32[2]{0:T(128)S(1)} %get-tuple-element.20.stat_ref, bf16[16,1,128,128]{3,2,1,0:T(8,128)(2,1)S(1)} %copy-done.6, bf16[12,2,128,128]{3,2,1,0:T(8,128)(2,1)} %collective-permute-done.1.less_ref, ...), custom_call_target="tpu_custom_call" | custom-call | tf_op jit(solution)/shard_map/pallas_call | solution.py:363
  114.6 0.0 copy-start.9
  114.6 0.0 all-to-all-done.3
  114.7 8.2 %all-to-all-start.2 = ((bf16[16,128,128]{2,1,0:T(8,128)(2,1)}), bf16[16,128,128]{2,1,0:T(8,128)(2,1)S(1)}, u32[]{:S(2)}, u32[]{:S(2)}) async-start(bf16[16,128,128]{2,1,0:T(8,128)(2,1)} %shard_map.69), calls=%async_computation.2 | async-start | bytes 1048576 | tf_op jit(solution)/shard_map/all_to_all | solution.py:406
  122.9 1.7 %shard_map.70.refs_0_ = bf16[16,8,3072]{2,1,0:T(8,128)(2,1)} custom-call(s32[24]{0:T(128)} %order_ref.7, bf16[8,16,8,128]{3,2,1,0:T(8,128)(2,1)} %bitcast.3.src_ref), custom_call_target="tpu_custom_call" | custom-call | tf_op jit(solution)/shard_map/pallas_call | solution.py:394
  124.6 6.9 %all-to-all-done.2 = bf16[16,128,128]{2,1,0:T(8,128)(2,1)S(1)} async-done(((bf16[16,128,128]{2,1,0:T(8,128)(2,1)}), bf16[16,128,128]{2,1,0:T(8,128)(2,1)S(1)}, u32[]{:S(2)}, u32[]{:S(2)}) %all-to-all-start.2) | async-done | bytes 524320 | tf_op jit(solution)/shard_map/all_to_all | solution.py:406
  131.5 0.0 copy-done.9
  131.5 1.5 %shard_map.71 = bf16[16,8,3072]{2,1,0:T(8,128)(2,1)} custom-call(s32[24]{0:T(128)S(1)} %copy-done.9, bf16[16,16,8,128]{3,2,1,0:T(8,128)(2,1)S(1)} %bitcast.5, bf16[16,8,3072]{2,1,0:T(8,128)(2,1)} %shard_map.70.refs_0_), custom_call_target="tpu_custom_call", output_to_operand_aliasing={{}: (2, {})} | custom-call | tf_op jit(solution)/shard_map/pallas_call | solution.py:394
Async XLA Ops:
  3.3 8.0 %copy-start = (bf16[128,3072]{1,0:T(8,128)(2,1)S(1)}, bf16[128,3072]{1,0:T(8,128)(2,1)}, u32[]{:S(2)}) copy-start(bf16[128,3072]{1,0:T(8,128)(2,1)} %q_ref.1) | copy-start | bytes 2359300
  3.3 8.0 %copy-start.1 = (bf16[128,3072]{1,0:T(8,128)(2,1)S(1)}, bf16[128,3072]{1,0:T(8,128)(2,1)}, u32[]{:S(2)}) copy-start(bf16[128,3072]{1,0:T(8,128)(2,1)} %k_ref.1) | copy-start | bytes 2359300
  3.3 8.0 %copy-start.8 = (s32[24]{0:T(128)S(1)}, s32[24]{0:T(128)}, u32[]{:S(2)}) copy-start(s32[24]{0:T(128)} %order_ref.7) | copy-start | bytes 292
  3.3 28.0 %all-to-all-start = ((bf16[16,3,128,128]{3,2,1,0:T(8,128)(2,1)}), bf16[16,3,128,128]{3,2,1,0:T(8,128)(2,1)S(1)}, u32[]{:S(2)}, u32[]{:S(2)}) async-start(bf16[16,3,128,128]{3,2,1,0:T(8,128)(2,1)} %shard_map.64), calls=%async_computation | async-start | bytes 3145728 | tf_op jit(solution)/shard_map/all_to_all | solution.py:406
  11.3 1.1 copy-start.2
  13.2 6.1 %collective-permute-start = (bf16[64,3,8,128]{3,2,1,0:T(8,128)(2,1)S(1)}, bf16[64,3,8,128]{3,2,1,0:T(8,128)(2,1)S(1)}, u32[]{:S(2)}, u32[]{:S(2)}) collective-permute-start(bf16[64,3,8,128]{3,2,1,0:T(8,128)(2,1)S(1)} %get-tuple-element.16), channel_id=1, source_target_pairs={{0,64},{64,0},{1,65},{65,1},{2,66},{66,2},{3,67},{67,3},{4,68},{68... | collective-permute-start | bytes 1179656 | tf_op jit(solution)/shard_map/ppermute | solution.py:426
  19.3 27.8 %copy-start.11 = (s32[128,6]{0,1:T(8,128)S(1)}, s32[128,6]{0,1:T(8,128)}, u32[]{:S(2)}) copy-start(s32[128,6]{0,1:T(8,128)} %param.10) | copy-start | bytes 9220
  31.3 46.8 %all-to-all-start.1 = ((bf16[64,2,3,8,128]{4,3,2,1,0:T(8,128)(2,1)}), bf16[64,2,3,8,128]{4,3,2,1,0:T(8,128)(2,1)S(1)}, u32[]{:S(2)}, u32[]{:S(2)}) async-start(bf16[64,2,3,8,128]{4,3,2,1,0:T(8,128)(2,1)} %shard_map.66), calls=%async_computation.1 | async-start | bytes 1572864 | tf_op jit(solution)/shard_map/all_to_all | solution.py:406
  47.2 11.0 %copy-start.10 = (s32[128]{0:T(128)S(1)}, s32[128]{0:T(128)}, u32[]{:S(2)}) copy-start(s32[128]{0:T(128)} %bc_ref.3) | copy-start | bytes 1540
  48.6 50.7 %collective-permute-start.2 = (bf16[12,2,128,128]{3,2,1,0:T(8,128)(2,1)}, bf16[12,2,128,128]{3,2,1,0:T(8,128)(2,1)}, u32[]{:S(2)}, u32[]{:S(2)}) collective-permute-start(bf16[12,2,128,128]{3,2,1,0:T(8,128)(2,1)} %get-tuple-element.25), channel_id=1, source_target_pairs={{16,0},{32,16},{48,32},{64,48},{80,64},{96,80},{112,96},{128,112},... | collective-permute-start | bytes 2359304 | tf_op jit(solution)/shard_map/ppermute | solution.py:411
  56.2 43.1 %collective-permute-start.1 = (bf16[12,2,128,128]{3,2,1,0:T(8,128)(2,1)}, bf16[12,2,128,128]{3,2,1,0:T(8,128)(2,1)}, u32[]{:S(2)}, u32[]{:S(2)}) collective-permute-start(bf16[12,2,128,128]{3,2,1,0:T(8,128)(2,1)} %get-tuple-element.26), channel_id=1, source_target_pairs={{496,0},{0,16},{16,32},{32,48},{48,64},{64,80},{80,96},{96,112},{1... | collective-permute-start | bytes 2359304 | tf_op jit(solution)/shard_map/ppermute | solution.py:411
  76.3 1.0 copy-start.3
  77.3 0.8 copy-start.5
  78.1 21.2 %copy-start.4 = (f32[4,512,128]{2,1,0:T(8,128)S(1)}, f32[4,512,128]{2,1,0:T(8,128)}, u32[]{:S(2)}) copy-start(f32[4,512,128]{2,1,0:T(8,128)} %copy-done.3) | copy-start | bytes 3145732
  78.1 21.2 %copy-start.6 = (bf16[16,1,128,128]{3,2,1,0:T(8,128)(2,1)S(1)}, bf16[16,1,128,128]{3,2,1,0:T(8,128)(2,1)}, u32[]{:S(2)}) copy-start(bf16[16,1,128,128]{3,2,1,0:T(8,128)(2,1)} %copy-done.5) | copy-start | bytes 1572868
  80.3 0.7 copy-start.7
  81.0 33.7 %all-to-all-start.3 = ((bf16[128,8,128]{2,1,0:T(8,128)(2,1)}), bf16[128,8,128]{2,1,0:T(8,128)(2,1)}, u32[]{:S(2)}, u32[]{:S(2)}) async-start(bf16[128,8,128]{2,1,0:T(8,128)(2,1)} %copy-done.7), calls=%async_computation.3 | async-start | bytes 524288 | tf_op jit(solution)/shard_map/all_to_all | solution.py:406
  114.6 16.9 %copy-start.9 = (s32[24]{0:T(128)S(1)}, s32[24]{0:T(128)}, u32[]{:S(2)}) copy-start(s32[24]{0:T(128)} %order_ref.7) | copy-start | bytes 292
  114.7 16.8 %all-to-all-start.2 = ((bf16[16,128,128]{2,1,0:T(8,128)(2,1)}), bf16[16,128,128]{2,1,0:T(8,128)(2,1)S(1)}, u32[]{:S(2)}, u32[]{:S(2)}) async-start(bf16[16,128,128]{2,1,0:T(8,128)(2,1)} %shard_map.69), calls=%async_computation.2 | async-start | bytes 1048576 | tf_op jit(solution)/shard_map/all_to_all | solution.py:406

commit v8 on v6

--- a/solution.py
+++ b/solution.py
@@ -304,7 +304,7 @@
             finish(mine, add_frames(acc, query(mine), pairs))
             return carry
 
-        lax.fori_loop(0, BLOCK, frame, 0)
+        lax.fori_loop(0, BLOCK, frame, 0, unroll=True)
 
     @pl.when(jnp.logical_not(fast))
     def _():

time: 137 us -> 136 us (level)
  starting transfers between devices: 55 us -> 63.4 us
  Pallas kernels: 47.3 us -> 41.4 us
  waiting for transfers between devices: 28.9 us -> 24.8 us
    all_to_all x4, starting transfers between devices: 40.8 us -> 49.2 us  [exchange(): return lax.all_to_all(array, axes, 0, 0, tiled=True)]
    ppermute x2, waiting for transfers between devices: 9.57 us -> 4.66 us  [from_block(): lax.ppermute(array, ('zh', 'core', 'yh'), [((i + by) % count, i) for i in...]
    pallas_call x1, Pallas kernels: 19.3 us -> 14.5 us  [attend_own(): pl.pallas_call(functools.partial(own_kernel, frames), out_shape=[jax.Shap...]
  transfers between devices with their start and end apart: 7 -> 7, of which waited for: 4 -> 4; matrix products, arithmetic and copies ran while one was open for 1% -> 1% of each run, Pallas kernels for 31% -> 27%
where the time goes in v8:
time: 136 us; the launch traced here: 135 us
  starting transfers between devices  63.4 us (47%)
  Pallas kernels  41.4 us (30%)
  waiting for transfers between devices  24.8 us (18%)
  local copies, waits for them, and re-layouts  5.21 us (4%)
    all_to_all x4, starting transfers between devices, exchange(): return lax.all_to_all(array, axes, 0, 0, tiled=True)  49.2 us
    all_to_all x4, waiting for transfers between devices, exchange(): return lax.all_to_all(array, axes, 0, 0, tiled=True)  18.8 us
    pallas_call x1, Pallas kernels, attend_near(): pl.pallas_call(functools.partial(near_kernel, frames), out_shape=jax.Shap...  16.6 us
    pallas_call x1, Pallas kernels, attend_own(): pl.pallas_call(functools.partial(own_kernel, frames), out_shape=[jax.Shap...  14.5 us
    ppermute x2, starting transfers between devices, from_block(): lax.ppermute(array, ('zh', 'core', 'yh'), [((i + by) % count, i) for i in...  9.51 us
    ppermute x1, starting transfers between devices, local(): st = join(mine, lax.ppermute(other, 'core', [(0, 1), (1, 0)]))  4.72 us
    ppermute x2, waiting for transfers between devices, from_block(): lax.ppermute(array, ('zh', 'core', 'yh'), [((i + by) % count, i) for i in...  4.66 us
    unnamed x25, local copies, waits for them, and re-layouts  3.76 us
  transfers between devices with their start and end apart: 7, of which 4 were waited for; matrix products, arithmetic and copies ran while one was open for 1% of the time, Pallas kernels for 27%

profile of v8, /device:TPU:1, one launch (start us, length us, event | category | flops | bytes accessed | tf_op | source)
XLA Modules:
  0.0 135.3 jit_solution(2750029870241590096)
XLA Ops:
  0.0 3.3 %shard_map.64 = bf16[16,3,128,128]{3,2,1,0:T(8,128)(2,1)} custom-call(s32[24]{0:T(128)} %order_ref.7, bf16[128,3072]{1,0:T(8,128)(2,1)} %q_ref.1, bf16[128,3072]{1,0:T(8,128)(2,1)} %k_ref.1, bf16[128,3072]{1,0:T(8,128)(2,1)} %v_ref.1), custom_call_target="tpu_custom_call" | custom-call | tf_op jit(solution)/shard_map/pallas_call | solution.py:70
  3.3 0.0 copy-start
  3.3 0.0 copy-start.1
  3.3 0.0 copy-start.8
  3.3 7.9 %all-to-all-start = ((bf16[16,3,128,128]{3,2,1,0:T(8,128)(2,1)}), bf16[16,3,128,128]{3,2,1,0:T(8,128)(2,1)S(1)}, u32[]{:S(2)}, u32[]{:S(2)}) async-start(bf16[16,3,128,128]{3,2,1,0:T(8,128)(2,1)} %shard_map.64), calls=%async_computation | async-start | bytes 3145728 | tf_op jit(solution)/shard_map/all_to_all | solution.py:396
  11.3 0.0 copy-done
  11.3 0.0 copy-done.1
  11.3 0.0 copy-done.8
  11.3 0.0 copy-start.2
  11.3 1.1 copy-done.2
  12.4 0.7 shard_map.65
  13.2 4.7 %collective-permute-start = (bf16[64,3,8,128]{3,2,1,0:T(8,128)(2,1)S(1)}, bf16[64,3,8,128]{3,2,1,0:T(8,128)(2,1)S(1)}, u32[]{:S(2)}, u32[]{:S(2)}) collective-permute-start(bf16[64,3,8,128]{3,2,1,0:T(8,128)(2,1)S(1)} %get-tuple-element.16), channel_id=1, source_target_pairs={{0,64},{64,0},{1,65},{65,1},{2,66},{66,2},{3,67},{67,3},{4,68},{68... | collective-permute-start | bytes 1179656 | tf_op jit(solution)/shard_map/ppermute | solution.py:416
  17.9 1.3 collective-permute-done.b_ref
  19.3 0.0 copy-start.11
  19.3 0.9 shard_map.66
  20.2 11.1 %all-to-all-done.in_ref = bf16[16,3,128,128]{3,2,1,0:T(8,128)(2,1)S(1)} async-done(((bf16[16,3,128,128]{3,2,1,0:T(8,128)(2,1)}), bf16[16,3,128,128]{3,2,1,0:T(8,128)(2,1)S(1)}, u32[]{:S(2)}, u32[]{:S(2)}) %all-to-all-start) | async-done | bytes 1572896 | tf_op jit(solution)/shard_map/all_to_all | solution.py:396
  31.3 15.7 %all-to-all-start.1 = ((bf16[64,2,3,8,128]{4,3,2,1,0:T(8,128)(2,1)}), bf16[64,2,3,8,128]{4,3,2,1,0:T(8,128)(2,1)S(1)}, u32[]{:S(2)}, u32[]{:S(2)}) async-start(bf16[64,2,3,8,128]{4,3,2,1,0:T(8,128)(2,1)} %shard_map.66), calls=%async_computation.1 | async-start | bytes 1572864 | tf_op jit(solution)/shard_map/all_to_all | solution.py:396
  47.0 0.0 copy-done.11
  47.1 0.1 copy.9.kb_ref
  47.2 0.0 copy-start.10
  47.2 1.5 %fusion = (bf16[12,2,128,128]{3,2,1,0:T(8,128)(2,1)}, bf16[12,2,128,128]{3,2,1,0:T(8,128)(2,1)}) fusion(bf16[16,3,128,128]{3,2,1,0:T(8,128)(2,1)S(1)} %all-to-all-done.in_ref), kind=kLoop, calls=%fused_computation | loop fusion | bytes 3145728 | tf_op jit(solution)/shard_map/slice | solution.py:420
  48.6 7.6 %collective-permute-start.2 = (bf16[12,2,128,128]{3,2,1,0:T(8,128)(2,1)}, bf16[12,2,128,128]{3,2,1,0:T(8,128)(2,1)}, u32[]{:S(2)}, u32[]{:S(2)}) collective-permute-start(bf16[12,2,128,128]{3,2,1,0:T(8,128)(2,1)} %get-tuple-element.25), channel_id=1, source_target_pairs={{16,0},{32,16},{48,32},{64,48},{80,64},{96,80},{112,96},{128,112},... | collective-permute-start | bytes 2359304 | tf_op jit(solution)/shard_map/ppermute | solution.py:401
  56.2 1.9 %collective-permute-start.1 = (bf16[12,2,128,128]{3,2,1,0:T(8,128)(2,1)}, bf16[12,2,128,128]{3,2,1,0:T(8,128)(2,1)}, u32[]{:S(2)}, u32[]{:S(2)}) collective-permute-start(bf16[12,2,128,128]{3,2,1,0:T(8,128)(2,1)} %get-tuple-element.26), channel_id=1, source_target_pairs={{496,0},{0,16},{16,32},{32,48},{48,64},{64,80},{80,96},{96,112},{1... | collective-permute-start | bytes 2359304 | tf_op jit(solution)/shard_map/ppermute | solution.py:401
  58.2 0.0 copy-done.10
  58.2 14.5 %shard_map.68 = (f32[4,512,128]{2,1,0:T(8,128)S(1)}, f32[4,512,128]{2,1,0:T(8,128)S(1)}, bf16[16,1,128,128]{3,2,1,0:T(8,128)(2,1)S(1)}, f32[2]{0:T(128)S(1)}) custom-call(s32[1]{0:T(128)} %bitcast.base_ref, s32[128,6]{1,0:T(8,128)S(1)} %copy.9.kb_ref, s32[128]{0:T(128)S(1)} %copy-done.10, bf16[16,3,128,128]{3,2,1,0:T(8,128)(2,1)S(1)} %all-to-all-done.in_ref), custom_call_target="tpu_custom_call" | custom-call | flops 10000000000 | bytes 1048576 | tf_op jit(solution)/shard_map/pallas_call | solution.py:336
  72.7 0.0 copy-start.3
  72.7 1.0 copy-done.3
  73.7 0.0 copy-start.5
  73.7 0.8 copy-done.5
  74.5 0.0 all-to-all-done.1.in_ref
  74.5 0.0 copy-start.4
  74.5 0.0 copy-start.6
  74.5 2.1 %shard_map.67 = bf16[128,8,128]{2,1,0:T(8,128)(2,1)S(1)} custom-call(s32[1]{0:T(128)} %bitcast.1.core_ref, bf16[64,2,3,8,128]{4,3,2,1,0:T(8,128)(2,1)S(1)} %all-to-all-done.1.in_ref), custom_call_target="tpu_custom_call" | custom-call | flops 49999998976 | bytes 1048576 | tf_op jit(solution)/shard_map/pallas_call | solution.py:145
  76.7 0.0 copy-start.7
  76.7 0.7 copy-done.7
  77.3 17.3 %all-to-all-start.3 = ((bf16[128,8,128]{2,1,0:T(8,128)(2,1)}), bf16[128,8,128]{2,1,0:T(8,128)(2,1)}, u32[]{:S(2)}, u32[]{:S(2)}) async-start(bf16[128,8,128]{2,1,0:T(8,128)(2,1)} %copy-done.7), calls=%async_computation.3 | async-start | bytes 524288 | tf_op jit(solution)/shard_map/all_to_all | solution.py:396
  94.7 4.7 %collective-permute-done.2.more_ref = bf16[12,2,128,128]{3,2,1,0:T(8,128)(2,1)} collective-permute-done((bf16[12,2,128,128]{3,2,1,0:T(8,128)(2,1)}, bf16[12,2,128,128]{3,2,1,0:T(8,128)(2,1)}, u32[]{:S(2)}, u32[]{:S(2)}) %collective-permute-start.2) | collective-permute-done | bytes 786464 | tf_op jit(solution)/shard_map/ppermute | solution.py:401
  99.3 0.0 collective-permute-done.1.less_ref
  99.3 0.0 copy-done.4
  99.3 0.0 copy-done.6
  99.3 16.6 %shard_map.69 = bf16[16,128,128]{2,1,0:T(8,128)(2,1)} custom-call(s32[1]{0:T(128)} %bitcast.base_ref, s32[128,6]{1,0:T(8,128)S(1)} %copy.9.kb_ref, s32[128]{0:T(128)S(1)} %copy-done.10, f32[2]{0:T(128)S(1)} %get-tuple-element.20.stat_ref, bf16[16,1,128,128]{3,2,1,0:T(8,128)(2,1)S(1)} %copy-done.6, bf16[12,2,128,128]{3,2,1,0:T(8,128)(2,1)} %collective-permute-done.1.less_ref, ...), custom_call_target="tpu_custom_call" | custom-call | tf_op jit(solution)/shard_map/pallas_call | solution.py:355
  115.9 0.0 copy-start.9
  115.9 0.0 all-to-all-done.3
  116.0 8.3 %all-to-all-start.2 = ((bf16[16,128,128]{2,1,0:T(8,128)(2,1)}), bf16[16,128,128]{2,1,0:T(8,128)(2,1)S(1)}, u32[]{:S(2)}, u32[]{:S(2)}) async-start(bf16[16,128,128]{2,1,0:T(8,128)(2,1)} %shard_map.69), calls=%async_computation.2 | async-start | bytes 1048576 | tf_op jit(solution)/shard_map/all_to_all | solution.py:396
  124.2 1.7 %shard_map.70.refs_0_ = bf16[16,8,3072]{2,1,0:T(8,128)(2,1)} custom-call(s32[24]{0:T(128)} %order_ref.7, bf16[8,16,8,128]{3,2,1,0:T(8,128)(2,1)} %bitcast.3.src_ref), custom_call_target="tpu_custom_call" | custom-call | tf_op jit(solution)/shard_map/pallas_call | solution.py:384
  126.0 7.7 %all-to-all-done.2 = bf16[16,128,128]{2,1,0:T(8,128)(2,1)S(1)} async-done(((bf16[16,128,128]{2,1,0:T(8,128)(2,1)}), bf16[16,128,128]{2,1,0:T(8,128)(2,1)S(1)}, u32[]{:S(2)}, u32[]{:S(2)}) %all-to-all-start.2) | async-done | bytes 524320 | tf_op jit(solution)/shard_map/all_to_all | solution.py:396
  133.7 0.0 copy-done.9
  133.7 1.5 %shard_map.71 = bf16[16,8,3072]{2,1,0:T(8,128)(2,1)} custom-call(s32[24]{0:T(128)S(1)} %copy-done.9, bf16[16,16,8,128]{3,2,1,0:T(8,128)(2,1)S(1)} %bitcast.5, bf16[16,8,3072]{2,1,0:T(8,128)(2,1)} %shard_map.70.refs_0_), custom_call_target="tpu_custom_call", output_to_operand_aliasing={{}: (2, {})} | custom-call | tf_op jit(solution)/shard_map/pallas_call | solution.py:384
Async XLA Ops:
  3.3 8.0 %copy-start = (bf16[128,3072]{1,0:T(8,128)(2,1)S(1)}, bf16[128,3072]{1,0:T(8,128)(2,1)}, u32[]{:S(2)}) copy-start(bf16[128,3072]{1,0:T(8,128)(2,1)} %q_ref.1) | copy-start | bytes 2359300
  3.3 8.0 %copy-start.1 = (bf16[128,3072]{1,0:T(8,128)(2,1)S(1)}, bf16[128,3072]{1,0:T(8,128)(2,1)}, u32[]{:S(2)}) copy-start(bf16[128,3072]{1,0:T(8,128)(2,1)} %k_ref.1) | copy-start | bytes 2359300
  3.3 8.0 %copy-start.8 = (s32[24]{0:T(128)S(1)}, s32[24]{0:T(128)}, u32[]{:S(2)}) copy-start(s32[24]{0:T(128)} %order_ref.7) | copy-start | bytes 292
  3.3 28.0 %all-to-all-start = ((bf16[16,3,128,128]{3,2,1,0:T(8,128)(2,1)}), bf16[16,3,128,128]{3,2,1,0:T(8,128)(2,1)S(1)}, u32[]{:S(2)}, u32[]{:S(2)}) async-start(bf16[16,3,128,128]{3,2,1,0:T(8,128)(2,1)} %shard_map.64), calls=%async_computation | async-start | bytes 3145728 | tf_op jit(solution)/shard_map/all_to_all | solution.py:396
  11.3 1.1 copy-start.2
  13.2 6.1 %collective-permute-start = (bf16[64,3,8,128]{3,2,1,0:T(8,128)(2,1)S(1)}, bf16[64,3,8,128]{3,2,1,0:T(8,128)(2,1)S(1)}, u32[]{:S(2)}, u32[]{:S(2)}) collective-permute-start(bf16[64,3,8,128]{3,2,1,0:T(8,128)(2,1)S(1)} %get-tuple-element.16), channel_id=1, source_target_pairs={{0,64},{64,0},{1,65},{65,1},{2,66},{66,2},{3,67},{67,3},{4,68},{68... | collective-permute-start | bytes 1179656 | tf_op jit(solution)/shard_map/ppermute | solution.py:416
  19.3 27.8 %copy-start.11 = (s32[128,6]{0,1:T(8,128)S(1)}, s32[128,6]{0,1:T(8,128)}, u32[]{:S(2)}) copy-start(s32[128,6]{0,1:T(8,128)} %param.10) | copy-start | bytes 9220
  31.3 43.2 %all-to-all-start.1 = ((bf16[64,2,3,8,128]{4,3,2,1,0:T(8,128)(2,1)}), bf16[64,2,3,8,128]{4,3,2,1,0:T(8,128)(2,1)S(1)}, u32[]{:S(2)}, u32[]{:S(2)}) async-start(bf16[64,2,3,8,128]{4,3,2,1,0:T(8,128)(2,1)} %shard_map.66), calls=%async_computation.1 | async-start | bytes 1572864 | tf_op jit(solution)/shard_map/all_to_all | solution.py:396
  47.2 11.0 %copy-start.10 = (s32[128]{0:T(128)S(1)}, s32[128]{0:T(128)}, u32[]{:S(2)}) copy-start(s32[128]{0:T(128)} %bc_ref.3) | copy-start | bytes 1540
  48.6 50.7 %collective-permute-start.2 = (bf16[12,2,128,128]{3,2,1,0:T(8,128)(2,1)}, bf16[12,2,128,128]{3,2,1,0:T(8,128)(2,1)}, u32[]{:S(2)}, u32[]{:S(2)}) collective-permute-start(bf16[12,2,128,128]{3,2,1,0:T(8,128)(2,1)} %get-tuple-element.25), channel_id=1, source_target_pairs={{16,0},{32,16},{48,32},{64,48},{80,64},{96,80},{112,96},{128,112},... | collective-permute-start | bytes 2359304 | tf_op jit(solution)/shard_map/ppermute | solution.py:401
  56.2 43.1 %collective-permute-start.1 = (bf16[12,2,128,128]{3,2,1,0:T(8,128)(2,1)}, bf16[12,2,128,128]{3,2,1,0:T(8,128)(2,1)}, u32[]{:S(2)}, u32[]{:S(2)}) collective-permute-start(bf16[12,2,128,128]{3,2,1,0:T(8,128)(2,1)} %get-tuple-element.26), channel_id=1, source_target_pairs={{496,0},{0,16},{16,32},{32,48},{48,64},{64,80},{80,96},{96,112},{1... | collective-permute-start | bytes 2359304 | tf_op jit(solution)/shard_map/ppermute | solution.py:401
  72.7 1.0 copy-start.3
  73.7 0.8 copy-start.5
  74.5 24.8 %copy-start.4 = (f32[4,512,128]{2,1,0:T(8,128)S(1)}, f32[4,512,128]{2,1,0:T(8,128)}, u32[]{:S(2)}) copy-start(f32[4,512,128]{2,1,0:T(8,128)} %copy-done.3) | copy-start | bytes 3145732
  74.5 24.8 %copy-start.6 = (bf16[16,1,128,128]{3,2,1,0:T(8,128)(2,1)S(1)}, bf16[16,1,128,128]{3,2,1,0:T(8,128)(2,1)}, u32[]{:S(2)}) copy-start(bf16[16,1,128,128]{3,2,1,0:T(8,128)(2,1)} %copy-done.5) | copy-start | bytes 1572868
  76.7 0.7 copy-start.7
  77.3 38.6 %all-to-all-start.3 = ((bf16[128,8,128]{2,1,0:T(8,128)(2,1)}), bf16[128,8,128]{2,1,0:T(8,128)(2,1)}, u32[]{:S(2)}, u32[]{:S(2)}) async-start(bf16[128,8,128]{2,1,0:T(8,128)(2,1)} %copy-done.7), calls=%async_computation.3 | async-start | bytes 524288 | tf_op jit(solution)/shard_map/all_to_all | solution.py:396
  115.9 17.7 %copy-start.9 = (s32[24]{0:T(128)S(1)}, s32[24]{0:T(128)}, u32[]{:S(2)}) copy-start(s32[24]{0:T(128)} %order_ref.7) | copy-start | bytes 292
  116.0 17.7 %all-to-all-start.2 = ((bf16[16,128,128]{2,1,0:T(8,128)(2,1)}), bf16[16,128,128]{2,1,0:T(8,128)(2,1)S(1)}, u32[]{:S(2)}, u32[]{:S(2)}) async-start(bf16[16,128,128]{2,1,0:T(8,128)(2,1)} %shard_map.69), calls=%async_computation.2 | async-start | bytes 1048576 | tf_op jit(solution)/shard_map/all_to_all | solution.py:396
